TPU v7x, 32 devices: a whole 2x2x4 slice. The times are simulated.
32 devices in a mesh: groups: 2 (over x), expert: 8 (over z, y), tensor: 2 (over core).
Axes of the slice: x: 2, y: 2, z: 4, core: 2. Of those that a mesh axis runs over, the one named last changes fastest.
Arguments:
- tokens: bfloat16 [4, 512, 2048], P(None, ('groups', 'expert')), parts along dimension 1, may hold values from -6 to 6
- routes: int32 [4, 512, 8], P(None, ('groups', 'expert')), parts along dimension 1, may hold values from 0 to 31, all different within a row; in each aligned block of 32 rows (0 to 31, 32 to 63, ..., all dimensions but the last counted through in order) at most 16 rows name the same one
- mixing: float32 [4, 512, 8], P(None, ('groups', 'expert')), parts along dimension 1, may hold values from 0.1 to 0.4
- gate_weight: bfloat16 [32, 4096, 768], P(None, ('groups', 'expert', 'tensor')), parts along dimension 1, may hold values from -0.125 to 0.125
- up_weight: bfloat16 [32, 4096, 768], P(None, ('groups', 'expert', 'tensor')), parts along dimension 1, may hold values from -0.125 to 0.125
- down_weight: bfloat16 [32, 4096, 768], P(None, ('groups', 'expert', 'tensor')), parts along dimension 1, may hold values from -0.21875 to 0.21875
Outputs:
- block_out: bfloat16 [4, 512, 2048], P(None, ('groups', 'expert'), 'tensor'), parts along dimension 1
There are 2 independent parts, one for each index of `groups`. A program takes and returns all parts, laid end to end along the dimension named above; each array names one. Nothing has to cross between parts.
Inputs may be any that keep to these rules, and one draw needn't show every extreme that they name: `routes`: in every step each row names 8 different experts, and within each aligned block of 32 rows (the rows of one index of expert) no expert is named by more than 16 rows, a bound that some block reaches.
All inputs are finite; a program needn't handle non-finite values.
Results may differ from a plain program's by a relative error of at most 0.0058.
Values may be sent and summed in bfloat16 or wider, within the bound.
A program may use at most 192 MiB of HBM per device.

v0:
```python
import jax
import jax.numpy as jnp
from jax import lax
from jax.sharding import PartitionSpec as P


def ranks_of(chosen, expert_count):
    onehot_table = (chosen[:, None] == jnp.arange(expert_count, dtype=jnp.int32)[None, :]).astype(
        jnp.int32
    )
    before = jnp.cumsum(onehot_table, axis=0) - onehot_table
    return jnp.sum(before * onehot_table, axis=1)


def local(tokens, routes, mixing, gate_weight, up_weight, down_weight):
    owners = lax.axis_size("expert")
    pairs = lax.axis_size("tensor")
    expert_count, rows_block, hidden_all = gate_weight.shape
    local_count = expert_count // owners
    step_count, row_count, model_width = tokens.shape
    picks_per = routes.shape[2]
    capacity = row_count * picks_per * 2 // expert_count
    shaped = (
        gate_weight.reshape(expert_count, 1, rows_block, hidden_all),
        up_weight.reshape(expert_count, 1, rows_block, hidden_all),
        down_weight.reshape(expert_count, 1, rows_block, hidden_all),
    )
    relaid = (
        lax.all_to_all(
            lax.all_to_all(shaped[0], "expert", split_axis=0, concat_axis=1, tiled=True),
            "tensor",
            split_axis=3,
            concat_axis=2,
            tiled=True,
        ),
        lax.all_to_all(
            lax.all_to_all(shaped[1], "expert", split_axis=0, concat_axis=1, tiled=True),
            "tensor",
            split_axis=3,
            concat_axis=2,
            tiled=True,
        ),
        lax.all_to_all(
            lax.all_to_all(shaped[2], "expert", split_axis=0, concat_axis=1, tiled=True),
            "tensor",
            split_axis=3,
            concat_axis=2,
            tiled=True,
        ),
    )
    w_gate, w_up, w_down = [
        member.reshape(local_count, model_width, hidden_all // pairs) for member in relaid
    ]
    results = []
    for step_id in range(step_count):
        x_rows = tokens[step_id]
        chosen = routes[step_id].reshape(-1)
        rank_index = ranks_of(chosen, expert_count)
        slot_index = chosen * capacity + rank_index
        col_count = x_rows.shape[1]
        repeated = jnp.repeat(x_rows, picks_per, axis=0)
        buffer = (
            jnp.zeros((expert_count * capacity, col_count), jnp.bfloat16)
            .at[slot_index]
            .set(repeated)
        )
        buffer = buffer.reshape(owners, local_count, capacity, col_count)
        pieces = lax.all_to_all(buffer, "expert", split_axis=0, concat_axis=0, tiled=True)
        gate_act = jnp.einsum("skcd,kdf->skcf", pieces, w_gate, preferred_element_type=jnp.float32)
        up_act = jnp.einsum("skcd,kdf->skcf", pieces, w_up, preferred_element_type=jnp.float32)
        hidden_act = (jax.nn.silu(gate_act) * up_act).astype(jnp.bfloat16)
        partial_value = jnp.einsum(
            "skcf,kdf->skcd", hidden_act, w_down, preferred_element_type=jnp.float32
        )
        answers = lax.psum_scatter(partial_value, "tensor", scatter_dimension=3, tiled=True).astype(
            jnp.bfloat16
        )
        returned = lax.all_to_all(answers, "expert", split_axis=0, concat_axis=0, tiled=True)
        flat_rows = returned.reshape(expert_count * capacity, returned.shape[3])
        picked = (
            flat_rows[slot_index]
            .reshape(row_count, picks_per, returned.shape[3])
            .astype(jnp.float32)
        )
        combined = jnp.sum(mixing[step_id][:, :, None] * picked, axis=1)
        results.append(combined.astype(jnp.bfloat16))
    stacked = jnp.stack(results)
    return stacked


def solution(mesh):
    return jax.shard_map(
        local,
        mesh=mesh,
        in_specs=(
            P(None, ("groups", "expert"), None),
            P(None, ("groups", "expert"), None),
            P(None, ("groups", "expert"), None),
            P(None, ("groups", "expert", "tensor"), None),
            P(None, ("groups", "expert", "tensor"), None),
            P(None, ("groups", "expert", "tensor"), None),
        ),
        out_specs=P(None, ("groups", "expert"), "tensor"),
        check_vma=False,
    )
```

profile of v0, /device:TPU:0, one launch (start us, length us, event | category | flops | bytes accessed | tf_op | source)
XLA Modules:
  0.0 892.3 jit_solution(7893287876853426488)
XLA Ops:
  6.5 145.8 %all_to_all.139 = bf16[32,1,128,768]{3,2,1,0:T(8,128)(2,1)} all-to-all(bf16[32,1,128,768]{3,2,1,0:T(8,128)(2,1)} %bitcast.274), channel_id=1, replica_groups=mesh['groups'=2,'expert'=8,'tensor'=2] {'expert'}, dimensions={0} | all-to-all | bytes 12582912 | tf_op jit(solution)/shard_map/all_to_all | solution.py:30
  152.3 141.6 %all_to_all.140 = bf16[32,1,128,768]{3,2,1,0:T(8,128)(2,1)} all-to-all(bf16[32,1,128,768]{3,2,1,0:T(8,128)(2,1)S(1)} %bitcast.275), channel_id=1, replica_groups=mesh['groups'=2,'expert'=8,'tensor'=2] {'expert'}, dimensions={0} | all-to-all | bytes 12582912 | tf_op jit(solution)/shard_map/all_to_all | solution.py:37
  303.9 11.3 %copy.113 = bf16[4,8,128,768]{2,0,1,3:T(4,128)(2,1)} copy(bf16[4,8,128,768]{3,2,0,1:T(8,128)(2,1)} %bitcast.266) | data formatting | bytes 12582912 | tf_op jit(solution)/shard_map/all_to_all | solution.py:30
  315.2 11.2 %copy.117 = bf16[4,8,128,768]{2,0,1,3:T(4,128)(2,1)} copy(bf16[4,8,128,768]{3,2,0,1:T(8,128)(2,1)} %bitcast.265) | data formatting | bytes 12582912 | tf_op jit(solution)/shard_map/all_to_all | solution.py:37
  326.4 109.6 %all-to-all-done.5 = bf16[32,1,128,768]{3,2,1,0:T(8,128)(2,1)} async-done(((bf16[32,1,128,768]{3,2,1,0:T(8,128)(2,1)}), bf16[32,1,128,768]{3,2,1,0:T(8,128)(2,1)}, u32[]{:S(2)}, u32[]{:S(2)}) %all-to-all-start.5) | async-done | bytes 6291488 | tf_op jit(solution)/shard_map/all_to_all | solution.py:44
  442.3 11.3 %copy.121 = bf16[4,8,128,768]{2,0,1,3:T(4,128)(2,1)} copy(bf16[4,8,128,768]{3,2,0,1:T(8,128)(2,1)} %bitcast.30) | data formatting | bytes 12582912 | tf_op jit(solution)/shard_map/all_to_all | solution.py:44
  453.6 15.6 %all_to_all.141 = bf16[4,8,128,768]{2,0,1,3:T(4,128)(2,1)} all-to-all(bf16[4,8,128,768]{2,0,1,3:T(4,128)(2,1)} %copy.117), channel_id=1, replica_groups=mesh['groups'=2,'expert'=8,'tensor'=2] {'tensor'}, dimensions={3} | all-to-all | bytes 12582912 | tf_op jit(solution)/shard_map/all_to_all | solution.py:36
  469.3 10.0 %all_to_all.142 = bf16[4,8,128,768]{2,0,1,3:T(4,128)(2,1)} all-to-all(bf16[4,8,128,768]{2,0,1,3:T(4,128)(2,1)S(1)} %copy-done), channel_id=1, replica_groups=mesh['groups'=2,'expert'=8,'tensor'=2] {'tensor'}, dimensions={3} | all-to-all | bytes 12582912 | tf_op jit(solution)/shard_map/all_to_all | solution.py:43
  482.9 7.8 copy.114
  490.7 8.8 copy.115
  507.4 8.6 copy.119
  516.0 7.8 copy.122
  523.8 8.7 copy.123
  536.5 9.7 %convolution_bitcast_fusion.3 = f32[8,4,16,2048]{3,2,0,1:T(8,128)} fusion(bf16[4,2048,384,1]{2,1,3,0:T(8,128)(2,1)} %bitcast.258, bf16[4,2048,384,1]{2,1,3,0:T(8,128)(2,1)} %bitcast.254, bf16[8,4,16,2048]{3,2,1,0:T(8,128)(2,1)S(1)} %all-to-all-done, f32[8,4,16,384]{3,2,0,1:T(8,128)S(1)} %fusion.16), kind=kOutput, calls=%fused_computation.11 | convolution fusion | flops 1611792384 | bytes 19660800 | tf_op jit(solution)/shard_map/skcf,kdf->skcd/dot_general | solution.py:72
  551.7 54.1 %all_to_all.143 = bf16[8,4,16,2048]{3,2,1,0:T(8,128)(2,1)S(1)} all-to-all(bf16[8,4,16,2048]{3,2,1,0:T(8,128)(2,1)} %bitcast.272), channel_id=1, replica_groups=mesh['groups'=2,'expert'=8,'tensor'=2] {'expert'}, dimensions={0} | all-to-all | bytes 4194304 | tf_op jit(solution)/shard_map/all_to_all | solution.py:68
  609.9 9.8 %convolution_bitcast_fusion.2 = f32[8,4,16,2048]{3,2,0,1:T(8,128)} fusion(bf16[4,2048,384,1]{2,1,3,0:T(8,128)(2,1)} %bitcast.259, bf16[4,2048,384,1]{2,1,3,0:T(8,128)(2,1)} %bitcast.255, bf16[8,4,16,2048]{3,2,1,0:T(8,128)(2,1)S(1)} %all_to_all.143, f32[8,4,16,384]{3,2,0,1:T(8,128)S(1)} %fusion.22), kind=kOutput, calls=%fused_computation.10 | convolution fusion | flops 1611792384 | bytes 19660800 | tf_op jit(solution)/shard_map/skcf,kdf->skcd/dot_general | solution.py:72
  624.8 52.0 %all_to_all.144 = bf16[8,4,16,2048]{3,2,1,0:T(8,128)(2,1)S(1)} all-to-all(bf16[8,4,16,2048]{3,2,1,0:T(8,128)(2,1)} %bitcast.273), channel_id=1, replica_groups=mesh['groups'=2,'expert'=8,'tensor'=2] {'expert'}, dimensions={0} | all-to-all | bytes 4194304 | tf_op jit(solution)/shard_map/all_to_all | solution.py:68
  680.8 9.7 %convolution_bitcast_fusion = f32[8,4,16,2048]{3,2,0,1:T(8,128)} fusion(bf16[4,2048,384,1]{2,1,3,0:T(8,128)(2,1)} %bitcast.260, bf16[4,2048,384,1]{2,1,3,0:T(8,128)(2,1)} %bitcast.256, bf16[8,4,16,2048]{3,2,1,0:T(8,128)(2,1)S(1)} %all_to_all.144, f32[8,4,16,384]{3,2,0,1:T(8,128)S(1)} %fusion.34), kind=kOutput, calls=%fused_computation.8 | convolution fusion | flops 1611792384 | bytes 19660800 | tf_op jit(solution)/shard_map/skcf,kdf->skcd/dot_general | solution.py:72
  695.7 51.3 %all_to_all.145 = bf16[8,4,16,2048]{3,2,1,0:T(8,128)(2,1)S(1)} all-to-all(bf16[8,4,16,2048]{3,2,1,0:T(8,128)(2,1)} %bitcast.271), channel_id=1, replica_groups=mesh['groups'=2,'expert'=8,'tensor'=2] {'expert'}, dimensions={0} | all-to-all | bytes 4194304 | tf_op jit(solution)/shard_map/all_to_all | solution.py:68
  751.1 9.6 %convolution_bitcast_fusion.1 = f32[8,4,16,2048]{3,2,0,1:T(8,128)} fusion(bf16[4,2048,384,1]{2,1,3,0:T(8,128)(2,1)} %bitcast.261, bf16[4,2048,384,1]{2,1,3,0:T(8,128)(2,1)} %bitcast.257, bf16[8,4,16,2048]{3,2,1,0:T(8,128)(2,1)S(1)} %all_to_all.145, f32[8,4,16,384]{3,2,0,1:T(8,128)S(1)} %fusion.28), kind=kOutput, calls=%fused_computation.9 | convolution fusion | flops 1611792384 | bytes 19660800 | tf_op jit(solution)/shard_map/skcf,kdf->skcd/dot_general | solution.py:72
  770.5 22.1 %all-to-all-done.7 = bf16[8,4,16,1024]{3,2,1,0:T(8,128)(2,1)S(1)} async-done(((bf16[8,4,16,1024]{3,2,1,0:T(8,128)(2,1)}), bf16[8,4,16,1024]{3,2,1,0:T(8,128)(2,1)S(1)}, u32[]{:S(2)}, u32[]{:S(2)}) %all-to-all-start.7) | async-done | bytes 1048608 | tf_op jit(solution)/shard_map/all_to_all | solution.py:78
  799.0 22.9 %all-to-all-done.9 = bf16[8,4,16,1024]{3,2,1,0:T(8,128)(2,1)S(1)} async-done(((bf16[8,4,16,1024]{3,2,1,0:T(8,128)(2,1)}), bf16[8,4,16,1024]{3,2,1,0:T(8,128)(2,1)S(1)}, u32[]{:S(2)}, u32[]{:S(2)}) %all-to-all-start.9) | async-done | bytes 1048608 | tf_op jit(solution)/shard_map/all_to_all | solution.py:78
  828.6 23.0 %all-to-all-done.13 = bf16[8,4,16,1024]{3,2,1,0:T(8,128)(2,1)S(1)} async-done(((bf16[8,4,16,1024]{3,2,1,0:T(8,128)(2,1)}), bf16[8,4,16,1024]{3,2,1,0:T(8,128)(2,1)S(1)}, u32[]{:S(2)}, u32[]{:S(2)}) %all-to-all-start.13) | async-done | bytes 1048608 | tf_op jit(solution)/shard_map/all_to_all | solution.py:78
  861.7 19.8 %all-to-all-done.11 = bf16[8,4,16,1024]{3,2,1,0:T(8,128)(2,1)} async-done(((bf16[8,4,16,1024]{3,2,1,0:T(8,128)(2,1)}), bf16[8,4,16,1024]{3,2,1,0:T(8,128)(2,1)}, u32[]{:S(2)}, u32[]{:S(2)}) %all-to-all-start.11) | async-done | bytes 1048608 | tf_op jit(solution)/shard_map/all_to_all | solution.py:78
  (118 shorter events, 96.4 us)
Async XLA Ops:
  6.5 145.8 %copy-start.1 = (bf16[32,128,768]{2,1,0:T(8,128)(2,1)S(1)}, bf16[32,128,768]{2,1,0:T(8,128)(2,1)}, u32[]{:S(2)}) copy-start(bf16[32,128,768]{2,1,0:T(8,128)(2,1)} %param.10) | copy-start | bytes 18874372
  293.9 4.9 copy-start.4
  293.9 6.3 copy-start.3
  293.9 142.1 %all-to-all-start.5 = ((bf16[32,1,128,768]{3,2,1,0:T(8,128)(2,1)}), bf16[32,1,128,768]{3,2,1,0:T(8,128)(2,1)}, u32[]{:S(2)}, u32[]{:S(2)}) async-start(bf16[32,1,128,768]{3,2,1,0:T(8,128)(2,1)} %bitcast.276), calls=%async_computation.5 | async-start | bytes 12582912 | tf_op jit(solution)/shard_map/all_to_all | solution.py:44
  436.0 17.6 %all-to-all-start.2 = ((bf16[4,8,128,768]{2,0,1,3:T(4,128)(2,1)}), bf16[4,8,128,768]{2,0,1,3:T(4,128)(2,1)}, u32[]{:S(2)}, u32[]{:S(2)}) async-start(bf16[4,8,128,768]{2,0,1,3:T(4,128)(2,1)} %copy.113), calls=%async_computation.2 | async-start | bytes 12582912 | tf_op jit(solution)/shard_map/all_to_all | solution.py:29
  453.6 15.6 %copy-start = (bf16[4,8,128,768]{2,0,1,3:T(4,128)(2,1)S(1)}, bf16[4,8,128,768]{2,0,1,3:T(4,128)(2,1)}, u32[]{:S(2)}) copy-start(bf16[4,8,128,768]{2,0,1,3:T(4,128)(2,1)} %copy.121) | copy-start | bytes 18874372
  479.3 53.2 %all-to-all-start = ((bf16[8,4,16,2048]{3,2,1,0:T(8,128)(2,1)}), bf16[8,4,16,2048]{3,2,1,0:T(8,128)(2,1)S(1)}, u32[]{:S(2)}, u32[]{:S(2)}) async-start(bf16[8,4,16,2048]{3,2,1,0:T(8,128)(2,1)} %bitcast.270), calls=%async_computation | async-start | bytes 4194304 | tf_op jit(solution)/shard_map/all_to_all | solution.py:68
  482.9 277.9 %reduce-scatter.5.cloned.1.call-start = ((), (), s32[]{:S(2)}) async-start(), calls=%async_computation.18 | async-start | bytes 6291456 | tf_op jit(solution)/shard_map/reduce_scatter | solution.py:75
  546.3 220.9 %reduce-scatter.7.cloned.1.call-start = ((), (), s32[]{:S(2)}) async-start(), calls=%async_computation.19 | async-start | bytes 6291456 | tf_op jit(solution)/shard_map/reduce_scatter | solution.py:75
  619.6 176.5 %reduce-scatter.11.cloned.1.call-start = ((), (), s32[]{:S(2)}) async-start(), calls=%async_computation.21 | async-start | bytes 6291456 | tf_op jit(solution)/shard_map/reduce_scatter | solution.py:75
  690.6 135.2 %reduce-scatter.9.cloned.1.call-start = ((), (), s32[]{:S(2)}) async-start(), calls=%async_computation.20 | async-start | bytes 6291456 | tf_op jit(solution)/shard_map/reduce_scatter | solution.py:75
  763.6 29.0 %all-to-all-start.7 = ((bf16[8,4,16,1024]{3,2,1,0:T(8,128)(2,1)}), bf16[8,4,16,1024]{3,2,1,0:T(8,128)(2,1)S(1)}, u32[]{:S(2)}, u32[]{:S(2)}) async-start(bf16[8,4,16,1024]{3,2,1,0:T(8,128)(2,1)} %copy.124), calls=%async_computation.8 | async-start | bytes 2097152 | tf_op jit(solution)/shard_map/all_to_all | solution.py:78
  792.6 29.3 %all-to-all-start.9 = ((bf16[8,4,16,1024]{3,2,1,0:T(8,128)(2,1)}), bf16[8,4,16,1024]{3,2,1,0:T(8,128)(2,1)S(1)}, u32[]{:S(2)}, u32[]{:S(2)}) async-start(bf16[8,4,16,1024]{3,2,1,0:T(8,128)(2,1)} %copy.132), calls=%async_computation.11 | async-start | bytes 2097152 | tf_op jit(solution)/shard_map/all_to_all | solution.py:78
  821.9 29.7 %all-to-all-start.13 = ((bf16[8,4,16,1024]{3,2,1,0:T(8,128)(2,1)}), bf16[8,4,16,1024]{3,2,1,0:T(8,128)(2,1)S(1)}, u32[]{:S(2)}, u32[]{:S(2)}) async-start(bf16[8,4,16,1024]{3,2,1,0:T(8,128)(2,1)} %copy.148), calls=%async_computation.17 | async-start | bytes 2097152 | tf_op jit(solution)/shard_map/all_to_all | solution.py:78
  827.5 28.4 %copy-start.5 = (f32[4,32,8]{1,2,0:T(8,128)S(1)}, f32[4,32,8]{1,2,0:T(8,128)}, u32[]{:S(2)}) copy-start(f32[4,32,8]{1,2,0:T(8,128)} %param.8) | copy-start | bytes 12292
  851.6 29.9 %all-to-all-start.11 = ((bf16[8,4,16,1024]{3,2,1,0:T(8,128)(2,1)}), bf16[8,4,16,1024]{3,2,1,0:T(8,128)(2,1)}, u32[]{:S(2)}, u32[]{:S(2)}) async-start(bf16[8,4,16,1024]{3,2,1,0:T(8,128)(2,1)} %copy.140), calls=%async_computation.14 | async-start | bytes 2097152 | tf_op jit(solution)/shard_map/all_to_all | solution.py:78
  859.4 1.2 copy-start.2
Sparse Core Ops, SparseCore 0:
  546.4 13.3 reduce-scatter.4
  619.8 11.0 reduce-scatter.6
  690.7 10.9 reduce-scatter.10
  760.8 10.9 reduce-scatter.8
where the time goes:
time: 901 us; the launch traced here: 892 us
  blocking collectives  470 us (52%)
  waiting for transfers between devices  198 us (22%)
  local copies, waits for them, and re-layouts  113 us (13%)
  matrix products  55 us (6%)
  starting transfers between devices  30.2 us (3%)
  between operations  13.7 us (2%)
  other arithmetic  12.9 us (1%)
    all_to_all x3, blocking collectives, local(): lax.all_to_all(buffer, 'expert', split_axis=0, concat_axis=0, tiled=True)  157 us
    all_to_all x1, blocking collectives, local(): lax.all_to_all(shaped[0], 'expert', split_axis=0, concat_axis=1, tiled=True)  146 us
    all_to_all x1, blocking collectives, local(): lax.all_to_all(shaped[1], 'expert', split_axis=0, concat_axis=1, tiled=True)  142 us
    all_to_all x1, waiting for transfers between devices, local(): lax.all_to_all(shaped[2], 'expert', split_axis=0, concat_axis=1, tiled=True)  110 us
    all_to_all x4, waiting for transfers between devices, local(): lax.all_to_all(answers, 'expert', split_axis=0, concat_axis=0, tiled=True)  87.8 us
    dot_general x4, matrix products, local(): jnp.einsum('skcf,kdf->skcd', hidden_act, w_down, preferred_element_type=j...  38.8 us
  transfers between devices with their start and end apart: 11, of which 5 were waited for; matrix products, arithmetic and copies ran while one was open for 18% of the time, Pallas kernels for 0%

commit v1 on v0

v1 whole, which is shorter than its diff:
```python
import jax
import jax.numpy as jnp
from jax import lax
from jax.sharding import PartitionSpec as P

ALL = ("expert", "tensor")


def own_experts(weight):
    devices = lax.axis_size("expert") * lax.axis_size("tensor")
    expert_count, rows_block, hidden_all = weight.shape
    local_count = expert_count // devices
    parts = weight.reshape(devices, local_count, rows_block, hidden_all)
    moved = lax.all_to_all(parts, ALL, split_axis=0, concat_axis=0, tiled=True)
    return moved.transpose(1, 0, 2, 3).reshape(local_count, devices * rows_block, hidden_all)


def local(tokens, routes, mixing, gate_weight, up_weight, down_weight):
    owners = lax.axis_size("expert")
    pairs = lax.axis_size("tensor")
    expert_count = gate_weight.shape[0]
    step_count, row_count, model_width = tokens.shape
    local_count = expert_count // (owners * pairs)
    block = step_count * row_count
    named = routes[..., None] == jnp.arange(expert_count, dtype=jnp.int32)
    shares = jnp.sum(jnp.where(named, mixing[..., None], 0.0), axis=2)
    rows_all = lax.all_gather(tokens.reshape(block, model_width), "expert", axis=0, tiled=True)
    shares_all = lax.all_gather(shares.reshape(block, expert_count), "expert", axis=0, tiled=True)
    me = lax.axis_index("expert") * pairs + lax.axis_index("tensor")
    own_shares = lax.dynamic_slice_in_dim(shares_all, me * local_count, local_count, axis=1)
    w_gate = own_experts(gate_weight)
    w_up = own_experts(up_weight)
    w_down = own_experts(down_weight)
    total = jnp.zeros((owners * block, model_width), jnp.float32)
    for k in range(local_count):
        gate_act = jnp.dot(rows_all, w_gate[k], preferred_element_type=jnp.float32)
        up_act = jnp.dot(rows_all, w_up[k], preferred_element_type=jnp.float32)
        hidden_act = (jax.nn.silu(gate_act) * up_act * own_shares[:, k : k + 1]).astype(jnp.bfloat16)
        total = total + lax.dot_general(
            hidden_act, w_down[k], (((1,), (1,)), ((), ())), preferred_element_type=jnp.float32
        )
    half = model_width // pairs
    sent = total.reshape(owners * block, pairs, half).transpose(1, 0, 2).astype(jnp.bfloat16)
    both = lax.all_to_all(sent, "tensor", split_axis=0, concat_axis=0, tiled=True)
    chip_sum = jnp.sum(both.astype(jnp.float32), axis=0).astype(jnp.bfloat16)
    returned = lax.all_to_all(
        chip_sum.reshape(owners, block, half), "expert", split_axis=0, concat_axis=0, tiled=True
    )
    out = jnp.sum(returned.astype(jnp.float32), axis=0).astype(jnp.bfloat16)
    return out.reshape(step_count, row_count, half)


def solution(mesh):
    return jax.shard_map(
        local,
        mesh=mesh,
        in_specs=(
            P(None, ("groups", "expert"), None),
            P(None, ("groups", "expert"), None),
            P(None, ("groups", "expert"), None),
            P(None, ("groups", "expert", "tensor"), None),
            P(None, ("groups", "expert", "tensor"), None),
            P(None, ("groups", "expert", "tensor"), None),
        ),
        out_specs=P(None, ("groups", "expert"), "tensor"),
        check_vma=False,
    )
```

time: 901 us -> 643 us (0.71)
  waiting for transfers between devices: 198 us -> 0.68 us
  local copies, waits for them, and re-layouts: 113 us -> 18.6 us
  blocking collectives: 470 us -> 556 us
  starting transfers between devices: 30.2 us -> 5.71 us
  matrix products: 55 us -> 40.4 us
    all_gather x0 -> x1, blocking collectives: none -> 208 us  [local(): lax.all_gather(shares.reshape(block, expert_count), 'expert', axis=0, til...]
    all_to_all x7 -> x1, waiting for transfers between devices: 197 us -> 0.01 us  [own_experts(): moved = lax.all_to_all(parts, ALL, split_axis=0, concat_axis=0, tiled=True)]
    all_to_all x7 -> x4, blocking collectives: 470 us -> 348 us  [the longest x2 288 us: own_experts(): moved = lax.all_to_all(parts, ALL, split_axis=0, concat_axis=0, tiled=True)]
    all_to_all x9 -> x0, local copies, waits for them, and re-layouts: 83.3 us -> none  [the longest x2 16.6 us: local(): lax.all_to_all(lax.all_to_all(shaped[0], 'expert', split_axis=0, concat_a...]
    all_to_all x7 -> x1, starting transfers between devices: 30 us -> 5.67 us  [own_experts(): moved = lax.all_to_all(parts, ALL, split_axis=0, concat_axis=0, tiled=True)]
    slice x5 -> x4, local copies, waits for them, and re-layouts: 0.49 us -> 15.7 us  [the longest x1 6.36 us: local(): w_down[k]]
    scatter x4 -> x0, local copies, waits for them, and re-layouts: 14.9 us -> none  [local(): buffer = jnp.zeros((expert_count * capacity, col_count), jnp.bfloat16).at...]
    dot_general x8 -> x4, matrix products: 55 us -> 40.4 us  [the longest x2 27.9 us: local(): lax.dot_general(hidden_act, w_down[k], (((1,), (1,)), ((), ())), preferre...]
  transfers between devices with their start and end apart: 11 -> 2, of which waited for: 5 -> 0; matrix products, arithmetic and copies ran while one was open for 18% -> 3% of each run, Pallas kernels for 0% -> 0%
where the time goes in v1:
time: 643 us; the launch traced here: 642 us
  blocking collectives  556 us (86%)
  matrix products  40.4 us (6%)
  local copies, waits for them, and re-layouts  18.6 us (3%)
  between operations  13.5 us (2%)
  other arithmetic  7.19 us (1%)
    all_to_all x2, blocking collectives, own_experts(): moved = lax.all_to_all(parts, ALL, split_axis=0, concat_axis=0, tiled=True)  288 us
    all_gather x1, blocking collectives, local(): lax.all_gather(shares.reshape(block, expert_count), 'expert', axis=0, til...  208 us
    all_to_all x1, blocking collectives, local(): lax.all_to_all(chip_sum.reshape(owners, block, half), 'expert', split_axi...  52.1 us
    dot_general x2, matrix products, local(): lax.dot_general(hidden_act, w_down[k], (((1,), (1,)), ((), ())), preferre...  27.9 us
  transfers between devices with their start and end apart: 2, of which 0 were waited for; matrix products, arithmetic and copies ran while one was open for 3% of the time, Pallas kernels for 0%

profile of v1, /device:TPU:0, one launch (start us, length us, event | category | flops | bytes accessed | tf_op | source)
XLA Modules:
  0.0 642.2 jit_solution(14722512999229220737)
XLA Ops:
  6.5 145.0 %all_to_all.25 = bf16[16,2,128,768]{3,2,1,0:T(8,128)(2,1)} all-to-all(bf16[16,2,128,768]{3,2,1,0:T(8,128)(2,1)} %bitcast.41), channel_id=1, replica_groups=mesh['groups'=2,'expert'=8,'tensor'=2] {'expert','tensor'}, dimensions={0} | all-to-all | bytes 12582912 | tf_op jit(solution)/shard_map/all_to_all | solution.py:14
  151.5 142.6 %all_to_all.26 = bf16[16,2,128,768]{3,2,1,0:T(8,128)(2,1)} all-to-all(bf16[16,2,128,768]{3,2,1,0:T(8,128)(2,1)S(1)} %bitcast.42), channel_id=1, replica_groups=mesh['groups'=2,'expert'=8,'tensor'=2] {'expert','tensor'}, dimensions={0} | all-to-all | bytes 12582912 | tf_op jit(solution)/shard_map/all_to_all | solution.py:14
  294.1 5.7 all-to-all-start.2
  299.8 0.0 all-gather.2.cloned.1.call-start
  299.8 0.7 all-gather.2.cloned.1.call-update
  300.5 0.1 copy.14
  300.6 0.1 copy.15
  300.7 0.3 select_reduce_fusion
  301.0 0.1 copy.16
  301.1 208.3 %all_gather.7 = f32[1024,32]{0,1:T(8,128)S(1)} all-gather(f32[128,32]{0,1:T(8,128)S(1)} %copy.16), channel_id=1, replica_groups=mesh['groups'=2,'expert'=8,'tensor'=2] {'expert'}, dimensions={0}, use_global_device_ids=true | all-gather | bytes 147456 | tf_op jit(solution)/shard_map/all_gather | solution.py:28
  509.4 0.0 slice-start.1
  509.4 6.3 fusion.4
  515.7 3.1 fusion.3
  518.8 0.0 all-to-all-done.2
  518.8 6.4 fusion.5
  525.2 7.5 %fusion.7 = f32[1024,768]{1,0:T(8,128)} fusion(bf16[1024,2048]{1,0:T(8,128)(2,1)} %all-gather.2.cloned.1.call-done, bf16[2048,768]{1,0:T(8,128)(2,1)S(1)} %bitcast.49), kind=kOutput, calls=%fused_computation.15 | convolution fusion | flops 3221225472 | bytes 10485760 | tf_op jit(solution)/shard_map/dot_general | solution.py:36
  532.6 5.1 fusion.6
  537.7 13.9 %fusion = f32[1024,2048]{1,0:T(8,128)} fusion(bf16[2048,768]{1,0:T(8,128)(2,1)} %bitcast.50, f32[1024,768]{1,0:T(8,128)} %fusion.6, bf16[1024,2048]{1,0:T(8,128)(2,1)} %all-gather.2.cloned.1.call-done, bf16[2048,768]{1,0:T(8,128)(2,1)} %bitcast.46, f32[1024]{0:T(1024)S(1)} %bitcast.54), kind=kOutput, calls=%fused_computation.4 | convolution fusion | flops 6447955968 | bytes 22024192 | tf_op jit(solution)/shard_map/dot_general | solution.py:39
  551.6 13.9 %add_convert_fusion = bf16[1024,2048]{1,0:T(8,128)(2,1)} fusion(f32[1024,2048]{1,0:T(8,128)} %fusion, bf16[2048,768]{1,0:T(8,128)(2,1)} %bitcast.47, f32[1024,768]{1,0:T(8,128)} %fusion.7, bf16[1024,2048]{1,0:T(8,128)(2,1)} %all-gather.2.cloned.1.call-done, bf16[2048,768]{1,0:T(8,128)(2,1)S(1)} %bitcast.45, f32[1024]{0:T(1024)S(1)} %bitcast.53), kind=kOutput, calls=%fused_computation | convolution fusion | flops 6452150272 | bytes 26218496 | tf_op jit(solution)/shard_map/dot_general | solution.py:39
  565.6 2.6 copy.20
  568.2 8.2 %all_to_all.27 = bf16[2,1024,1024]{2,1,0:T(8,128)(2,1)} all-to-all(bf16[2,1024,1024]{2,1,0:T(8,128)(2,1)S(1)} %bitcast.39), channel_id=1, replica_groups=mesh['groups'=2,'expert'=8,'tensor'=2] {'tensor'}, dimensions={0} | all-to-all | bytes 8388608 | tf_op jit(solution)/shard_map/all_to_all | solution.py:44
  576.4 4.1 reduce_sum.34
  580.5 52.1 %all_to_all.28 = bf16[8,128,1024]{2,1,0:T(8,128)(2,1)} all-to-all(bf16[8,128,1024]{2,1,0:T(8,128)(2,1)S(1)} %bitcast.40), channel_id=1, replica_groups=mesh['groups'=2,'expert'=8,'tensor'=2] {'expert'}, dimensions={0} | all-to-all | bytes 4194304 | tf_op jit(solution)/shard_map/all_to_all | solution.py:46
  632.6 2.7 reduce_sum.35
  (20 shorter events, 0.0 us)
Async XLA Ops:
  6.5 145.0 %copy-start = (bf16[32,128,768]{2,1,0:T(8,128)(2,1)S(1)}, bf16[32,128,768]{2,1,0:T(8,128)(2,1)}, u32[]{:S(2)}) copy-start(bf16[32,128,768]{2,1,0:T(8,128)(2,1)} %param.10) | copy-start | bytes 18874372
  294.1 6.4 %copy-start.4 = (s32[4,32,8]{1,2,0:T(8,128)S(1)}, s32[4,32,8]{1,2,0:T(8,128)}, u32[]{:S(2)}) copy-start(s32[4,32,8]{1,2,0:T(8,128)} %param.7) | copy-start | bytes 12292
  294.1 6.5 %copy-start.5 = (f32[4,32,8]{1,2,0:T(8,128)S(1)}, f32[4,32,8]{1,2,0:T(8,128)}, u32[]{:S(2)}) copy-start(f32[4,32,8]{1,2,0:T(8,128)} %param.8) | copy-start | bytes 12292
  294.1 224.7 %all-to-all-start.2 = ((bf16[16,2,128,768]{3,2,1,0:T(8,128)(2,1)}), bf16[16,2,128,768]{3,2,1,0:T(8,128)(2,1)}, u32[]{:S(2)}, u32[]{:S(2)}) async-start(bf16[16,2,128,768]{3,2,1,0:T(8,128)(2,1)} %bitcast.43), calls=%async_computation.2 | async-start | bytes 12582912 | tf_op jit(solution)/shard_map/all_to_all | solution.py:14
  299.8 225.4 %all-gather.2.cloned.1.call-start = ((), (), s32[]{:S(2)}) async-start(), calls=%async_computation.5 | async-start | bytes 4718592 | tf_op jit(solution)/shard_map/all_gather | solution.py:27
  300.7 215.0 %slice-start = ((s8[6291456]{0:T(1024)(128)(4,1)}), s8[2097152]{0:T(1024)(128)(4,1)S(1)}, s32[]{:S(2)}) async-start(s8[6291456]{0:T(1024)(128)(4,1)} %bitcast.35), calls=%async_computation.6 | async-start | bytes 4194304
  509.4 6.3 slice-start.1
  518.8 6.4 copy-start.3
  525.1 7.5 %copy-start.2 = (bf16[1,16,128,768]{3,2,0,1:T(8,128)(2,1)S(1)}, bf16[1,16,128,768]{3,2,0,1:T(8,128)(2,1)}, u32[]{:S(2)}) copy-start(bf16[1,16,128,768]{3,2,0,1:T(8,128)(2,1)} %get-tuple-element.8) | copy-start | bytes 9437188
  525.1 7.5 %copy-start.6 = (bf16[1024,2048]{1,0:T(8,128)(2,1)S(1)}, bf16[1024,2048]{1,0:T(8,128)(2,1)}, u32[]{:S(2)}) copy-start(bf16[1024,2048]{1,0:T(8,128)(2,1)} %all-gather.2.cloned.1.call-done) | copy-start | bytes 12582916
  537.7 14.0 %copy-start.1 = (bf16[1,16,128,768]{3,2,0,1:T(8,128)(2,1)S(1)}, bf16[1,16,128,768]{3,2,0,1:T(8,128)(2,1)}, u32[]{:S(2)}) copy-start(bf16[1,16,128,768]{3,2,0,1:T(8,128)(2,1)} %get-tuple-element.5) | copy-start | bytes 9437188
Sparse Core Ops, SparseCore 0:
  302.7 153.0 all-gather.1

commit v2 on v1

v2 whole, which is shorter than its diff:
```python
import jax
import jax.numpy as jnp
from jax import lax
from jax.sharding import PartitionSpec as P

ALL = ("expert", "tensor")


def own_experts(weight):
    devices = lax.axis_size("expert") * lax.axis_size("tensor")
    expert_count, rows_block, hidden_all = weight.shape
    local_count = expert_count // devices
    parts = weight.reshape(devices, local_count, rows_block, hidden_all)
    moved = lax.all_to_all(parts, ALL, split_axis=0, concat_axis=0, tiled=True)
    return moved.transpose(1, 0, 2, 3).reshape(local_count, devices * rows_block, hidden_all)


def swap(value, axis, distance):
    count = lax.axis_size(axis)
    return lax.ppermute(value, axis, [(i, i ^ distance) for i in range(count)])


def distances_of(owners):
    found, distance = [], owners // 2
    while distance >= 1:
        found.append(distance)
        distance //= 2
    return found


def local(tokens, routes, mixing, gate_weight, up_weight, down_weight):
    owners = lax.axis_size("expert")
    pairs = lax.axis_size("tensor")
    expert_count = gate_weight.shape[0]
    step_count, row_count, model_width = tokens.shape
    devices = owners * pairs
    local_count = expert_count // devices
    block = step_count * row_count
    half = model_width // pairs
    side = lax.axis_index("tensor")
    me = lax.axis_index("expert") * pairs + side
    named = routes[..., None] == jnp.arange(expert_count, dtype=jnp.int32)
    shares = jnp.sum(jnp.where(named, mixing[..., None], 0.0), axis=2).reshape(block, expert_count)
    x_half = lax.dynamic_slice_in_dim(tokens.reshape(block, model_width), side * half, half, axis=1)
    for distance in distances_of(owners):
        x_half = jnp.concatenate([x_half, swap(x_half, "expert", distance)], axis=0)
        shares = jnp.concatenate([shares, swap(shares, "expert", distance)], axis=0)
    x_other = swap(x_half, "tensor", 1)
    rows_all = jnp.concatenate(
        [jnp.where(side == 0, x_half, x_other), jnp.where(side == 0, x_other, x_half)], axis=1
    )
    own_shares = lax.dynamic_slice_in_dim(shares, me * local_count, local_count, axis=1)

    w_gate = own_experts(gate_weight)
    up_weight, rows_all, w_gate = lax.optimization_barrier((up_weight, rows_all, w_gate))
    w_up = own_experts(up_weight)
    down_weight, w_up = lax.optimization_barrier((down_weight, w_up))
    down_parts = down_weight.reshape(devices, local_count, *down_weight.shape[1:])
    hidden = []
    for k in range(local_count):
        gate_act = jnp.dot(rows_all, w_gate[k], preferred_element_type=jnp.float32)
        up_act = jnp.dot(rows_all, w_up[k], preferred_element_type=jnp.float32)
        hidden.append(
            (jax.nn.silu(gate_act) * up_act * own_shares[:, k : k + 1]).astype(jnp.bfloat16)
        )
    total = None
    for k in range(local_count):
        piece = down_parts[:, k]
        if k > 0:
            piece, w_down = lax.optimization_barrier((piece, w_down))
        moved = lax.all_to_all(piece, ALL, split_axis=0, concat_axis=0, tiled=True)
        w_down = moved.reshape(model_width, moved.shape[2])
        part = lax.dot_general(
            hidden[k], w_down, (((1,), (1,)), ((), ())), preferred_element_type=jnp.float32
        )
        total = part if total is None else total + part
    kept = lax.dynamic_slice_in_dim(total, side * half, half, axis=1)
    given = lax.dynamic_slice_in_dim(total, (1 - side) * half, half, axis=1).astype(jnp.bfloat16)
    kept = kept + swap(given, "tensor", 1).astype(jnp.float32)
    for distance in reversed(distances_of(owners)):
        count = kept.shape[0] // 2
        got = swap(kept[count:].astype(jnp.bfloat16), "expert", distance)
        kept = kept[:count] + got.astype(jnp.float32)
    return kept.astype(jnp.bfloat16).reshape(step_count, row_count, half)


def solution(mesh):
    return jax.shard_map(
        local,
        mesh=mesh,
        in_specs=(
            P(None, ("groups", "expert"), None),
            P(None, ("groups", "expert"), None),
            P(None, ("groups", "expert"), None),
            P(None, ("groups", "expert", "tensor"), None),
            P(None, ("groups", "expert", "tensor"), None),
            P(None, ("groups", "expert", "tensor"), None),
        ),
        out_specs=P(None, ("groups", "expert"), "tensor"),
        check_vma=False,
    )
```

time: 643 us -> 628 us (0.977)
  blocking collectives: 556 us -> 216 us
  waiting for transfers between devices: 0.68 us -> 317 us
  starting transfers between devices: 5.71 us -> 23.6 us
  between operations: 13.5 us -> 0.21 us
    ppermute x0 -> x11, waiting for transfers between devices: none -> 317 us  [swap(): return lax.ppermute(value, axis, [(i, i ^ distance) for i in range(count)])]
    all_gather x1 -> x0, blocking collectives: 208 us -> none  [local(): lax.all_gather(shares.reshape(block, expert_count), 'expert', axis=0, til...]
    all_to_all x2 -> x1, blocking collectives: 288 us -> 141 us  [own_experts(): moved = lax.all_to_all(parts, ALL, split_axis=0, concat_axis=0, tiled=True)]
    slice x3, local copies, waits for them, and re-layouts: 15.7 us -> 0.26 us  [local(): got = swap(kept[count:].astype(jnp.bfloat16), 'expert', distance)]
    all_to_all x2 -> x1, blocking collectives: 60.3 us -> 75.2 us  [local(): moved = lax.all_to_all(piece, ALL, split_axis=0, concat_axis=0, tiled=True)]
    ppermute x0 -> x11, starting transfers between devices: none -> 10.7 us  [swap(): return lax.ppermute(value, axis, [(i, i ^ distance) for i in range(count)])]
    transpose x0 -> x2, local copies, waits for them, and re-layouts: none -> 9.88 us  [own_experts(): moved.transpose(1, 0, 2, 3)]
    reduce_sum x3 -> x1, other arithmetic: 7.19 us -> 0.35 us  [local(): jnp.sum(jnp.where(named, mixing[..., None], 0.0), axis=2)]
  transfers between devices with their start and end apart: 2 -> 13, of which waited for: 0 -> 11; matrix products, arithmetic and copies ran while one was open for 3% -> 5% of each run, Pallas kernels for 0% -> 0%
where the time goes in v2:
time: 628 us; the launch traced here: 627 us
  waiting for transfers between devices  317 us (50%)
  blocking collectives  216 us (34%)
  matrix products  42.9 us (7%)
  starting transfers between devices  23.6 us (4%)
  local copies, waits for them, and re-layouts  16.5 us (3%)
  other arithmetic  11 us (2%)
    ppermute x11, waiting for transfers between devices, swap(): return lax.ppermute(value, axis, [(i, i ^ distance) for i in range(count)])  317 us
    all_to_all x1, blocking collectives, own_experts(): moved = lax.all_to_all(parts, ALL, split_axis=0, concat_axis=0, tiled=True)  141 us
    all_to_all x1, blocking collectives, local(): moved = lax.all_to_all(piece, ALL, split_axis=0, concat_axis=0, tiled=True)  75.2 us
    dot_general x2, matrix products, local(): lax.dot_general(hidden[k], w_down, (((1,), (1,)), ((), ())), preferred_el...  29.4 us
    dot_general x2, matrix products, local(): up_act = jnp.dot(rows_all, w_up[k], preferred_element_type=jnp.float32)  13.4 us
  transfers between devices with their start and end apart: 13, of which 11 were waited for; matrix products, arithmetic and copies ran while one was open for 5% of the time, Pallas kernels for 0%

profile of v2, /device:TPU:0, one launch (start us, length us, event | category | flops | bytes accessed | tf_op | source)
XLA Modules:
  0.0 627.1 jit_solution(2150059599494838046)
XLA Ops:
  0.0 7.6 %all-to-all-start = ((bf16[16,2,128,768]{3,2,1,0:T(8,128)(2,1)}), bf16[16,2,128,768]{3,2,1,0:T(8,128)(2,1)}, u32[]{:S(2)}, u32[]{:S(2)}) async-start(bf16[16,2,128,768]{3,2,1,0:T(8,128)(2,1)} %bitcast.46), calls=%async_computation | async-start | bytes 12582912 | tf_op jit(solution)/shard_map/all_to_all | solution.py:14
  7.6 2.8 collective-permute-start
  10.5 147.3 %collective-permute-done = bf16[128,1024]{1,0:T(8,128)(2,1)S(1)} collective-permute-done((bf16[128,1024]{1,0:T(8,128)(2,1)S(1)}, bf16[128,1024]{1,0:T(8,128)(2,1)S(1)}, u32[]{:S(2)}, u32[]{:S(2)}) %collective-permute-start) | collective-permute-done | bytes 262176 | tf_op jit(solution)/shard_map/ppermute | solution.py:20
  157.9 13.5 %collective-permute-done.1 = bf16[256,1024]{1,0:T(8,128)(2,1)S(1)} collective-permute-done((bf16[256,1024]{1,0:T(8,128)(2,1)S(1)}, bf16[256,1024]{1,0:T(8,128)(2,1)S(1)}, u32[]{:S(2)}, u32[]{:S(2)}) %collective-permute-start.1) | collective-permute-done | bytes 524320 | tf_op jit(solution)/shard_map/ppermute | solution.py:20
  172.9 22.3 %collective-permute-done.2 = bf16[512,1024]{1,0:T(8,128)(2,1)S(1)} collective-permute-done((bf16[512,1024]{1,0:T(8,128)(2,1)S(1)}, bf16[512,1024]{1,0:T(8,128)(2,1)S(1)}, u32[]{:S(2)}, u32[]{:S(2)}) %collective-permute-start.2) | collective-permute-done | bytes 1048608 | tf_op jit(solution)/shard_map/ppermute | solution.py:20
  196.8 4.5 collective-permute-done.3
  206.2 6.3 copy.15
  212.5 140.6 %all_to_all.20 = bf16[16,2,128,768]{3,2,1,0:T(8,128)(2,1)S(1)} all-to-all(bf16[16,2,128,768]{3,2,1,0:T(8,128)(2,1)S(1)} %bitcast.49), channel_id=1, replica_groups=mesh['groups'=2,'expert'=8,'tensor'=2] {'expert','tensor'}, dimensions={0} | all-to-all | bytes 12582912 | tf_op jit(solution)/shard_map/all_to_all | solution.py:14
  353.1 3.6 copy.16
  360.3 75.2 %all_to_all.21 = bf16[16,128,768]{2,1,0:T(8,128)(2,1)} all-to-all(bf16[16,128,768]{2,1,0:T(8,128)(2,1)S(1)} %get-tuple-element.18), channel_id=1, replica_groups=mesh['groups'=2,'expert'=8,'tensor'=2] {'expert','tensor'}, dimensions={0} | all-to-all | bytes 6291456 | tf_op jit(solution)/shard_map/all_to_all | solution.py:71
  435.5 5.4 all-to-all-start.3
  441.5 2.8 collective-permute-start.4
  444.3 68.8 %collective-permute-done.4 = f32[128,32]{0,1:T(8,128)S(1)} collective-permute-done((f32[128,32]{0,1:T(8,128)S(1)}, f32[128,32]{0,1:T(8,128)S(1)}, u32[]{:S(2)}, u32[]{:S(2)}) %collective-permute-start.4) | collective-permute-done | bytes 16416 | tf_op jit(solution)/shard_map/ppermute | solution.py:20
  513.1 3.9 collective-permute-done.5
  518.5 2.8 collective-permute-done.6
  521.3 8.4 %fusion = f32[1024,768]{1,0:T(8,128)} fusion(bf16[1024,2048]{1,0:T(8,128)(2,1)} %pad_maximum_fusion, bf16[2,2048,768]{2,1,0:T(8,128)(2,1)} %bitcast.55), kind=kOutput, calls=%fused_computation.6 | convolution fusion | flops 3221225472 | bytes 10485760 | tf_op jit(solution)/shard_map/dot_general | solution.py:62
  529.8 5.0 fusion.4
  534.8 13.9 %fusion.17 = f32[1024,2048]{1,0:T(8,128)} fusion(bf16[2048,768]{1,0:T(8,128)(2,1)} %bitcast.59, f32[1024,768]{1,0:T(8,128)} %fusion.4, bf16[1024,2048]{1,0:T(8,128)(2,1)} %pad_maximum_fusion, bf16[2,2048,768]{2,1,0:T(8,128)(2,1)} %bitcast.53, f32[1024]{0:T(1024)S(1)} %bitcast.62), kind=kOutput, calls=%fused_computation.25 | convolution fusion | flops 6447955968 | bytes 22024192 | tf_op jit(solution)/shard_map/dot_general | solution.py:73
  548.7 15.6 %convolution_add_fusion = f32[1024,2048]{1,0:T(8,128)} fusion(f32[1024,2048]{1,0:T(8,128)} %fusion.17, bf16[2048,768]{1,0:T(8,128)(2,1)} %bitcast.18, f32[1024,768]{1,0:T(8,128)} %fusion, bf16[1024,2048]{1,0:T(8,128)(2,1)} %pad_maximum_fusion, bf16[2,2048,768]{2,1,0:T(8,128)(2,1)} %bitcast.54, f32[1024]{0:T(1024)S(1)} %bitcast.61), kind=kOutput, calls=%fused_computation.3 | convolution fusion | flops 6450053120 | bytes 30412800 | tf_op jit(solution)/shard_map/dot_general | solution.py:73
  566.8 4.1 collective-permute-done.7
  571.0 2.9 convert_add_fusion
  575.6 23.7 %collective-permute-done.8 = bf16[512,1024]{1,0:T(8,128)(2,1)S(1)} collective-permute-done((bf16[512,1024]{1,0:T(8,128)(2,1)S(1)}, bf16[512,1024]{1,0:T(8,128)(2,1)S(1)}, u32[]{:S(2)}, u32[]{:S(2)}) %collective-permute-start.8) | collective-permute-done | bytes 1048608 | tf_op jit(solution)/shard_map/ppermute | solution.py:20
  599.8 13.1 %collective-permute-done.9 = bf16[256,1024]{1,0:T(8,128)(2,1)S(1)} collective-permute-done((bf16[256,1024]{1,0:T(8,128)(2,1)S(1)}, bf16[256,1024]{1,0:T(8,128)(2,1)S(1)}, u32[]{:S(2)}, u32[]{:S(2)}) %collective-permute-start.9) | collective-permute-done | bytes 524320 | tf_op jit(solution)/shard_map/ppermute | solution.py:20
  613.5 12.9 %collective-permute-done.10 = bf16[128,1024]{1,0:T(8,128)(2,1)S(1)} collective-permute-done((bf16[128,1024]{1,0:T(8,128)(2,1)S(1)}, bf16[128,1024]{1,0:T(8,128)(2,1)S(1)}, u32[]{:S(2)}, u32[]{:S(2)}) %collective-permute-start.10) | collective-permute-done | bytes 262176 | tf_op jit(solution)/shard_map/ppermute | solution.py:20
  (58 shorter events, 19.8 us)
Async XLA Ops:
  0.0 7.6 %copy-start = (bf16[4,32,2048]{2,1,0:T(8,128)(2,1)S(1)}, bf16[4,32,2048]{2,1,0:T(8,128)(2,1)}, u32[]{:S(2)}) copy-start(bf16[4,32,2048]{2,1,0:T(8,128)(2,1)} %param.6) | copy-start | bytes 1572868
  0.0 206.2 %all-to-all-start = ((bf16[16,2,128,768]{3,2,1,0:T(8,128)(2,1)}), bf16[16,2,128,768]{3,2,1,0:T(8,128)(2,1)}, u32[]{:S(2)}, u32[]{:S(2)}) async-start(bf16[16,2,128,768]{3,2,1,0:T(8,128)(2,1)} %bitcast.46), calls=%async_computation | async-start | bytes 12582912 | tf_op jit(solution)/shard_map/all_to_all | solution.py:14
  7.6 150.1 %collective-permute-start = (bf16[128,1024]{1,0:T(8,128)(2,1)S(1)}, bf16[128,1024]{1,0:T(8,128)(2,1)S(1)}, u32[]{:S(2)}, u32[]{:S(2)}) collective-permute-start(bf16[128,1024]{1,0:T(8,128)(2,1)S(1)} %constant_dynamic-slice_fusion), channel_id=1, source_target_pairs={{0,8},{2,10},{4,12},{6,14},{8,0},{10,2},{12,4},{14,6},{1,9},{3,11}... | collective-permute-start | bytes 786440 | tf_op jit(solution)/shard_map/ppermute | solution.py:20
  157.8 13.5 %collective-permute-start.1 = (bf16[256,1024]{1,0:T(8,128)(2,1)S(1)}, bf16[256,1024]{1,0:T(8,128)(2,1)S(1)}, u32[]{:S(2)}, u32[]{:S(2)}) collective-permute-start(bf16[256,1024]{1,0:T(8,128)(2,1)S(1)} %pad_maximum_fusion.3), channel_id=1, source_target_pairs={{0,4},{2,6},{4,0},{6,2},{8,12},{10,14},{12,8},{14,10},{1,5},{3,7},... | collective-permute-start | bytes 1572872 | tf_op jit(solution)/shard_map/ppermute | solution.py:20
  171.4 23.9 %collective-permute-start.2 = (bf16[512,1024]{1,0:T(8,128)(2,1)S(1)}, bf16[512,1024]{1,0:T(8,128)(2,1)S(1)}, u32[]{:S(2)}, u32[]{:S(2)}) collective-permute-start(bf16[512,1024]{1,0:T(8,128)(2,1)S(1)} %pad_maximum_fusion.2), channel_id=1, source_target_pairs={{0,2},{2,0},{4,6},{6,4},{8,10},{10,8},{12,14},{14,12},{1,3},{3,1},... | collective-permute-start | bytes 3145736 | tf_op jit(solution)/shard_map/ppermute | solution.py:20
  196.8 4.5 collective-permute-start.3
  206.2 6.3 %slice-start = ((s8[6291456]{0:T(1024)(128)(4,1)}), s8[4194304]{0:T(1024)(128)(4,1)S(1)}, s32[]{:S(2)}) async-start(s8[6291456]{0:T(1024)(128)(4,1)} %bitcast.47), calls=%async_computation.4 | async-start | bytes 8388608
  206.2 6.3 %slice-start.1 = ((s8[6291456]{0:T(1024)(128)(4,1)}), s8[2097152]{0:T(1024)(128)(4,1)S(1)}, s32[]{:S(2)}) async-start(s8[6291456]{0:T(1024)(128)(4,1)} %bitcast.47), calls=%async_computation.5 | async-start | bytes 4194304
  353.1 4.2 slice-start.2
  353.1 5.1 slice-start.3
  435.5 5.4 copy-start.3
  435.5 5.5 copy-start.4
  435.5 113.2 %all-to-all-start.3 = ((bf16[16,128,768]{2,1,0:T(8,128)(2,1)}), bf16[16,128,768]{2,1,0:T(8,128)(2,1)}, u32[]{:S(2)}, u32[]{:S(2)}) async-start(bf16[16,128,768]{2,1,0:T(8,128)(2,1)} %get-tuple-element.16), calls=%async_computation.3 | async-start | bytes 6291456 | tf_op jit(solution)/shard_map/all_to_all | solution.py:71
  441.0 88.7 %slice-start.4 = ((s8[6291456]{0:T(1024)(128)(4,1)}), s8[2097152]{0:T(1024)(128)(4,1)S(1)}, s32[]{:S(2)}) async-start(s8[6291456]{0:T(1024)(128)(4,1)} %bitcast.56), calls=%async_computation.8 | async-start | bytes 4194304
  441.5 71.6 %collective-permute-start.4 = (f32[128,32]{0,1:T(8,128)S(1)}, f32[128,32]{0,1:T(8,128)S(1)}, u32[]{:S(2)}, u32[]{:S(2)}) collective-permute-start(f32[128,32]{0,1:T(8,128)S(1)} %copy.22), channel_id=1, source_target_pairs={{0,8},{2,10},{4,12},{6,14},{8,0},{10,2},{12,4},{14,6},{1,9},{3,11}... | collective-permute-start | bytes 49160 | tf_op jit(solution)/shard_map/ppermute | solution.py:20
  513.1 3.9 collective-permute-start.5
  517.0 4.3 collective-permute-start.6
  521.3 8.4 %slice-start.5 = ((s8[6291456]{0:T(1024)(128)(4,1)}), s8[4194304]{0:T(1024)(128)(4,1)S(1)}, s32[]{:S(2)}) async-start(s8[6291456]{0:T(1024)(128)(4,1)} %bitcast.56), calls=%async_computation.9 | async-start | bytes 8388608
  521.3 8.4 %copy-start.2 = (bf16[1024,2048]{1,0:T(8,128)(2,1)S(1)}, bf16[1024,2048]{1,0:T(8,128)(2,1)}, u32[]{:S(2)}) copy-start(bf16[1024,2048]{1,0:T(8,128)(2,1)} %pad_maximum_fusion) | copy-start | bytes 12582916
  566.8 4.2 collective-permute-start.7
  574.1 25.3 %collective-permute-start.8 = (bf16[512,1024]{1,0:T(8,128)(2,1)S(1)}, bf16[512,1024]{1,0:T(8,128)(2,1)S(1)}, u32[]{:S(2)}, u32[]{:S(2)}) collective-permute-start(bf16[512,1024]{1,0:T(8,128)(2,1)S(1)} %slice.103), channel_id=1, source_target_pairs={{0,2},{2,0},{4,6},{6,4},{8,10},{10,8},{12,14},{14,12},{1,3},{3,1},... | collective-permute-start | bytes 3145736 | tf_op jit(solution)/shard_map/ppermute | solution.py:20
  599.4 27.8 %copy-start.1 = (bf16[4,32,2048]{2,1,0:T(8,128)(2,1)S(1)}, bf16[4,32,2048]{2,1,0:T(8,128)(2,1)}, u32[]{:S(2)}) copy-start(bf16[4,32,2048]{2,1,0:T(8,128)(2,1)} %param.6) | copy-start | bytes 1572868
  599.8 13.2 %collective-permute-start.9 = (bf16[256,1024]{1,0:T(8,128)(2,1)S(1)}, bf16[256,1024]{1,0:T(8,128)(2,1)S(1)}, u32[]{:S(2)}, u32[]{:S(2)}) collective-permute-start(bf16[256,1024]{1,0:T(8,128)(2,1)S(1)} %slice.104), channel_id=1, source_target_pairs={{0,4},{2,6},{4,0},{6,2},{8,12},{10,14},{12,8},{14,10},{1,5},{3,7},... | collective-permute-start | bytes 1572872 | tf_op jit(solution)/shard_map/ppermute | solution.py:20
  613.2 13.2 %collective-permute-start.10 = (bf16[128,1024]{1,0:T(8,128)(2,1)S(1)}, bf16[128,1024]{1,0:T(8,128)(2,1)S(1)}, u32[]{:S(2)}, u32[]{:S(2)}) collective-permute-start(bf16[128,1024]{1,0:T(8,128)(2,1)S(1)} %slice.105), channel_id=1, source_target_pairs={{0,8},{2,10},{4,12},{6,14},{8,0},{10,2},{12,4},{14,6},{1,9},{3,11}... | collective-permute-start | bytes 786440 | tf_op jit(solution)/shard_map/ppermute | solution.py:20

commit v3 on v2

--- a/solution.py
+++ b/solution.py
@@ -20,12 +20,26 @@
     return lax.ppermute(value, axis, [(i, i ^ distance) for i in range(count)])
 
 
-def distances_of(owners):
-    found, distance = [], owners // 2
-    while distance >= 1:
-        found.append(distance)
-        distance //= 2
-    return found
+def orders_of(owners):
+    bits = [bit for bit in range(owners.bit_length() - 1)][::-1]
+    return bits, bits[:1] + bits[1:][::-1]
+
+
+def doubled(value, order):
+    count = len(order)
+    value = value.reshape((1,) * count + value.shape)
+    for bit in order:
+        value = jnp.concatenate([value, swap(value, "expert", 1 << bit)], axis=bit)
+    return value.reshape(-1, value.shape[-1])
+
+
+def halved(value, order, block):
+    value = value.reshape((2,) * len(order) + (block, value.shape[-1]))
+    for bit in order[::-1]:
+        near = lax.slice_in_dim(value, 0, 1, axis=bit)
+        far = lax.slice_in_dim(value, 1, 2, axis=bit).astype(jnp.bfloat16)
+        value = near + swap(far, "expert", 1 << bit).astype(jnp.float32)
+    return value.reshape(block, value.shape[-1])
 
 
 def local(tokens, routes, mixing, gate_weight, up_weight, down_weight):
@@ -37,14 +51,18 @@
     local_count = expert_count // devices
     block = step_count * row_count
     half = model_width // pairs
+    quarter = half // 2
     side = lax.axis_index("tensor")
     me = lax.axis_index("expert") * pairs + side
+    orders = orders_of(owners)
     named = routes[..., None] == jnp.arange(expert_count, dtype=jnp.int32)
     shares = jnp.sum(jnp.where(named, mixing[..., None], 0.0), axis=2).reshape(block, expert_count)
     x_half = lax.dynamic_slice_in_dim(tokens.reshape(block, model_width), side * half, half, axis=1)
-    for distance in distances_of(owners):
-        x_half = jnp.concatenate([x_half, swap(x_half, "expert", distance)], axis=0)
-        shares = jnp.concatenate([shares, swap(shares, "expert", distance)], axis=0)
+    x_half = jnp.concatenate(
+        [doubled(x_half[:, :quarter], orders[0]), doubled(x_half[:, quarter:], orders[1])], axis=1
+    )
+    shares = doubled(shares, orders[0])
+    x_half, shares, gate_weight = lax.optimization_barrier((x_half, shares, gate_weight))
     x_other = swap(x_half, "tensor", 1)
     rows_all = jnp.concatenate(
         [jnp.where(side == 0, x_half, x_other), jnp.where(side == 0, x_other, x_half)], axis=1
@@ -52,7 +70,7 @@
     own_shares = lax.dynamic_slice_in_dim(shares, me * local_count, local_count, axis=1)
 
     w_gate = own_experts(gate_weight)
-    up_weight, rows_all, w_gate = lax.optimization_barrier((up_weight, rows_all, w_gate))
+    up_weight, w_gate = lax.optimization_barrier((up_weight, w_gate))
     w_up = own_experts(up_weight)
     down_weight, w_up = lax.optimization_barrier((down_weight, w_up))
     down_parts = down_weight.reshape(devices, local_count, *down_weight.shape[1:])
@@ -63,25 +81,29 @@
         hidden.append(
             (jax.nn.silu(gate_act) * up_act * own_shares[:, k : k + 1]).astype(jnp.bfloat16)
         )
-    total = None
+    sums = [None, None]
     for k in range(local_count):
         piece = down_parts[:, k]
         if k > 0:
             piece, w_down = lax.optimization_barrier((piece, w_down))
         moved = lax.all_to_all(piece, ALL, split_axis=0, concat_axis=0, tiled=True)
         w_down = moved.reshape(model_width, moved.shape[2])
-        part = lax.dot_general(
-            hidden[k], w_down, (((1,), (1,)), ((), ())), preferred_element_type=jnp.float32
-        )
-        total = part if total is None else total + part
-    kept = lax.dynamic_slice_in_dim(total, side * half, half, axis=1)
-    given = lax.dynamic_slice_in_dim(total, (1 - side) * half, half, axis=1).astype(jnp.bfloat16)
-    kept = kept + swap(given, "tensor", 1).astype(jnp.float32)
-    for distance in reversed(distances_of(owners)):
-        count = kept.shape[0] // 2
-        got = swap(kept[count:].astype(jnp.bfloat16), "expert", distance)
-        kept = kept[:count] + got.astype(jnp.float32)
-    return kept.astype(jnp.bfloat16).reshape(step_count, row_count, half)
+        for index, part_side in enumerate((1 - side, side)):
+            w_part = lax.dynamic_slice_in_dim(w_down, part_side * half, half, axis=0)
+            part = lax.dot_general(
+                hidden[k], w_part, (((1,), (1,)), ((), ())), preferred_element_type=jnp.float32
+            )
+            sums[index] = part if sums[index] is None else sums[index] + part
+    given, kept = sums
+    kept = kept + swap(given.astype(jnp.bfloat16), "tensor", 1).astype(jnp.float32)
+    out = jnp.concatenate(
+        [
+            halved(kept[:, :quarter], orders[0], block),
+            halved(kept[:, quarter:], orders[1], block),
+        ],
+        axis=1,
+    )
+    return out.astype(jnp.bfloat16).reshape(step_count, row_count, half)
 
 
 def solution(mesh):

time: 628 us -> 543 us (0.86)
  waiting for transfers between devices: 317 us -> 140 us
  blocking collectives: 216 us -> 287 us
  starting transfers between devices: 23.6 us -> 62.1 us
  matrix products: 42.9 us -> 32.7 us
  other arithmetic: 11 us -> 4.31 us
    ppermute x11 -> x17, waiting for transfers between devices: 317 us -> 45.6 us  [swap(): return lax.ppermute(value, axis, [(i, i ^ distance) for i in range(count)])]
    all_to_all x1 -> x2, blocking collectives: 141 us -> 287 us  [own_experts(): moved = lax.all_to_all(parts, ALL, split_axis=0, concat_axis=0, tiled=True)]
    all_to_all x1 -> x2, waiting for transfers between devices: 0.01 us -> 94.3 us  [local(): moved = lax.all_to_all(piece, ALL, split_axis=0, concat_axis=0, tiled=True)]
    all_to_all x1 -> x0, blocking collectives: 75.2 us -> none  [local(): moved = lax.all_to_all(piece, ALL, split_axis=0, concat_axis=0, tiled=True)]
    ppermute x11 -> x17, starting transfers between devices: 10.7 us -> 40.9 us  [swap(): return lax.ppermute(value, axis, [(i, i ^ distance) for i in range(count)])]
    all_to_all x1 -> x2, starting transfers between devices: 5.37 us -> 21.2 us  [local(): moved = lax.all_to_all(piece, ALL, split_axis=0, concat_axis=0, tiled=True)]
    all_to_all x1 -> x0, starting transfers between devices: 7.56 us -> none  [own_experts(): moved = lax.all_to_all(parts, ALL, split_axis=0, concat_axis=0, tiled=True)]
    dot_general x2 -> x6, matrix products: 29.4 us -> 25.2 us  [the longest x4 16.4 us: local(): lax.dot_general(hidden[k], w_part, (((1,), (1,)), ((), ())), preferred_el...]
  transfers between devices with their start and end apart: 13 -> 19, of which waited for: 11 -> 13; matrix products, arithmetic and copies ran while one was open for 5% -> 6% of each run, Pallas kernels for 0% -> 0%
where the time goes in v3:
time: 543 us
  blocking collectives  287 us (53%)
  waiting for transfers between devices  140 us (26%)
  starting transfers between devices  62.1 us (11%)
  matrix products  32.7 us (6%)
  local copies, waits for them, and re-layouts  16.7 us (3%)
    all_to_all x2, blocking collectives, own_experts(): moved = lax.all_to_all(parts, ALL, split_axis=0, concat_axis=0, tiled=True)  287 us
    all_to_all x2, waiting for transfers between devices, local(): moved = lax.all_to_all(piece, ALL, split_axis=0, concat_axis=0, tiled=True)  94.3 us
    ppermute x17, waiting for transfers between devices, swap(): return lax.ppermute(value, axis, [(i, i ^ distance) for i in range(count)])  45.6 us
    ppermute x17, starting transfers between devices, swap(): return lax.ppermute(value, axis, [(i, i ^ distance) for i in range(count)])  40.9 us
    all_to_all x2, starting transfers between devices, local(): moved = lax.all_to_all(piece, ALL, split_axis=0, concat_axis=0, tiled=True)  21.2 us
    dot_general x4, matrix products, local(): lax.dot_general(hidden[k], w_part, (((1,), (1,)), ((), ())), preferred_el...  16.4 us
  transfers between devices with their start and end apart: 19, of which 13 were waited for; matrix products, arithmetic and copies ran while one was open for 6% of the time, Pallas kernels for 0%

profile of v3, /device:TPU:0, one launch (start us, length us, event | category | flops | bytes accessed | tf_op | source)
XLA Modules:
  0.0 542.7 jit_solution(14920075599931364510)
XLA Ops:
  1.0 4.1 collective-permute-start
  6.8 8.3 %collective-permute-done = bf16[1,1,1,128,512]{4,3,2,1,0:T(8,128)(2,1)S(1)} collective-permute-done((bf16[1,1,1,128,512]{4,3,2,1,0:T(8,128)(2,1)S(1)}, bf16[1,1,1,128,512]{4,3,2,1,0:T(8,128)(2,1)S(1)}, u32[]{:S(2)}, u32[]{:S(2)}) %collective-permute-start) | collective-permute-done | bytes 131104 | tf_op jit(solution)/shard_map/ppermute | solution.py:20
  27.6 10.6 %collective-permute-done.7 = f32[1,1,2,128,32]{3,4,2,1,0:T(8,128)S(1)} collective-permute-done((f32[1,1,2,128,32]{3,4,2,1,0:T(8,128)S(1)}, f32[1,1,2,128,32]{3,4,2,1,0:T(8,128)S(1)}, u32[]{:S(2)}, u32[]{:S(2)}) %collective-permute-start.7) | collective-permute-done | bytes 32800 | tf_op jit(solution)/shard_map/ppermute | solution.py:20
  43.2 144.1 %all_to_all.20 = bf16[16,2,128,768]{3,2,1,0:T(8,128)(2,1)S(1)} all-to-all(bf16[16,2,128,768]{3,2,1,0:T(8,128)(2,1)} %bitcast.54), channel_id=1, replica_groups=mesh['groups'=2,'expert'=8,'tensor'=2] {'expert','tensor'}, dimensions={0} | all-to-all | bytes 12582912 | tf_op jit(solution)/shard_map/all_to_all | solution.py:14
  187.3 3.6 copy.31
  192.4 142.5 %all_to_all.21 = bf16[16,2,128,768]{3,2,1,0:T(8,128)(2,1)S(1)} all-to-all(bf16[16,2,128,768]{3,2,1,0:T(8,128)(2,1)S(1)} %bitcast.57), channel_id=1, replica_groups=mesh['groups'=2,'expert'=8,'tensor'=2] {'expert','tensor'}, dimensions={0} | all-to-all | bytes 12582912 | tf_op jit(solution)/shard_map/all_to_all | solution.py:14
  334.9 3.6 copy.32
  343.1 5.5 %all-to-all-start.2 = ((bf16[16,128,768]{2,1,0:T(8,128)(2,1)}), bf16[16,128,768]{2,1,0:T(8,128)(2,1)}, u32[]{:S(2)}, u32[]{:S(2)}) async-start(bf16[16,128,768]{2,1,0:T(8,128)(2,1)} %get-tuple-element.22), calls=%async_computation.2 | async-start | bytes 6291456 | tf_op jit(solution)/shard_map/all_to_all | solution.py:89
  349.0 59.1 %all-to-all-done.2 = bf16[16,128,768]{2,1,0:T(8,128)(2,1)} async-done(((bf16[16,128,768]{2,1,0:T(8,128)(2,1)}), bf16[16,128,768]{2,1,0:T(8,128)(2,1)}, u32[]{:S(2)}, u32[]{:S(2)}) %all-to-all-start.2) | async-done | bytes 3145760 | tf_op jit(solution)/shard_map/all_to_all | solution.py:89
  408.0 15.7 %all-to-all-start.3 = ((bf16[16,128,768]{2,1,0:T(8,128)(2,1)}), bf16[16,128,768]{2,1,0:T(8,128)(2,1)}, u32[]{:S(2)}, u32[]{:S(2)}) async-start(bf16[16,128,768]{2,1,0:T(8,128)(2,1)} %get-tuple-element.20), calls=%async_computation.3 | async-start | bytes 6291456 | tf_op jit(solution)/shard_map/all_to_all | solution.py:89
  425.8 5.4 %fusion.2 = f32[1024,768]{1,0:T(8,128)S(1)} fusion(bf16[2,2048,768]{2,1,0:T(8,128)(2,1)} %bitcast.65, bf16[1024,1024]{1,0:T(8,128)(2,1)S(1)} %get-tuple-element.24, bf16[1024,1024]{1,0:T(8,128)(2,1)S(1)} %get-tuple-element.23), kind=kOutput, calls=%fused_computation.7 | convolution fusion | flops 3229614080 | bytes 10485760 | tf_op jit(solution)/shard_map/dot_general | solution.py:79
  431.3 3.4 fusion.6
  434.7 3.7 multiply_convert_fusion.1
  438.5 3.7 multiply_convert_fusion
  442.2 5.4 %fusion.13 = f32[1024,1024]{1,0:T(8,128)} fusion(bf16[1024,768]{1,0:T(8,128)(2,1)S(1)} %multiply_convert_fusion.1, bf16[2048,768]{1,0:T(8,128)(2,1)} %bitcast.17, s32[]{:T(128)S(6)} %select_n.34), kind=kOutput, calls=%fused_computation.23 | convolution fusion | flops 1610612736 | bytes 7340036 | tf_op jit(solution)/shard_map/dot_general | solution.py:93
  447.7 35.3 %all-to-all-done.3 = bf16[16,128,768]{2,1,0:T(8,128)(2,1)} async-done(((bf16[16,128,768]{2,1,0:T(8,128)(2,1)}), bf16[16,128,768]{2,1,0:T(8,128)(2,1)}, u32[]{:S(2)}, u32[]{:S(2)}) %all-to-all-start.3) | async-done | bytes 3145760 | tf_op jit(solution)/shard_map/all_to_all | solution.py:89
  482.9 4.5 add_convert_fusion
  492.1 3.2 convert_add_fusion
  495.4 4.9 collective-permute-start.11
  500.5 8.6 %collective-permute-start.14 = (bf16[2,1,2,128,512]{4,3,2,1,0:T(8,128)(2,1)S(1)}, bf16[2,1,2,128,512]{4,3,2,1,0:T(8,128)(2,1)S(1)}, u32[]{:S(2)}, u32[]{:S(2)}) collective-permute-start(bf16[2,1,2,128,512]{4,3,2,1,0:T(8,128)(2,1)S(1)} %slice.158), channel_id=1, source_target_pairs={{0,4},{2,6},{4,0},{6,2},{8,12},{10,14},{12,8},{14,10},{1,5},{3,7},... | collective-permute-start | bytes 1572872 | tf_op jit(solution)/shard_map/ppermute | solution.py:20
  509.3 3.4 collective-permute-done.11
  512.9 8.6 %collective-permute-start.12 = (bf16[1,1,2,128,512]{4,3,2,1,0:T(8,128)(2,1)S(1)}, bf16[1,1,2,128,512]{4,3,2,1,0:T(8,128)(2,1)S(1)}, u32[]{:S(2)}, u32[]{:S(2)}) collective-permute-start(bf16[1,1,2,128,512]{4,3,2,1,0:T(8,128)(2,1)S(1)} %slice.161), channel_id=1, source_target_pairs={{0,4},{2,6},{4,0},{6,2},{8,12},{10,14},{12,8},{14,10},{1,5},{3,7},... | collective-permute-start | bytes 786440 | tf_op jit(solution)/shard_map/ppermute | solution.py:20
  523.5 4.2 collective-permute-done.12
  531.1 9.0 %collective-permute-done.13 = bf16[1,1,1,128,512]{4,3,2,1,0:T(8,128)(2,1)S(1)} collective-permute-done((bf16[1,1,1,128,512]{4,3,2,1,0:T(8,128)(2,1)S(1)}, bf16[1,1,1,128,512]{4,3,2,1,0:T(8,128)(2,1)S(1)}, u32[]{:S(2)}, u32[]{:S(2)}) %collective-permute-start.13) | collective-permute-done | bytes 131104 | tf_op jit(solution)/shard_map/ppermute | solution.py:20
  (81 shorter events, 41.8 us)
Async XLA Ops:
  1.0 14.0 %collective-permute-start = (bf16[1,1,1,128,512]{4,3,2,1,0:T(8,128)(2,1)S(1)}, bf16[1,1,1,128,512]{4,3,2,1,0:T(8,128)(2,1)S(1)}, u32[]{:S(2)}, u32[]{:S(2)}) collective-permute-start(bf16[1,1,1,128,512]{4,3,2,1,0:T(8,128)(2,1)S(1)} %get-tuple-element.25), channel_id=1, source_target_pairs={{0,8},{2,10},{4,12},{6,14},{8,0},{10,2},{12,4},{14,6},{1,9},{3,11}... | collective-permute-start | bytes 393224 | tf_op jit(solution)/shard_map/ppermute | solution.py:20
  5.1 12.0 %collective-permute-start.3 = (bf16[1,1,1,128,512]{4,3,2,1,0:T(8,128)(2,1)S(1)}, bf16[1,1,1,128,512]{4,3,2,1,0:T(8,128)(2,1)S(1)}, u32[]{:S(2)}, u32[]{:S(2)}) collective-permute-start(bf16[1,1,1,128,512]{4,3,2,1,0:T(8,128)(2,1)S(1)} %get-tuple-element.26), channel_id=1, source_target_pairs={{0,8},{2,10},{4,12},{6,14},{8,0},{10,2},{12,4},{14,6},{1,9},{3,11}... | collective-permute-start | bytes 393224 | tf_op jit(solution)/shard_map/ppermute | solution.py:20
  15.1 7.7 %collective-permute-start.1 = (bf16[1,1,2,128,512]{4,3,2,1,0:T(8,128)(2,1)S(1)}, bf16[1,1,2,128,512]{4,3,2,1,0:T(8,128)(2,1)S(1)}, u32[]{:S(2)}, u32[]{:S(2)}) collective-permute-start(bf16[1,1,2,128,512]{4,3,2,1,0:T(8,128)(2,1)S(1)} %pad_maximum_fusion.6), channel_id=1, source_target_pairs={{0,4},{2,6},{4,0},{6,2},{8,12},{10,14},{12,8},{14,10},{1,5},{3,7},... | collective-permute-start | bytes 786440 | tf_op jit(solution)/shard_map/ppermute | solution.py:20
  17.1 8.3 %collective-permute-start.4 = (bf16[1,1,2,128,512]{4,3,2,1,0:T(8,128)(2,1)S(1)}, bf16[1,1,2,128,512]{4,3,2,1,0:T(8,128)(2,1)S(1)}, u32[]{:S(2)}, u32[]{:S(2)}) collective-permute-start(bf16[1,1,2,128,512]{4,3,2,1,0:T(8,128)(2,1)S(1)} %pad_maximum_fusion.7), channel_id=1, source_target_pairs={{0,2},{2,0},{4,6},{6,4},{8,10},{10,8},{12,14},{14,12},{1,3},{3,1},... | collective-permute-start | bytes 786440 | tf_op jit(solution)/shard_map/ppermute | solution.py:20
  19.2 7.6 %collective-permute-start.6 = (f32[1,1,1,128,32]{3,4,2,1,0:T(8,128)S(1)}, f32[1,1,1,128,32]{3,4,2,1,0:T(8,128)S(1)}, u32[]{:S(2)}, u32[]{:S(2)}) collective-permute-start(f32[1,1,1,128,32]{3,4,2,1,0:T(8,128)S(1)} %copy.29), channel_id=1, source_target_pairs={{0,8},{2,10},{4,12},{6,14},{8,0},{10,2},{12,4},{14,6},{1,9},{3,11}... | collective-permute-start | bytes 49160 | tf_op jit(solution)/shard_map/ppermute | solution.py:20
  22.9 19.8 %collective-permute-start.2 = (bf16[1,2,2,128,512]{4,3,2,1,0:T(8,128)(2,1)S(1)}, bf16[1,2,2,128,512]{4,3,2,1,0:T(8,128)(2,1)S(1)}, u32[]{:S(2)}, u32[]{:S(2)}) collective-permute-start(bf16[1,2,2,128,512]{4,3,2,1,0:T(8,128)(2,1)S(1)} %pad_maximum_fusion.4), channel_id=1, source_target_pairs={{0,2},{2,0},{4,6},{6,4},{8,10},{10,8},{12,14},{14,12},{1,3},{3,1},... | collective-permute-start | bytes 1572872 | tf_op jit(solution)/shard_map/ppermute | solution.py:20
  25.5 17.3 %collective-permute-start.5 = (bf16[2,1,2,128,512]{4,3,2,1,0:T(8,128)(2,1)S(1)}, bf16[2,1,2,128,512]{4,3,2,1,0:T(8,128)(2,1)S(1)}, u32[]{:S(2)}, u32[]{:S(2)}) collective-permute-start(bf16[2,1,2,128,512]{4,3,2,1,0:T(8,128)(2,1)S(1)} %pad_maximum_fusion.5), channel_id=1, source_target_pairs={{0,4},{2,6},{4,0},{6,2},{8,12},{10,14},{12,8},{14,10},{1,5},{3,7},... | collective-permute-start | bytes 1572872 | tf_op jit(solution)/shard_map/ppermute | solution.py:20
  26.8 11.3 %collective-permute-start.7 = (f32[1,1,2,128,32]{3,4,2,1,0:T(8,128)S(1)}, f32[1,1,2,128,32]{3,4,2,1,0:T(8,128)S(1)}, u32[]{:S(2)}, u32[]{:S(2)}) collective-permute-start(f32[1,1,2,128,32]{3,4,2,1,0:T(8,128)S(1)} %pad_maximum_fusion.11), channel_id=1, source_target_pairs={{0,4},{2,6},{4,0},{6,2},{8,12},{10,14},{12,8},{14,10},{1,5},{3,7},... | collective-permute-start | bytes 98312 | tf_op jit(solution)/shard_map/ppermute | solution.py:20
  38.2 4.3 collective-permute-start.8
  187.3 5.1 slice-start.1
  334.9 5.1 slice-start.3
  343.1 65.0 %all-to-all-start.2 = ((bf16[16,128,768]{2,1,0:T(8,128)(2,1)}), bf16[16,128,768]{2,1,0:T(8,128)(2,1)}, u32[]{:S(2)}, u32[]{:S(2)}) async-start(bf16[16,128,768]{2,1,0:T(8,128)(2,1)} %get-tuple-element.22), calls=%async_computation.2 | async-start | bytes 6291456 | tf_op jit(solution)/shard_map/all_to_all | solution.py:89
  348.6 75.1 %collective-permute-start.9 = (bf16[1024,1024]{1,0:T(8,128)(2,1)S(1)}, bf16[1024,1024]{1,0:T(8,128)(2,1)}, u32[]{:S(2)}, u32[]{:S(2)}) collective-permute-start(bf16[1024,1024]{1,0:T(8,128)(2,1)S(1)} %pad_maximum_fusion.1), channel_id=1, source_target_pairs={{0,1},{1,0},{2,3},{3,2},{4,5},{5,4},{6,7},{7,6},{8,9},{9,8},{10,11... | collective-permute-start | bytes 6291464 | tf_op jit(solution)/shard_map/ppermute | solution.py:20
  408.0 74.9 %all-to-all-start.3 = ((bf16[16,128,768]{2,1,0:T(8,128)(2,1)}), bf16[16,128,768]{2,1,0:T(8,128)(2,1)}, u32[]{:S(2)}, u32[]{:S(2)}) async-start(bf16[16,128,768]{2,1,0:T(8,128)(2,1)} %get-tuple-element.20), calls=%async_computation.3 | async-start | bytes 6291456 | tf_op jit(solution)/shard_map/all_to_all | solution.py:89
  423.7 7.5 %slice-start.6 = ((s8[6291456]{0:T(1024)(128)(4,1)}), s8[4194304]{0:T(1024)(128)(4,1)S(1)}, s32[]{:S(2)}) async-start(s8[6291456]{0:T(1024)(128)(4,1)} %bitcast.66), calls=%async_computation.10 | async-start | bytes 8388608
  425.8 5.5 %slice-start.7 = ((s8[6291456]{0:T(1024)(128)(4,1)}), s8[2097152]{0:T(1024)(128)(4,1)S(1)}, s32[]{:S(2)}) async-start(s8[6291456]{0:T(1024)(128)(4,1)} %bitcast.66), calls=%async_computation.11 | async-start | bytes 4194304
  425.8 8.9 %slice-start.4 = ((s8[6291456]{0:T(1024)(128)(4,1)}), s8[4194304]{0:T(1024)(128)(4,1)S(1)}, s32[]{:S(2)}) async-start(s8[6291456]{0:T(1024)(128)(4,1)} %bitcast.61), calls=%async_computation.8 | async-start | bytes 8388608
  487.4 4.6 collective-permute-start.10
  495.4 17.3 %collective-permute-start.11 = (bf16[1,2,2,128,512]{4,3,2,1,0:T(8,128)(2,1)S(1)}, bf16[1,2,2,128,512]{4,3,2,1,0:T(8,128)(2,1)S(1)}, u32[]{:S(2)}, u32[]{:S(2)}) collective-permute-start(bf16[1,2,2,128,512]{4,3,2,1,0:T(8,128)(2,1)S(1)} %bitcast.72), channel_id=1, source_target_pairs={{0,2},{2,0},{4,6},{6,4},{8,10},{10,8},{12,14},{14,12},{1,3},{3,1},... | collective-permute-start | bytes 1572872 | tf_op jit(solution)/shard_map/ppermute | solution.py:20
  500.5 21.0 %collective-permute-start.14 = (bf16[2,1,2,128,512]{4,3,2,1,0:T(8,128)(2,1)S(1)}, bf16[2,1,2,128,512]{4,3,2,1,0:T(8,128)(2,1)S(1)}, u32[]{:S(2)}, u32[]{:S(2)}) collective-permute-start(bf16[2,1,2,128,512]{4,3,2,1,0:T(8,128)(2,1)S(1)} %slice.158), channel_id=1, source_target_pairs={{0,4},{2,6},{4,0},{6,2},{8,12},{10,14},{12,8},{14,10},{1,5},{3,7},... | collective-permute-start | bytes 1572872 | tf_op jit(solution)/shard_map/ppermute | solution.py:20
  512.9 14.9 %collective-permute-start.12 = (bf16[1,1,2,128,512]{4,3,2,1,0:T(8,128)(2,1)S(1)}, bf16[1,1,2,128,512]{4,3,2,1,0:T(8,128)(2,1)S(1)}, u32[]{:S(2)}, u32[]{:S(2)}) collective-permute-start(bf16[1,1,2,128,512]{4,3,2,1,0:T(8,128)(2,1)S(1)} %slice.161), channel_id=1, source_target_pairs={{0,4},{2,6},{4,0},{6,2},{8,12},{10,14},{12,8},{14,10},{1,5},{3,7},... | collective-permute-start | bytes 786440 | tf_op jit(solution)/shard_map/ppermute | solution.py:20
  521.7 8.9 %collective-permute-start.15 = (bf16[1,1,2,128,512]{4,3,2,1,0:T(8,128)(2,1)S(1)}, bf16[1,1,2,128,512]{4,3,2,1,0:T(8,128)(2,1)S(1)}, u32[]{:S(2)}, u32[]{:S(2)}) collective-permute-start(bf16[1,1,2,128,512]{4,3,2,1,0:T(8,128)(2,1)S(1)} %slice.160), channel_id=1, source_target_pairs={{0,2},{2,0},{4,6},{6,4},{8,10},{10,8},{12,14},{14,12},{1,3},{3,1},... | collective-permute-start | bytes 786440 | tf_op jit(solution)/shard_map/ppermute | solution.py:20
  527.9 12.3 %collective-permute-start.13 = (bf16[1,1,1,128,512]{4,3,2,1,0:T(8,128)(2,1)S(1)}, bf16[1,1,1,128,512]{4,3,2,1,0:T(8,128)(2,1)S(1)}, u32[]{:S(2)}, u32[]{:S(2)}) collective-permute-start(bf16[1,1,1,128,512]{4,3,2,1,0:T(8,128)(2,1)S(1)} %slice.163), channel_id=1, source_target_pairs={{0,8},{2,10},{4,12},{6,14},{8,0},{10,2},{12,4},{14,6},{1,9},{3,11}... | collective-permute-start | bytes 393224 | tf_op jit(solution)/shard_map/ppermute | solution.py:20
  530.7 11.2 %collective-permute-start.16 = (bf16[1,1,1,128,512]{4,3,2,1,0:T(8,128)(2,1)S(1)}, bf16[1,1,1,128,512]{4,3,2,1,0:T(8,128)(2,1)S(1)}, u32[]{:S(2)}, u32[]{:S(2)}) collective-permute-start(bf16[1,1,1,128,512]{4,3,2,1,0:T(8,128)(2,1)S(1)} %slice.162), channel_id=1, source_target_pairs={{0,8},{2,10},{4,12},{6,14},{8,0},{10,2},{12,4},{14,6},{1,9},{3,11}... | collective-permute-start | bytes 393224 | tf_op jit(solution)/shard_map/ppermute | solution.py:20
  (3 other events, 11.9 us)

commit v4 on v3

--- a/solution.py
+++ b/solution.py
@@ -4,15 +4,6 @@
 from jax.sharding import PartitionSpec as P
 
 ALL = ("expert", "tensor")
-
-
-def own_experts(weight):
-    devices = lax.axis_size("expert") * lax.axis_size("tensor")
-    expert_count, rows_block, hidden_all = weight.shape
-    local_count = expert_count // devices
-    parts = weight.reshape(devices, local_count, rows_block, hidden_all)
-    moved = lax.all_to_all(parts, ALL, split_axis=0, concat_axis=0, tiled=True)
-    return moved.transpose(1, 0, 2, 3).reshape(local_count, devices * rows_block, hidden_all)
 
 
 def swap(value, axis, distance):
@@ -25,12 +16,8 @@
     return bits, bits[:1] + bits[1:][::-1]
 
 
-def doubled(value, order):
-    count = len(order)
-    value = value.reshape((1,) * count + value.shape)
-    for bit in order:
-        value = jnp.concatenate([value, swap(value, "expert", 1 << bit)], axis=bit)
-    return value.reshape(-1, value.shape[-1])
+def doubled(value, bit):
+    return jnp.concatenate([value, swap(value, "expert", 1 << bit)], axis=bit)
 
 
 def halved(value, order, block):
@@ -58,22 +45,47 @@
     named = routes[..., None] == jnp.arange(expert_count, dtype=jnp.int32)
     shares = jnp.sum(jnp.where(named, mixing[..., None], 0.0), axis=2).reshape(block, expert_count)
     x_half = lax.dynamic_slice_in_dim(tokens.reshape(block, model_width), side * half, half, axis=1)
-    x_half = jnp.concatenate(
-        [doubled(x_half[:, :quarter], orders[0]), doubled(x_half[:, quarter:], orders[1])], axis=1
+    ones = (1,) * len(orders[0])
+    state = (
+        x_half[:, :quarter].reshape(ones + (block, quarter)),
+        x_half[:, quarter:].reshape(ones + (block, half - quarter)),
+        shares.reshape(ones + (block, expert_count)),
     )
-    shares = doubled(shares, orders[0])
-    x_half, shares, gate_weight = lax.optimization_barrier((x_half, shares, gate_weight))
-    x_other = swap(x_half, "tensor", 1)
+
+    def advance(state, stage):
+        if stage < len(orders[0]):
+            first, second = orders[0][stage], orders[1][stage]
+            return doubled(state[0], first), doubled(state[1], second), doubled(state[2], first)
+        x_half = jnp.concatenate(
+            [state[0].reshape(-1, quarter), state[1].reshape(-1, half - quarter)], axis=1
+        )
+        return x_half, swap(x_half, "tensor", 1), state[2].reshape(-1, expert_count)
+
+    stages = len(orders[0]) + 1
+    pieces = []
+    for weight in (gate_weight, up_weight, down_weight):
+        parts = weight.reshape(devices, local_count, *weight.shape[1:])
+        pieces += [parts[:, k] for k in range(local_count)]
+    moved = []
+    for index, piece in enumerate(pieces):
+        if index > 0 and index <= stages:
+            piece, state, moved[-1] = lax.optimization_barrier((piece, state, moved[-1]))
+        elif index > 0:
+            piece, moved[-1] = lax.optimization_barrier((piece, moved[-1]))
+        if index < stages:
+            state = advance(state, index)
+        moved.append(lax.all_to_all(piece, ALL, split_axis=0, concat_axis=0, tiled=True))
+    for stage in range(len(pieces), stages):
+        state = advance(state, stage)
+    x_half, x_other, shares = state
     rows_all = jnp.concatenate(
         [jnp.where(side == 0, x_half, x_other), jnp.where(side == 0, x_other, x_half)], axis=1
     )
     own_shares = lax.dynamic_slice_in_dim(shares, me * local_count, local_count, axis=1)
-
-    w_gate = own_experts(gate_weight)
-    up_weight, w_gate = lax.optimization_barrier((up_weight, w_gate))
-    w_up = own_experts(up_weight)
-    down_weight, w_up = lax.optimization_barrier((down_weight, w_up))
-    down_parts = down_weight.reshape(devices, local_count, *down_weight.shape[1:])
+    moved = [value.reshape(model_width, value.shape[2]) for value in moved]
+    w_gate, w_up, w_downs = [
+        moved[i * local_count : (i + 1) * local_count] for i in range(3)
+    ]
     hidden = []
     for k in range(local_count):
         gate_act = jnp.dot(rows_all, w_gate[k], preferred_element_type=jnp.float32)
@@ -83,11 +95,7 @@
         )
     sums = [None, None]
     for k in range(local_count):
-        piece = down_parts[:, k]
-        if k > 0:
-            piece, w_down = lax.optimization_barrier((piece, w_down))
-        moved = lax.all_to_all(piece, ALL, split_axis=0, concat_axis=0, tiled=True)
-        w_down = moved.reshape(model_width, moved.shape[2])
+        w_down = w_downs[k]
         for index, part_side in enumerate((1 - side, side)):
             w_part = lax.dynamic_slice_in_dim(w_down, part_side * half, half, axis=0)
             part = lax.dot_general(

time: 543 us -> 522 us (0.961)
  blocking collectives: 287 us -> 85.1 us
  waiting for transfers between devices: 140 us -> 292 us
  starting transfers between devices: 62.1 us -> 78.8 us
    all_to_all x2 -> x1, blocking collectives: 287 us -> 85.1 us  [local(): lax.all_to_all(piece, ALL, split_axis=0, concat_axis=0, tiled=True)]
    ppermute x17, waiting for transfers between devices: 45.6 us -> 208 us  [swap(): return lax.ppermute(value, axis, [(i, i ^ distance) for i in range(count)])]
    all_to_all x2 -> x5, starting transfers between devices: 21.2 us -> 42.7 us  [local(): lax.all_to_all(piece, ALL, split_axis=0, concat_axis=0, tiled=True)]
    squeeze x1 -> x3, local copies, waits for them, and re-layouts: 3.05 us -> 17.3 us  [local(): pieces += [parts[:, k] for k in range(local_count)]]
    all_to_all x2 -> x5, waiting for transfers between devices: 94.3 us -> 83.8 us  [local(): lax.all_to_all(piece, ALL, split_axis=0, concat_axis=0, tiled=True)]
    transpose x2 -> x0, local copies, waits for them, and re-layouts: 7.22 us -> none  [own_experts(): moved.transpose(1, 0, 2, 3)]
    dot_general x2, matrix products: 7.46 us -> 13.2 us  [local(): up_act = jnp.dot(rows_all, w_up[k], preferred_element_type=jnp.float32)]
  transfers between devices with their start and end apart: 19 -> 22, of which waited for: 13 -> 13; matrix products, arithmetic and copies ran while one was open for 6% -> 10% of each run, Pallas kernels for 0% -> 0%
where the time goes in v4:
time: 522 us
  waiting for transfers between devices  292 us (56%)
  blocking collectives  85.1 us (16%)
  starting transfers between devices  78.8 us (15%)
  matrix products  34 us (7%)
  local copies, waits for them, and re-layouts  22.1 us (4%)
  other arithmetic  9.42 us (2%)
    ppermute x17, waiting for transfers between devices, swap(): return lax.ppermute(value, axis, [(i, i ^ distance) for i in range(count)])  208 us
    all_to_all x1, blocking collectives, local(): lax.all_to_all(piece, ALL, split_axis=0, concat_axis=0, tiled=True)  85.1 us
    all_to_all x5, waiting for transfers between devices, local(): lax.all_to_all(piece, ALL, split_axis=0, concat_axis=0, tiled=True)  83.8 us
    all_to_all x5, starting transfers between devices, local(): lax.all_to_all(piece, ALL, split_axis=0, concat_axis=0, tiled=True)  42.7 us
    ppermute x17, starting transfers between devices, swap(): return lax.ppermute(value, axis, [(i, i ^ distance) for i in range(count)])  36.2 us
    squeeze x3, local copies, waits for them, and re-layouts, local(): pieces += [parts[:, k] for k in range(local_count)]  17.3 us
    dot_general x2, matrix products, local(): up_act = jnp.dot(rows_all, w_up[k], preferred_element_type=jnp.float32)  13.2 us
    dot_general x4, matrix products, local(): lax.dot_general(hidden[k], w_part, (((1,), (1,)), ((), ())), preferred_el...  12.1 us
  transfers between devices with their start and end apart: 22, of which 13 were waited for; matrix products, arithmetic and copies ran while one was open for 10% of the time, Pallas kernels for 0%

profile of v4, /device:TPU:0, one launch (start us, length us, event | category | flops | bytes accessed | tf_op | source)
XLA Modules:
  0.0 521.8 jit_solution(3288205197390672229)
XLA Ops:
  0.0 6.1 %slice_bitcast_fusion.1 = (bf16[16,128,768]{2,1,0:T(8,128)(2,1)}, bf16[16,128,768]{2,1,0:T(8,128)(2,1)}) fusion(bf16[16,2,128,768]{3,2,1,0:T(8,128)(2,1)} %bitcast.48), kind=kLoop, calls=%fused_computation.4 | loop fusion | bytes 12582912 | tf_op jit(solution)/shard_map/squeeze | solution.py:68
  6.1 7.5 %all-to-all-start = ((bf16[16,128,768]{2,1,0:T(8,128)(2,1)}), bf16[16,128,768]{2,1,0:T(8,128)(2,1)S(1)}, u32[]{:S(2)}, u32[]{:S(2)}) async-start(bf16[16,128,768]{2,1,0:T(8,128)(2,1)} %get-tuple-element.53), calls=%async_computation | async-start | bytes 6291456 | tf_op jit(solution)/shard_map/all_to_all | solution.py:77
  22.6 72.3 %collective-permute-done.2 = f32[1,1,1,128,32]{3,4,2,1,0:T(8,128)S(1)} collective-permute-done((f32[1,1,1,128,32]{3,4,2,1,0:T(8,128)S(1)}, f32[1,1,1,128,32]{3,4,2,1,0:T(8,128)S(1)}, u32[]{:S(2)}, u32[]{:S(2)}) %collective-permute-start.2) | collective-permute-done | bytes 16416 | tf_op jit(solution)/shard_map/ppermute | solution.py:11
  99.6 4.5 all-to-all-start.1
  107.9 6.2 %slice_bitcast_fusion.3 = (bf16[16,128,768]{2,1,0:T(8,128)(2,1)}, bf16[16,128,768]{2,1,0:T(8,128)(2,1)}) fusion(bf16[16,2,128,768]{3,2,1,0:T(8,128)(2,1)} %bitcast.49), kind=kLoop, calls=%fused_computation.6 | loop fusion | bytes 12582912 | tf_op jit(solution)/shard_map/squeeze | solution.py:68
  114.0 48.0 %collective-permute-done.5 = f32[1,1,2,128,32]{3,4,2,1,0:T(8,128)S(1)} collective-permute-done((f32[1,1,2,128,32]{3,4,2,1,0:T(8,128)S(1)}, f32[1,1,2,128,32]{3,4,2,1,0:T(8,128)S(1)}, u32[]{:S(2)}, u32[]{:S(2)}) %collective-permute-start.5) | collective-permute-done | bytes 32800 | tf_op jit(solution)/shard_map/ppermute | solution.py:11
  163.5 15.5 %all-to-all-start.2 = ((bf16[16,128,768]{2,1,0:T(8,128)(2,1)}), bf16[16,128,768]{2,1,0:T(8,128)(2,1)}, u32[]{:S(2)}, u32[]{:S(2)}) async-start(bf16[16,128,768]{2,1,0:T(8,128)(2,1)} %get-tuple-element.34), calls=%async_computation.2 | async-start | bytes 6291456 | tf_op jit(solution)/shard_map/all_to_all | solution.py:77
  182.9 37.1 %collective-permute-done.8 = f32[1,2,2,128,32]{3,4,2,1,0:T(8,128)S(1)} collective-permute-done((f32[1,2,2,128,32]{3,4,2,1,0:T(8,128)S(1)}, f32[1,2,2,128,32]{3,4,2,1,0:T(8,128)S(1)}, u32[]{:S(2)}, u32[]{:S(2)}) %collective-permute-start.8) | collective-permute-done | bytes 65568 | tf_op jit(solution)/shard_map/ppermute | solution.py:11
  220.1 23.8 %collective-permute-done.7 = bf16[2,1,2,128,512]{4,3,2,1,0:T(8,128)(2,1)S(1)} collective-permute-done((bf16[2,1,2,128,512]{4,3,2,1,0:T(8,128)(2,1)S(1)}, bf16[2,1,2,128,512]{4,3,2,1,0:T(8,128)(2,1)S(1)}, u32[]{:S(2)}, u32[]{:S(2)}) %collective-permute-start.7) | collective-permute-done | bytes 524320 | tf_op jit(solution)/shard_map/ppermute | solution.py:11
  244.0 10.0 %all-to-all-start.3 = ((bf16[16,128,768]{2,1,0:T(8,128)(2,1)}), bf16[16,128,768]{2,1,0:T(8,128)(2,1)}, u32[]{:S(2)}, u32[]{:S(2)}) async-start(bf16[16,128,768]{2,1,0:T(8,128)(2,1)} %get-tuple-element.38), calls=%async_computation.3 | async-start | bytes 6291456 | tf_op jit(solution)/shard_map/all_to_all | solution.py:77
  256.0 5.0 slice_bitcast_fusion
  261.3 52.1 %all-to-all-done.3 = bf16[16,128,768]{2,1,0:T(8,128)(2,1)} async-done(((bf16[16,128,768]{2,1,0:T(8,128)(2,1)}), bf16[16,128,768]{2,1,0:T(8,128)(2,1)}, u32[]{:S(2)}, u32[]{:S(2)}) %all-to-all-start.3) | async-done | bytes 3145760 | tf_op jit(solution)/shard_map/all_to_all | solution.py:77
  313.4 85.1 %all_to_all.30 = bf16[16,128,768]{2,1,0:T(8,128)(2,1)} all-to-all(bf16[16,128,768]{2,1,0:T(8,128)(2,1)S(1)} %get-tuple-element.44), channel_id=1, replica_groups=mesh['groups'=2,'expert'=8,'tensor'=2] {'expert','tensor'}, dimensions={0} | all-to-all | bytes 6291456 | tf_op jit(solution)/shard_map/all_to_all | solution.py:77
  398.5 5.2 all-to-all-start.5
  410.4 5.3 %fusion.12 = f32[1024,768]{1,0:T(8,128)S(1)} fusion(bf16[2048,768]{1,0:T(8,128)(2,1)} %bitcast.19, bf16[1024,1024]{1,0:T(8,128)(2,1)S(1)} %get-tuple-element.56, bf16[1024,1024]{1,0:T(8,128)(2,1)S(1)} %get-tuple-element.55), kind=kOutput, calls=%fused_computation.54 | convolution fusion | flops 3229614080 | bytes 10485760 | tf_op jit(solution)/shard_map/dot_general | solution.py:91
  415.7 5.8 %multiply_convert_fusion.1 = bf16[1024,768]{1,0:T(8,128)(2,1)S(1)} fusion(f32[1024,768]{1,0:T(8,128)S(1)} %fusion.13, bf16[2048,768]{1,0:T(8,128)(2,1)} %bitcast.15, f32[1024]{0:T(1024)S(1)} %bitcast.65, bf16[1024,1024]{1,0:T(8,128)(2,1)S(1)} %get-tuple-element.56, bf16[1024,1024]{1,0:T(8,128)(2,1)S(1)} %get-tuple-element.55), kind=kOutput, calls=%fused_computation.10 | convolution fusion | flops 3235119104 | bytes 12062720 | tf_op jit(solution)/shard_map/dot_general | solution.py:92
  421.5 7.3 %multiply_convert_fusion = bf16[1024,768]{1,0:T(8,128)(2,1)} fusion(f32[1024,768]{1,0:T(8,128)S(1)} %fusion.12, bf16[2048,768]{1,0:T(8,128)(2,1)} %bitcast.20, f32[1024]{0:T(1024)S(1)} %bitcast.64, bf16[1024,1024]{1,0:T(8,128)(2,1)S(1)} %get-tuple-element.56, bf16[1024,1024]{1,0:T(8,128)(2,1)S(1)} %get-tuple-element.55), kind=kOutput, calls=%fused_computation.9 | convolution fusion | flops 3235119104 | bytes 12062720 | tf_op jit(solution)/shard_map/dot_general | solution.py:92
  428.9 3.8 fusion.1
  432.7 30.4 %all-to-all-done.5 = bf16[16,128,768]{2,1,0:T(8,128)(2,1)S(1)} async-done(((bf16[16,128,768]{2,1,0:T(8,128)(2,1)}), bf16[16,128,768]{2,1,0:T(8,128)(2,1)S(1)}, u32[]{:S(2)}, u32[]{:S(2)}) %all-to-all-start.5) | async-done | bytes 3145760 | tf_op jit(solution)/shard_map/all_to_all | solution.py:77
  463.1 4.6 add_convert_fusion
  474.5 10.6 %collective-permute-start.14 = (bf16[2,1,2,128,512]{4,3,2,1,0:T(8,128)(2,1)S(1)}, bf16[2,1,2,128,512]{4,3,2,1,0:T(8,128)(2,1)S(1)}, u32[]{:S(2)}, u32[]{:S(2)}) collective-permute-start(bf16[2,1,2,128,512]{4,3,2,1,0:T(8,128)(2,1)S(1)} %slice.146), channel_id=1, source_target_pairs={{0,4},{2,6},{4,0},{6,2},{8,12},{10,14},{12,8},{14,10},{1,5},{3,7},... | collective-permute-start | bytes 1572872 | tf_op jit(solution)/shard_map/ppermute | solution.py:11
  488.2 9.1 %collective-permute-done.14 = bf16[2,1,2,128,512]{4,3,2,1,0:T(8,128)(2,1)S(1)} collective-permute-done((bf16[2,1,2,128,512]{4,3,2,1,0:T(8,128)(2,1)S(1)}, bf16[2,1,2,128,512]{4,3,2,1,0:T(8,128)(2,1)S(1)}, u32[]{:S(2)}, u32[]{:S(2)}) %collective-permute-start.14) | collective-permute-done | bytes 524320 | tf_op jit(solution)/shard_map/ppermute | solution.py:11
  502.6 4.2 collective-permute-done.15
  510.2 8.7 %collective-permute-done.16 = bf16[1,1,1,128,512]{4,3,2,1,0:T(8,128)(2,1)S(1)} collective-permute-done((bf16[1,1,1,128,512]{4,3,2,1,0:T(8,128)(2,1)S(1)}, bf16[1,1,1,128,512]{4,3,2,1,0:T(8,128)(2,1)S(1)}, u32[]{:S(2)}, u32[]{:S(2)}) %collective-permute-start.16) | collective-permute-done | bytes 131104 | tf_op jit(solution)/shard_map/ppermute | solution.py:11
  (90 shorter events, 53.0 us)
Async XLA Ops:
  6.1 91.8 %all-to-all-start = ((bf16[16,128,768]{2,1,0:T(8,128)(2,1)}), bf16[16,128,768]{2,1,0:T(8,128)(2,1)S(1)}, u32[]{:S(2)}, u32[]{:S(2)}) async-start(bf16[16,128,768]{2,1,0:T(8,128)(2,1)} %get-tuple-element.53), calls=%async_computation | async-start | bytes 6291456 | tf_op jit(solution)/shard_map/all_to_all | solution.py:77
  14.7 80.8 %copy-start.5 = (bf16[1,1,1,128,512]{4,3,2,1,0:T(8,128)(2,1)}, bf16[1,1,1,128,512]{4,3,2,1,0:T(8,128)(2,1)S(1)}, u32[]{:S(2)}) copy-start(bf16[1,1,1,128,512]{4,3,2,1,0:T(8,128)(2,1)S(1)} %get-tuple-element.58) | copy-start | bytes 393220
  14.7 80.8 %collective-permute-start = (bf16[1,1,1,128,512]{4,3,2,1,0:T(8,128)(2,1)S(1)}, bf16[1,1,1,128,512]{4,3,2,1,0:T(8,128)(2,1)}, u32[]{:S(2)}, u32[]{:S(2)}) collective-permute-start(bf16[1,1,1,128,512]{4,3,2,1,0:T(8,128)(2,1)S(1)} %get-tuple-element.58), channel_id=1, source_target_pairs={{0,8},{2,10},{4,12},{6,14},{8,0},{10,2},{12,4},{14,6},{1,9},{3,11}... | collective-permute-start | bytes 393224 | tf_op jit(solution)/shard_map/ppermute | solution.py:11
  19.6 75.2 %collective-permute-start.2 = (f32[1,1,1,128,32]{3,4,2,1,0:T(8,128)S(1)}, f32[1,1,1,128,32]{3,4,2,1,0:T(8,128)S(1)}, u32[]{:S(2)}, u32[]{:S(2)}) collective-permute-start(f32[1,1,1,128,32]{3,4,2,1,0:T(8,128)S(1)} %copy.21), channel_id=1, source_target_pairs={{0,8},{2,10},{4,12},{6,14},{8,0},{10,2},{12,4},{14,6},{1,9},{3,11}... | collective-permute-start | bytes 49160 | tf_op jit(solution)/shard_map/ppermute | solution.py:11
  19.7 77.4 %collective-permute-start.1 = (bf16[1,1,1,128,512]{4,3,2,1,0:T(8,128)(2,1)S(1)}, bf16[1,1,1,128,512]{4,3,2,1,0:T(8,128)(2,1)S(1)}, u32[]{:S(2)}, u32[]{:S(2)}) collective-permute-start(bf16[1,1,1,128,512]{4,3,2,1,0:T(8,128)(2,1)S(1)} %get-tuple-element.57), channel_id=1, source_target_pairs={{0,8},{2,10},{4,12},{6,14},{8,0},{10,2},{12,4},{14,6},{1,9},{3,11}... | collective-permute-start | bytes 393224 | tf_op jit(solution)/shard_map/ppermute | solution.py:11
  99.6 63.9 %all-to-all-start.1 = ((bf16[16,128,768]{2,1,0:T(8,128)(2,1)}), bf16[16,128,768]{2,1,0:T(8,128)(2,1)}, u32[]{:S(2)}, u32[]{:S(2)}) async-start(bf16[16,128,768]{2,1,0:T(8,128)(2,1)} %get-tuple-element.30), calls=%async_computation.1 | async-start | bytes 6291456 | tf_op jit(solution)/shard_map/all_to_all | solution.py:77
  104.1 58.0 %collective-permute-start.3 = (bf16[1,1,2,128,512]{4,3,2,1,0:T(8,128)(2,1)S(1)}, bf16[1,1,2,128,512]{4,3,2,1,0:T(8,128)(2,1)S(1)}, u32[]{:S(2)}, u32[]{:S(2)}) collective-permute-start(bf16[1,1,2,128,512]{4,3,2,1,0:T(8,128)(2,1)S(1)} %pad_maximum_fusion.6), channel_id=1, source_target_pairs={{0,4},{2,6},{4,0},{6,2},{8,12},{10,14},{12,8},{14,10},{1,5},{3,7},... | collective-permute-start | bytes 786440 | tf_op jit(solution)/shard_map/ppermute | solution.py:11
  105.9 56.3 %collective-permute-start.4 = (bf16[1,1,2,128,512]{4,3,2,1,0:T(8,128)(2,1)}, bf16[1,1,2,128,512]{4,3,2,1,0:T(8,128)(2,1)S(1)}, u32[]{:S(2)}, u32[]{:S(2)}) collective-permute-start(bf16[1,1,2,128,512]{4,3,2,1,0:T(8,128)(2,1)} %pad_maximum_fusion.7), channel_id=1, source_target_pairs={{0,2},{2,0},{4,6},{6,4},{8,10},{10,8},{12,14},{14,12},{1,3},{3,1},... | collective-permute-start | bytes 786440 | tf_op jit(solution)/shard_map/ppermute | solution.py:11
  107.3 54.7 %collective-permute-start.5 = (f32[1,1,2,128,32]{3,4,2,1,0:T(8,128)S(1)}, f32[1,1,2,128,32]{3,4,2,1,0:T(8,128)S(1)}, u32[]{:S(2)}, u32[]{:S(2)}) collective-permute-start(f32[1,1,2,128,32]{3,4,2,1,0:T(8,128)S(1)} %copy-done.6), channel_id=1, source_target_pairs={{0,4},{2,6},{4,0},{6,2},{8,12},{10,14},{12,8},{14,10},{1,5},{3,7},... | collective-permute-start | bytes 98312 | tf_op jit(solution)/shard_map/ppermute | solution.py:11
  107.9 54.3 %copy-start.4 = (bf16[1,1,2,128,512]{4,3,2,1,0:T(8,128)(2,1)S(1)}, bf16[1,1,2,128,512]{4,3,2,1,0:T(8,128)(2,1)}, u32[]{:S(2)}) copy-start(bf16[1,1,2,128,512]{4,3,2,1,0:T(8,128)(2,1)} %pad_maximum_fusion.7) | copy-start | bytes 786436
  163.5 80.5 %all-to-all-start.2 = ((bf16[16,128,768]{2,1,0:T(8,128)(2,1)}), bf16[16,128,768]{2,1,0:T(8,128)(2,1)}, u32[]{:S(2)}, u32[]{:S(2)}) async-start(bf16[16,128,768]{2,1,0:T(8,128)(2,1)} %get-tuple-element.34), calls=%async_computation.2 | async-start | bytes 6291456 | tf_op jit(solution)/shard_map/all_to_all | solution.py:77
  179.0 41.0 %collective-permute-start.6 = (bf16[1,2,2,128,512]{4,3,2,1,0:T(8,128)(2,1)S(1)}, bf16[1,2,2,128,512]{4,3,2,1,0:T(8,128)(2,1)S(1)}, u32[]{:S(2)}, u32[]{:S(2)}) collective-permute-start(bf16[1,2,2,128,512]{4,3,2,1,0:T(8,128)(2,1)S(1)} %pad_maximum_fusion.4), channel_id=1, source_target_pairs={{0,2},{2,0},{4,6},{6,4},{8,10},{10,8},{12,14},{14,12},{1,3},{3,1},... | collective-permute-start | bytes 1572872 | tf_op jit(solution)/shard_map/ppermute | solution.py:11
  180.9 63.0 %collective-permute-start.7 = (bf16[2,1,2,128,512]{4,3,2,1,0:T(8,128)(2,1)S(1)}, bf16[2,1,2,128,512]{4,3,2,1,0:T(8,128)(2,1)S(1)}, u32[]{:S(2)}, u32[]{:S(2)}) collective-permute-start(bf16[2,1,2,128,512]{4,3,2,1,0:T(8,128)(2,1)S(1)} %pad_maximum_fusion.5), channel_id=1, source_target_pairs={{0,4},{2,6},{4,0},{6,2},{8,12},{10,14},{12,8},{14,10},{1,5},{3,7},... | collective-permute-start | bytes 1572872 | tf_op jit(solution)/shard_map/ppermute | solution.py:11
  182.3 37.7 %collective-permute-start.8 = (f32[1,2,2,128,32]{3,4,2,1,0:T(8,128)S(1)}, f32[1,2,2,128,32]{3,4,2,1,0:T(8,128)S(1)}, u32[]{:S(2)}, u32[]{:S(2)}) collective-permute-start(f32[1,2,2,128,32]{3,4,2,1,0:T(8,128)S(1)} %pad_maximum_fusion.10), channel_id=1, source_target_pairs={{0,2},{2,0},{4,6},{6,4},{8,10},{10,8},{12,14},{14,12},{1,3},{3,1},... | collective-permute-start | bytes 196616 | tf_op jit(solution)/shard_map/ppermute | solution.py:11
  244.0 69.4 %all-to-all-start.3 = ((bf16[16,128,768]{2,1,0:T(8,128)(2,1)}), bf16[16,128,768]{2,1,0:T(8,128)(2,1)}, u32[]{:S(2)}, u32[]{:S(2)}) async-start(bf16[16,128,768]{2,1,0:T(8,128)(2,1)} %get-tuple-element.38), calls=%async_computation.3 | async-start | bytes 6291456 | tf_op jit(solution)/shard_map/all_to_all | solution.py:77
  255.7 5.6 %collective-permute-start.9 = (bf16[1024,1024]{1,0:T(8,128)(2,1)}, bf16[1024,1024]{1,0:T(8,128)(2,1)}, u32[]{:S(2)}, u32[]{:S(2)}) collective-permute-start(bf16[1024,1024]{1,0:T(8,128)(2,1)} %pad_maximum_fusion.1), channel_id=1, source_target_pairs={{0,1},{1,0},{2,3},{3,2},{4,5},{5,4},{6,7},{7,6},{8,9},{9,8},{10,11... | collective-permute-start | bytes 6291464 | tf_op jit(solution)/shard_map/ppermute | solution.py:11
  398.5 64.6 %all-to-all-start.5 = ((bf16[16,128,768]{2,1,0:T(8,128)(2,1)}), bf16[16,128,768]{2,1,0:T(8,128)(2,1)S(1)}, u32[]{:S(2)}, u32[]{:S(2)}) async-start(bf16[16,128,768]{2,1,0:T(8,128)(2,1)} %get-tuple-element.48), calls=%async_computation.5 | async-start | bytes 6291456 | tf_op jit(solution)/shard_map/all_to_all | solution.py:77
  467.7 4.6 collective-permute-start.10
  474.5 22.8 %collective-permute-start.14 = (bf16[2,1,2,128,512]{4,3,2,1,0:T(8,128)(2,1)S(1)}, bf16[2,1,2,128,512]{4,3,2,1,0:T(8,128)(2,1)S(1)}, u32[]{:S(2)}, u32[]{:S(2)}) collective-permute-start(bf16[2,1,2,128,512]{4,3,2,1,0:T(8,128)(2,1)S(1)} %slice.146), channel_id=1, source_target_pairs={{0,4},{2,6},{4,0},{6,2},{8,12},{10,14},{12,8},{14,10},{1,5},{3,7},... | collective-permute-start | bytes 1572872 | tf_op jit(solution)/shard_map/ppermute | solution.py:11
  485.2 15.5 %collective-permute-start.11 = (bf16[1,2,2,128,512]{4,3,2,1,0:T(8,128)(2,1)S(1)}, bf16[1,2,2,128,512]{4,3,2,1,0:T(8,128)(2,1)S(1)}, u32[]{:S(2)}, u32[]{:S(2)}) collective-permute-start(bf16[1,2,2,128,512]{4,3,2,1,0:T(8,128)(2,1)S(1)} %bitcast.59), channel_id=1, source_target_pairs={{0,2},{2,0},{4,6},{6,4},{8,10},{10,8},{12,14},{14,12},{1,3},{3,1},... | collective-permute-start | bytes 1572872 | tf_op jit(solution)/shard_map/ppermute | solution.py:11
  497.5 9.4 %collective-permute-start.15 = (bf16[1,1,2,128,512]{4,3,2,1,0:T(8,128)(2,1)S(1)}, bf16[1,1,2,128,512]{4,3,2,1,0:T(8,128)(2,1)S(1)}, u32[]{:S(2)}, u32[]{:S(2)}) collective-permute-start(bf16[1,1,2,128,512]{4,3,2,1,0:T(8,128)(2,1)S(1)} %slice.148), channel_id=1, source_target_pairs={{0,2},{2,0},{4,6},{6,4},{8,10},{10,8},{12,14},{14,12},{1,3},{3,1},... | collective-permute-start | bytes 786440 | tf_op jit(solution)/shard_map/ppermute | solution.py:11
  500.8 8.9 %collective-permute-start.12 = (bf16[1,1,2,128,512]{4,3,2,1,0:T(8,128)(2,1)S(1)}, bf16[1,1,2,128,512]{4,3,2,1,0:T(8,128)(2,1)S(1)}, u32[]{:S(2)}, u32[]{:S(2)}) collective-permute-start(bf16[1,1,2,128,512]{4,3,2,1,0:T(8,128)(2,1)S(1)} %slice.149), channel_id=1, source_target_pairs={{0,4},{2,6},{4,0},{6,2},{8,12},{10,14},{12,8},{14,10},{1,5},{3,7},... | collective-permute-start | bytes 786440 | tf_op jit(solution)/shard_map/ppermute | solution.py:11
  507.0 11.9 %collective-permute-start.16 = (bf16[1,1,1,128,512]{4,3,2,1,0:T(8,128)(2,1)S(1)}, bf16[1,1,1,128,512]{4,3,2,1,0:T(8,128)(2,1)S(1)}, u32[]{:S(2)}, u32[]{:S(2)}) collective-permute-start(bf16[1,1,1,128,512]{4,3,2,1,0:T(8,128)(2,1)S(1)} %slice.150), channel_id=1, source_target_pairs={{0,8},{2,10},{4,12},{6,14},{8,0},{10,2},{12,4},{14,6},{1,9},{3,11}... | collective-permute-start | bytes 393224 | tf_op jit(solution)/shard_map/ppermute | solution.py:11
  509.8 11.2 %collective-permute-start.13 = (bf16[1,1,1,128,512]{4,3,2,1,0:T(8,128)(2,1)S(1)}, bf16[1,1,1,128,512]{4,3,2,1,0:T(8,128)(2,1)S(1)}, u32[]{:S(2)}, u32[]{:S(2)}) collective-permute-start(bf16[1,1,1,128,512]{4,3,2,1,0:T(8,128)(2,1)S(1)} %slice.151), channel_id=1, source_target_pairs={{0,8},{2,10},{4,12},{6,14},{8,0},{10,2},{12,4},{14,6},{1,9},{3,11}... | collective-permute-start | bytes 393224 | tf_op jit(solution)/shard_map/ppermute | solution.py:11
  (10 other events, 67.5 us)

commit v5 on v4

--- a/solution.py
+++ b/solution.py
@@ -64,14 +64,13 @@
     stages = len(orders[0]) + 1
     pieces = []
     for weight in (gate_weight, up_weight, down_weight):
-        parts = weight.reshape(devices, local_count, *weight.shape[1:])
-        pieces += [parts[:, k] for k in range(local_count)]
+        pieces += [weight[k * devices : (k + 1) * devices] for k in range(local_count)]
     moved = []
     for index, piece in enumerate(pieces):
-        if index > 0 and index <= stages:
-            piece, state, moved[-1] = lax.optimization_barrier((piece, state, moved[-1]))
-        elif index > 0:
-            piece, moved[-1] = lax.optimization_barrier((piece, moved[-1]))
+        if index > 1 and index <= stages:
+            piece, state, moved[-2] = lax.optimization_barrier((piece, state, moved[-2]))
+        elif index > 1:
+            piece, moved[-2] = lax.optimization_barrier((piece, moved[-2]))
         if index < stages:
             state = advance(state, index)
         moved.append(lax.all_to_all(piece, ALL, split_axis=0, concat_axis=0, tiled=True))
@@ -81,7 +80,9 @@
     rows_all = jnp.concatenate(
         [jnp.where(side == 0, x_half, x_other), jnp.where(side == 0, x_other, x_half)], axis=1
     )
-    own_shares = lax.dynamic_slice_in_dim(shares, me * local_count, local_count, axis=1)
+    own_shares = [
+        lax.dynamic_slice_in_dim(shares, k * devices + me, 1, axis=1) for k in range(local_count)
+    ]
     moved = [value.reshape(model_width, value.shape[2]) for value in moved]
     w_gate, w_up, w_downs = [
         moved[i * local_count : (i + 1) * local_count] for i in range(3)
@@ -91,7 +92,7 @@
         gate_act = jnp.dot(rows_all, w_gate[k], preferred_element_type=jnp.float32)
         up_act = jnp.dot(rows_all, w_up[k], preferred_element_type=jnp.float32)
         hidden.append(
-            (jax.nn.silu(gate_act) * up_act * own_shares[:, k : k + 1]).astype(jnp.bfloat16)
+            (jax.nn.silu(gate_act) * up_act * own_shares[k]).astype(jnp.bfloat16)
         )
     sums = [None, None]
     for k in range(local_count):

time: 522 us -> 532 us (1.019)
  blocking collectives: 85.1 us -> 77.1 us
  starting transfers between devices: 78.8 us -> 84.8 us
    all_to_all x5, waiting for transfers between devices: 83.8 us -> 143 us  [local(): lax.all_to_all(piece, ALL, split_axis=0, concat_axis=0, tiled=True)]
    ppermute x17, waiting for transfers between devices: 208 us -> 154 us  [swap(): return lax.ppermute(value, axis, [(i, i ^ distance) for i in range(count)])]
    squeeze x3 -> x0, local copies, waits for them, and re-layouts: 17.3 us -> none  [local(): pieces += [parts[:, k] for k in range(local_count)]]
    slice x1 -> x3, local copies, waits for them, and re-layouts: 0.01 us -> 17.3 us  [local(): weight[k * devices:(k + 1) * devices]]
    all_to_all x1, blocking collectives: 85.1 us -> 77.1 us  [local(): lax.all_to_all(piece, ALL, split_axis=0, concat_axis=0, tiled=True)]
    all_to_all x5, starting transfers between devices: 42.7 us -> 48.7 us  [local(): lax.all_to_all(piece, ALL, split_axis=0, concat_axis=0, tiled=True)]
  transfers between devices with their start and end apart: 22 -> 22, of which waited for: 13 -> 12; matrix products, arithmetic and copies ran while one was open for 10% -> 11% of each run, Pallas kernels for 0% -> 0%
where the time goes in v5:
time: 532 us
  waiting for transfers between devices  297 us (56%)
  starting transfers between devices  84.8 us (16%)
  blocking collectives  77.1 us (14%)
  matrix products  35.5 us (7%)
  local copies, waits for them, and re-layouts  24.3 us (5%)
  other arithmetic  12.3 us (2%)
    ppermute x17, waiting for transfers between devices, swap(): return lax.ppermute(value, axis, [(i, i ^ distance) for i in range(count)])  154 us
    all_to_all x5, waiting for transfers between devices, local(): lax.all_to_all(piece, ALL, split_axis=0, concat_axis=0, tiled=True)  143 us
    all_to_all x1, blocking collectives, local(): lax.all_to_all(piece, ALL, split_axis=0, concat_axis=0, tiled=True)  77.1 us
    all_to_all x5, starting transfers between devices, local(): lax.all_to_all(piece, ALL, split_axis=0, concat_axis=0, tiled=True)  48.7 us
    ppermute x17, starting transfers between devices, swap(): return lax.ppermute(value, axis, [(i, i ^ distance) for i in range(count)])  36.1 us
    slice x3, local copies, waits for them, and re-layouts, local(): weight[k * devices:(k + 1) * devices]  17.3 us
    dot_general x4, matrix products, local(): lax.dot_general(hidden[k], w_part, (((1,), (1,)), ((), ())), preferred_el...  16.3 us
    dot_general x2, matrix products, local(): up_act = jnp.dot(rows_all, w_up[k], preferred_element_type=jnp.float32)  12.4 us
  transfers between devices with their start and end apart: 22, of which 12 were waited for; matrix products, arithmetic and copies ran while one was open for 11% of the time, Pallas kernels for 0%

profile of v5, /device:TPU:0, one launch (start us, length us, event | category | flops | bytes accessed | tf_op | source)
XLA Modules:
  0.0 531.5 jit_solution(244164587768757362)
XLA Ops:
  0.0 5.1 fusion.15
  5.1 77.1 %all_to_all.30 = bf16[16,128,768]{2,1,0:T(8,128)(2,1)} all-to-all(bf16[16,128,768]{2,1,0:T(8,128)(2,1)S(1)} %get-tuple-element.42), channel_id=1, replica_groups=mesh['groups'=2,'expert'=8,'tensor'=2] {'expert','tensor'}, dimensions={0} | all-to-all | bytes 6291456 | tf_op jit(solution)/shard_map/all_to_all | solution.py:76
  82.2 5.3 %all-to-all-start.1 = ((bf16[16,128,768]{2,1,0:T(8,128)(2,1)}), bf16[16,128,768]{2,1,0:T(8,128)(2,1)S(1)}, u32[]{:S(2)}, u32[]{:S(2)}) async-start(bf16[16,128,768]{2,1,0:T(8,128)(2,1)} %get-tuple-element.41), calls=%async_computation.1 | async-start | bytes 6291456 | tf_op jit(solution)/shard_map/all_to_all | solution.py:76
  99.2 69.5 %collective-permute-done.4 = f32[1,1,1,128,32]{3,4,2,1,0:T(8,128)S(1)} collective-permute-done((f32[1,1,1,128,32]{3,4,2,1,0:T(8,128)S(1)}, f32[1,1,1,128,32]{3,4,2,1,0:T(8,128)S(1)}, u32[]{:S(2)}, u32[]{:S(2)}) %collective-permute-start.4) | collective-permute-done | bytes 16416 | tf_op jit(solution)/shard_map/ppermute | solution.py:11
  172.6 6.1 %fusion.16 = (bf16[16,128,768]{2,1,0:T(8,128)(2,1)}, bf16[16,128,768]{2,1,0:T(8,128)(2,1)}) fusion(bf16[32,128,768]{2,1,0:T(8,128)(2,1)} %param.10), kind=kLoop, calls=%fused_computation.52 | loop fusion | bytes 12582912 | tf_op jit(solution)/shard_map/slice | solution.py:67
  182.8 4.5 all-to-all-start.2
  191.1 37.1 %collective-permute-done.8 = f32[1,2,2,128,32]{3,4,2,1,0:T(8,128)S(1)} collective-permute-done((f32[1,2,2,128,32]{3,4,2,1,0:T(8,128)S(1)}, f32[1,2,2,128,32]{3,4,2,1,0:T(8,128)S(1)}, u32[]{:S(2)}, u32[]{:S(2)}) %collective-permute-start.8) | collective-permute-done | bytes 65568 | tf_op jit(solution)/shard_map/ppermute | solution.py:11
  229.4 22.8 %collective-permute-done.7 = bf16[2,1,2,128,512]{4,3,2,1,0:T(8,128)(2,1)S(1)} collective-permute-done((bf16[2,1,2,128,512]{4,3,2,1,0:T(8,128)(2,1)}, bf16[2,1,2,128,512]{4,3,2,1,0:T(8,128)(2,1)S(1)}, u32[]{:S(2)}, u32[]{:S(2)}) %collective-permute-start.7) | collective-permute-done | bytes 524320 | tf_op jit(solution)/shard_map/ppermute | solution.py:11
  254.2 8.0 %all-to-all-start.4 = ((bf16[16,128,768]{2,1,0:T(8,128)(2,1)}), bf16[16,128,768]{2,1,0:T(8,128)(2,1)}, u32[]{:S(2)}, u32[]{:S(2)}) async-start(bf16[16,128,768]{2,1,0:T(8,128)(2,1)} %get-tuple-element.36), calls=%async_computation.4 | async-start | bytes 6291456 | tf_op jit(solution)/shard_map/all_to_all | solution.py:76
  264.1 6.1 %fusion.14 = (bf16[16,128,768]{2,1,0:T(8,128)(2,1)}, bf16[16,128,768]{2,1,0:T(8,128)(2,1)}) fusion(bf16[32,128,768]{2,1,0:T(8,128)(2,1)} %param.11), kind=kLoop, calls=%fused_computation.50 | loop fusion | bytes 12582912 | tf_op jit(solution)/shard_map/slice | solution.py:67
  270.5 51.2 %all-to-all-done.4 = bf16[16,128,768]{2,1,0:T(8,128)(2,1)} async-done(((bf16[16,128,768]{2,1,0:T(8,128)(2,1)}), bf16[16,128,768]{2,1,0:T(8,128)(2,1)}, u32[]{:S(2)}, u32[]{:S(2)}) %all-to-all-start.4) | async-done | bytes 3145760 | tf_op jit(solution)/shard_map/all_to_all | solution.py:76
  321.6 15.5 %all-to-all-start.3 = ((bf16[16,128,768]{2,1,0:T(8,128)(2,1)}), bf16[16,128,768]{2,1,0:T(8,128)(2,1)}, u32[]{:S(2)}, u32[]{:S(2)}) async-start(bf16[16,128,768]{2,1,0:T(8,128)(2,1)} %get-tuple-element.34), calls=%async_computation.3 | async-start | bytes 6291456 | tf_op jit(solution)/shard_map/all_to_all | solution.py:76
  337.1 59.4 %all-to-all-done.3 = bf16[16,128,768]{2,1,0:T(8,128)(2,1)} async-done(((bf16[16,128,768]{2,1,0:T(8,128)(2,1)}), bf16[16,128,768]{2,1,0:T(8,128)(2,1)}, u32[]{:S(2)}, u32[]{:S(2)}) %all-to-all-start.3) | async-done | bytes 3145760 | tf_op jit(solution)/shard_map/all_to_all | solution.py:76
  396.5 15.5 %all-to-all-start.5 = ((bf16[16,128,768]{2,1,0:T(8,128)(2,1)}), bf16[16,128,768]{2,1,0:T(8,128)(2,1)}, u32[]{:S(2)}, u32[]{:S(2)}) async-start(bf16[16,128,768]{2,1,0:T(8,128)(2,1)} %get-tuple-element.38), calls=%async_computation.5 | async-start | bytes 6291456 | tf_op jit(solution)/shard_map/all_to_all | solution.py:76
  414.6 3.4 fusion.13
  421.5 5.8 %multiply_convert_fusion.1 = bf16[1024,768]{1,0:T(8,128)(2,1)S(1)} fusion(f32[1024,768]{1,0:T(8,128)S(1)} %fusion.13, bf16[2048,768]{1,0:T(8,128)(2,1)} %bitcast.7, f32[1024]{0:T(1024)S(1)} %bitcast.44, bf16[1024,1024]{1,0:T(8,128)(2,1)S(1)} %get-tuple-element.46, bf16[1024,1024]{1,0:T(8,128)(2,1)S(1)} %get-tuple-element.45), kind=kOutput, calls=%fused_computation.4 | convolution fusion | flops 3235119104 | bytes 12062720 | tf_op jit(solution)/shard_map/dot_general | solution.py:93
  427.3 6.6 %multiply_convert_fusion = bf16[1024,768]{1,0:T(8,128)(2,1)S(1)} fusion(f32[1024,768]{1,0:T(8,128)S(1)} %fusion.12, bf16[2048,768]{1,0:T(8,128)(2,1)} %bitcast.11, f32[1024]{0:T(1024)S(1)} %bitcast.43, bf16[1024,1024]{1,0:T(8,128)(2,1)S(1)} %get-tuple-element.46, bf16[1024,1024]{1,0:T(8,128)(2,1)S(1)} %get-tuple-element.45), kind=kOutput, calls=%fused_computation.3 | convolution fusion | flops 3235119104 | bytes 12062720 | tf_op jit(solution)/shard_map/dot_general | solution.py:93
  433.9 5.2 fusion.1
  439.1 32.4 %all-to-all-done.5 = bf16[16,128,768]{2,1,0:T(8,128)(2,1)} async-done(((bf16[16,128,768]{2,1,0:T(8,128)(2,1)}), bf16[16,128,768]{2,1,0:T(8,128)(2,1)}, u32[]{:S(2)}, u32[]{:S(2)}) %all-to-all-start.5) | async-done | bytes 3145760 | tf_op jit(solution)/shard_map/all_to_all | solution.py:76
  471.5 4.6 add_convert_fusion
  484.2 10.5 %collective-permute-start.14 = (bf16[2,1,2,128,512]{4,3,2,1,0:T(8,128)(2,1)S(1)}, bf16[2,1,2,128,512]{4,3,2,1,0:T(8,128)(2,1)S(1)}, u32[]{:S(2)}, u32[]{:S(2)}) collective-permute-start(bf16[2,1,2,128,512]{4,3,2,1,0:T(8,128)(2,1)S(1)} %slice.126), channel_id=1, source_target_pairs={{0,4},{2,6},{4,0},{6,2},{8,12},{10,14},{12,8},{14,10},{1,5},{3,7},... | collective-permute-start | bytes 1572872 | tf_op jit(solution)/shard_map/ppermute | solution.py:11
  497.9 9.0 %collective-permute-done.14 = bf16[2,1,2,128,512]{4,3,2,1,0:T(8,128)(2,1)S(1)} collective-permute-done((bf16[2,1,2,128,512]{4,3,2,1,0:T(8,128)(2,1)S(1)}, bf16[2,1,2,128,512]{4,3,2,1,0:T(8,128)(2,1)S(1)}, u32[]{:S(2)}, u32[]{:S(2)}) %collective-permute-start.14) | collective-permute-done | bytes 524320 | tf_op jit(solution)/shard_map/ppermute | solution.py:11
  512.4 4.2 collective-permute-done.15
  519.9 8.7 %collective-permute-done.16 = bf16[1,1,1,128,512]{4,3,2,1,0:T(8,128)(2,1)S(1)} collective-permute-done((bf16[1,1,1,128,512]{4,3,2,1,0:T(8,128)(2,1)S(1)}, bf16[1,1,1,128,512]{4,3,2,1,0:T(8,128)(2,1)S(1)}, u32[]{:S(2)}, u32[]{:S(2)}) %collective-permute-start.16) | collective-permute-done | bytes 131104 | tf_op jit(solution)/shard_map/ppermute | solution.py:11
  (80 shorter events, 57.7 us)
Async XLA Ops:
  82.2 9.2 %copy-start.4 = (f32[4,32,8]{1,2,0:T(8,128)S(1)}, f32[4,32,8]{1,2,0:T(8,128)}, u32[]{:S(2)}) copy-start(f32[4,32,8]{1,2,0:T(8,128)} %param.8) | copy-start | bytes 12292
  82.2 98.9 %all-to-all-start.1 = ((bf16[16,128,768]{2,1,0:T(8,128)(2,1)}), bf16[16,128,768]{2,1,0:T(8,128)(2,1)S(1)}, u32[]{:S(2)}, u32[]{:S(2)}) async-start(bf16[16,128,768]{2,1,0:T(8,128)(2,1)} %get-tuple-element.41), calls=%async_computation.1 | async-start | bytes 6291456 | tf_op jit(solution)/shard_map/all_to_all | solution.py:76
  88.5 80.2 %collective-permute-start = (bf16[1,1,1,128,512]{4,3,2,1,0:T(8,128)(2,1)S(1)}, bf16[1,1,1,128,512]{4,3,2,1,0:T(8,128)(2,1)S(1)}, u32[]{:S(2)}, u32[]{:S(2)}) collective-permute-start(bf16[1,1,1,128,512]{4,3,2,1,0:T(8,128)(2,1)S(1)} %get-tuple-element.48), channel_id=1, source_target_pairs={{0,8},{2,10},{4,12},{6,14},{8,0},{10,2},{12,4},{14,6},{1,9},{3,11}... | collective-permute-start | bytes 393224 | tf_op jit(solution)/shard_map/ppermute | solution.py:11
  96.2 72.4 %collective-permute-start.4 = (f32[1,1,1,128,32]{3,4,2,1,0:T(8,128)S(1)}, f32[1,1,1,128,32]{3,4,2,1,0:T(8,128)S(1)}, u32[]{:S(2)}, u32[]{:S(2)}) collective-permute-start(f32[1,1,1,128,32]{3,4,2,1,0:T(8,128)S(1)} %copy.21), channel_id=1, source_target_pairs={{0,8},{2,10},{4,12},{6,14},{8,0},{10,2},{12,4},{14,6},{1,9},{3,11}... | collective-permute-start | bytes 49160 | tf_op jit(solution)/shard_map/ppermute | solution.py:11
  96.4 74.7 %collective-permute-start.2 = (bf16[1,1,1,128,512]{4,3,2,1,0:T(8,128)(2,1)S(1)}, bf16[1,1,1,128,512]{4,3,2,1,0:T(8,128)(2,1)S(1)}, u32[]{:S(2)}, u32[]{:S(2)}) collective-permute-start(bf16[1,1,1,128,512]{4,3,2,1,0:T(8,128)(2,1)S(1)} %get-tuple-element.47), channel_id=1, source_target_pairs={{0,8},{2,10},{4,12},{6,14},{8,0},{10,2},{12,4},{14,6},{1,9},{3,11}... | collective-permute-start | bytes 393224 | tf_op jit(solution)/shard_map/ppermute | solution.py:11
  168.7 10.1 %collective-permute-start.5 = (f32[1,1,2,128,32]{3,4,2,1,0:T(8,128)S(1)}, f32[1,1,2,128,32]{3,4,2,1,0:T(8,128)S(1)}, u32[]{:S(2)}, u32[]{:S(2)}) collective-permute-start(f32[1,1,2,128,32]{3,4,2,1,0:T(8,128)S(1)} %pad_maximum_fusion.11), channel_id=1, source_target_pairs={{0,4},{2,6},{4,0},{6,2},{8,12},{10,14},{12,8},{14,10},{1,5},{3,7},... | collective-permute-start | bytes 98312 | tf_op jit(solution)/shard_map/ppermute | solution.py:11
  168.7 10.7 %collective-permute-start.1 = (bf16[1,1,2,128,512]{4,3,2,1,0:T(8,128)(2,1)S(1)}, bf16[1,1,2,128,512]{4,3,2,1,0:T(8,128)(2,1)S(1)}, u32[]{:S(2)}, u32[]{:S(2)}) collective-permute-start(bf16[1,1,2,128,512]{4,3,2,1,0:T(8,128)(2,1)S(1)} %pad_maximum_fusion.6), channel_id=1, source_target_pairs={{0,4},{2,6},{4,0},{6,2},{8,12},{10,14},{12,8},{14,10},{1,5},{3,7},... | collective-permute-start | bytes 786440 | tf_op jit(solution)/shard_map/ppermute | solution.py:11
  171.1 9.2 %collective-permute-start.3 = (bf16[1,1,2,128,512]{4,3,2,1,0:T(8,128)(2,1)S(1)}, bf16[1,1,2,128,512]{4,3,2,1,0:T(8,128)(2,1)S(1)}, u32[]{:S(2)}, u32[]{:S(2)}) collective-permute-start(bf16[1,1,2,128,512]{4,3,2,1,0:T(8,128)(2,1)S(1)} %pad_maximum_fusion.7), channel_id=1, source_target_pairs={{0,2},{2,0},{4,6},{6,4},{8,10},{10,8},{12,14},{14,12},{1,3},{3,1},... | collective-permute-start | bytes 786440 | tf_op jit(solution)/shard_map/ppermute | solution.py:11
  181.1 9.5 %copy-start.3 = (f32[1,2,2,128,32]{3,4,2,1,0:T(8,128)S(1)}, f32[1,2,2,128,32]{3,4,2,1,0:T(8,128)}, u32[]{:S(2)}) copy-start(f32[1,2,2,128,32]{3,4,2,1,0:T(8,128)} %pad_maximum_fusion.10) | copy-start | bytes 196612
  182.8 71.4 %all-to-all-start.2 = ((bf16[16,128,768]{2,1,0:T(8,128)(2,1)}), bf16[16,128,768]{2,1,0:T(8,128)(2,1)}, u32[]{:S(2)}, u32[]{:S(2)}) async-start(bf16[16,128,768]{2,1,0:T(8,128)(2,1)} %get-tuple-element.28), calls=%async_computation.2 | async-start | bytes 6291456 | tf_op jit(solution)/shard_map/all_to_all | solution.py:76
  187.3 40.9 %collective-permute-start.6 = (bf16[1,2,2,128,512]{4,3,2,1,0:T(8,128)(2,1)}, bf16[1,2,2,128,512]{4,3,2,1,0:T(8,128)(2,1)S(1)}, u32[]{:S(2)}, u32[]{:S(2)}) collective-permute-start(bf16[1,2,2,128,512]{4,3,2,1,0:T(8,128)(2,1)} %pad_maximum_fusion.4), channel_id=1, source_target_pairs={{0,2},{2,0},{4,6},{6,4},{8,10},{10,8},{12,14},{14,12},{1,3},{3,1},... | collective-permute-start | bytes 1572872 | tf_op jit(solution)/shard_map/ppermute | solution.py:11
  189.1 63.1 %collective-permute-start.7 = (bf16[2,1,2,128,512]{4,3,2,1,0:T(8,128)(2,1)}, bf16[2,1,2,128,512]{4,3,2,1,0:T(8,128)(2,1)S(1)}, u32[]{:S(2)}, u32[]{:S(2)}) collective-permute-start(bf16[2,1,2,128,512]{4,3,2,1,0:T(8,128)(2,1)} %pad_maximum_fusion.5), channel_id=1, source_target_pairs={{0,4},{2,6},{4,0},{6,2},{8,12},{10,14},{12,8},{14,10},{1,5},{3,7},... | collective-permute-start | bytes 1572872 | tf_op jit(solution)/shard_map/ppermute | solution.py:11
  190.6 37.6 %collective-permute-start.8 = (f32[1,2,2,128,32]{3,4,2,1,0:T(8,128)S(1)}, f32[1,2,2,128,32]{3,4,2,1,0:T(8,128)S(1)}, u32[]{:S(2)}, u32[]{:S(2)}) collective-permute-start(f32[1,2,2,128,32]{3,4,2,1,0:T(8,128)S(1)} %copy-done.3), channel_id=1, source_target_pairs={{0,2},{2,0},{4,6},{6,4},{8,10},{10,8},{12,14},{14,12},{1,3},{3,1},... | collective-permute-start | bytes 196616 | tf_op jit(solution)/shard_map/ppermute | solution.py:11
  254.2 67.4 %all-to-all-start.4 = ((bf16[16,128,768]{2,1,0:T(8,128)(2,1)}), bf16[16,128,768]{2,1,0:T(8,128)(2,1)}, u32[]{:S(2)}, u32[]{:S(2)}) async-start(bf16[16,128,768]{2,1,0:T(8,128)(2,1)} %get-tuple-element.36), calls=%async_computation.4 | async-start | bytes 6291456 | tf_op jit(solution)/shard_map/all_to_all | solution.py:76
  263.7 6.8 %collective-permute-start.9 = (bf16[1024,1024]{1,0:T(8,128)(2,1)S(1)}, bf16[1024,1024]{1,0:T(8,128)(2,1)}, u32[]{:S(2)}, u32[]{:S(2)}) collective-permute-start(bf16[1024,1024]{1,0:T(8,128)(2,1)S(1)} %pad_maximum_fusion.1), channel_id=1, source_target_pairs={{0,1},{1,0},{2,3},{3,2},{4,5},{5,4},{6,7},{7,6},{8,9},{9,8},{10,11... | collective-permute-start | bytes 6291464 | tf_op jit(solution)/shard_map/ppermute | solution.py:11
  321.6 74.9 %all-to-all-start.3 = ((bf16[16,128,768]{2,1,0:T(8,128)(2,1)}), bf16[16,128,768]{2,1,0:T(8,128)(2,1)}, u32[]{:S(2)}, u32[]{:S(2)}) async-start(bf16[16,128,768]{2,1,0:T(8,128)(2,1)} %get-tuple-element.34), calls=%async_computation.3 | async-start | bytes 6291456 | tf_op jit(solution)/shard_map/all_to_all | solution.py:76
  396.5 74.9 %all-to-all-start.5 = ((bf16[16,128,768]{2,1,0:T(8,128)(2,1)}), bf16[16,128,768]{2,1,0:T(8,128)(2,1)}, u32[]{:S(2)}, u32[]{:S(2)}) async-start(bf16[16,128,768]{2,1,0:T(8,128)(2,1)} %get-tuple-element.38), calls=%async_computation.5 | async-start | bytes 6291456 | tf_op jit(solution)/shard_map/all_to_all | solution.py:76
  476.1 4.6 collective-permute-start.10
  484.2 22.7 %collective-permute-start.14 = (bf16[2,1,2,128,512]{4,3,2,1,0:T(8,128)(2,1)S(1)}, bf16[2,1,2,128,512]{4,3,2,1,0:T(8,128)(2,1)S(1)}, u32[]{:S(2)}, u32[]{:S(2)}) collective-permute-start(bf16[2,1,2,128,512]{4,3,2,1,0:T(8,128)(2,1)S(1)} %slice.126), channel_id=1, source_target_pairs={{0,4},{2,6},{4,0},{6,2},{8,12},{10,14},{12,8},{14,10},{1,5},{3,7},... | collective-permute-start | bytes 1572872 | tf_op jit(solution)/shard_map/ppermute | solution.py:11
  494.8 15.6 %collective-permute-start.11 = (bf16[1,2,2,128,512]{4,3,2,1,0:T(8,128)(2,1)S(1)}, bf16[1,2,2,128,512]{4,3,2,1,0:T(8,128)(2,1)S(1)}, u32[]{:S(2)}, u32[]{:S(2)}) collective-permute-start(bf16[1,2,2,128,512]{4,3,2,1,0:T(8,128)(2,1)S(1)} %bitcast.38), channel_id=1, source_target_pairs={{0,2},{2,0},{4,6},{6,4},{8,10},{10,8},{12,14},{14,12},{1,3},{3,1},... | collective-permute-start | bytes 1572872 | tf_op jit(solution)/shard_map/ppermute | solution.py:11
  507.1 9.5 %collective-permute-start.15 = (bf16[1,1,2,128,512]{4,3,2,1,0:T(8,128)(2,1)S(1)}, bf16[1,1,2,128,512]{4,3,2,1,0:T(8,128)(2,1)S(1)}, u32[]{:S(2)}, u32[]{:S(2)}) collective-permute-start(bf16[1,1,2,128,512]{4,3,2,1,0:T(8,128)(2,1)S(1)} %slice.128), channel_id=1, source_target_pairs={{0,2},{2,0},{4,6},{6,4},{8,10},{10,8},{12,14},{14,12},{1,3},{3,1},... | collective-permute-start | bytes 786440 | tf_op jit(solution)/shard_map/ppermute | solution.py:11
  510.6 8.8 %collective-permute-start.12 = (bf16[1,1,2,128,512]{4,3,2,1,0:T(8,128)(2,1)S(1)}, bf16[1,1,2,128,512]{4,3,2,1,0:T(8,128)(2,1)S(1)}, u32[]{:S(2)}, u32[]{:S(2)}) collective-permute-start(bf16[1,1,2,128,512]{4,3,2,1,0:T(8,128)(2,1)S(1)} %slice.129), channel_id=1, source_target_pairs={{0,4},{2,6},{4,0},{6,2},{8,12},{10,14},{12,8},{14,10},{1,5},{3,7},... | collective-permute-start | bytes 786440 | tf_op jit(solution)/shard_map/ppermute | solution.py:11
  516.7 11.9 %collective-permute-start.16 = (bf16[1,1,1,128,512]{4,3,2,1,0:T(8,128)(2,1)S(1)}, bf16[1,1,1,128,512]{4,3,2,1,0:T(8,128)(2,1)S(1)}, u32[]{:S(2)}, u32[]{:S(2)}) collective-permute-start(bf16[1,1,1,128,512]{4,3,2,1,0:T(8,128)(2,1)S(1)} %slice.130), channel_id=1, source_target_pairs={{0,8},{2,10},{4,12},{6,14},{8,0},{10,2},{12,4},{14,6},{1,9},{3,11}... | collective-permute-start | bytes 393224 | tf_op jit(solution)/shard_map/ppermute | solution.py:11
  519.5 11.2 %collective-permute-start.13 = (bf16[1,1,1,128,512]{4,3,2,1,0:T(8,128)(2,1)S(1)}, bf16[1,1,1,128,512]{4,3,2,1,0:T(8,128)(2,1)S(1)}, u32[]{:S(2)}, u32[]{:S(2)}) collective-permute-start(bf16[1,1,1,128,512]{4,3,2,1,0:T(8,128)(2,1)S(1)} %slice.131), channel_id=1, source_target_pairs={{0,8},{2,10},{4,12},{6,14},{8,0},{10,2},{12,4},{14,6},{1,9},{3,11}... | collective-permute-start | bytes 393224 | tf_op jit(solution)/shard_map/ppermute | solution.py:11
  (5 other events, 19.7 us)

commit v6 on v4

--- a/solution.py
+++ b/solution.py
@@ -62,8 +62,8 @@
         return x_half, swap(x_half, "tensor", 1), state[2].reshape(-1, expert_count)
 
     stages = len(orders[0]) + 1
-    pieces = []
-    for weight in (gate_weight, up_weight, down_weight):
+    pieces = [gate_weight.reshape(devices, local_count, *gate_weight.shape[1:])]
+    for weight in (up_weight, down_weight):
         parts = weight.reshape(devices, local_count, *weight.shape[1:])
         pieces += [parts[:, k] for k in range(local_count)]
     moved = []
@@ -82,6 +82,7 @@
         [jnp.where(side == 0, x_half, x_other), jnp.where(side == 0, x_other, x_half)], axis=1
     )
     own_shares = lax.dynamic_slice_in_dim(shares, me * local_count, local_count, axis=1)
+    moved = [moved[0][:, k] for k in range(local_count)] + moved[1:]
     moved = [value.reshape(model_width, value.shape[2]) for value in moved]
     w_gate, w_up, w_downs = [
         moved[i * local_count : (i + 1) * local_count] for i in range(3)

time: 522 us -> 510 us (0.977)
  blocking collectives: 85.1 us -> 0 us
  waiting for transfers between devices: 292 us -> 361 us
  starting transfers between devices: 78.8 us -> 86.3 us
    all_to_all x1 -> x0, blocking collectives: 85.1 us -> none  [local(): lax.all_to_all(piece, ALL, split_axis=0, concat_axis=0, tiled=True)]
    ppermute x17, waiting for transfers between devices: 208 us -> 276 us  [swap(): return lax.ppermute(value, axis, [(i, i ^ distance) for i in range(count)])]
    all_to_all x5, starting transfers between devices: 42.7 us -> 49.9 us  [local(): lax.all_to_all(piece, ALL, split_axis=0, concat_axis=0, tiled=True)]
    squeeze x3 -> x2, local copies, waits for them, and re-layouts: 17.3 us -> 12.4 us  [local(): pieces += [parts[:, k] for k in range(local_count)]]
  transfers between devices with their start and end apart: 22 -> 22, of which waited for: 13 -> 12; matrix products, arithmetic and copies ran while one was open for 10% -> 10% of each run, Pallas kernels for 0% -> 0%
where the time goes in v6:
time: 510 us; the launch traced here: 509 us
  waiting for transfers between devices  361 us (71%)
  starting transfers between devices  86.3 us (17%)
  matrix products  33.7 us (7%)
  local copies, waits for them, and re-layouts  18.3 us (4%)
  other arithmetic  9.62 us (2%)
    ppermute x17, waiting for transfers between devices, swap(): return lax.ppermute(value, axis, [(i, i ^ distance) for i in range(count)])  276 us
    all_to_all x5, waiting for transfers between devices, local(): lax.all_to_all(piece, ALL, split_axis=0, concat_axis=0, tiled=True)  85.1 us
    all_to_all x5, starting transfers between devices, local(): lax.all_to_all(piece, ALL, split_axis=0, concat_axis=0, tiled=True)  49.9 us
    ppermute x17, starting transfers between devices, swap(): return lax.ppermute(value, axis, [(i, i ^ distance) for i in range(count)])  36.4 us
    dot_general x4, matrix products, local(): lax.dot_general(hidden[k], w_part, (((1,), (1,)), ((), ())), preferred_el...  16.8 us
    squeeze x2, local copies, waits for them, and re-layouts, local(): pieces += [parts[:, k] for k in range(local_count)]  12.4 us
  transfers between devices with their start and end apart: 22, of which 12 were waited for; matrix products, arithmetic and copies ran while one was open for 10% of the time, Pallas kernels for 0%

profile of v6, /device:TPU:0, one launch (start us, length us, event | category | flops | bytes accessed | tf_op | source)
XLA Modules:
  0.0 508.9 jit_solution(6591189605574697025)
XLA Ops:
  0.0 7.6 %all-to-all-start = ((bf16[16,2,128,768]{3,2,1,0:T(8,128)(2,1)}), bf16[16,2,128,768]{3,2,1,0:T(8,128)(2,1)}, u32[]{:S(2)}, u32[]{:S(2)}) async-start(bf16[16,2,128,768]{3,2,1,0:T(8,128)(2,1)} %bitcast.45), calls=%async_computation | async-start | bytes 12582912 | tf_op jit(solution)/shard_map/all_to_all | solution.py:77
  14.0 6.1 %slice_bitcast_fusion.1 = (bf16[16,128,768]{2,1,0:T(8,128)(2,1)}, bf16[16,128,768]{2,1,0:T(8,128)(2,1)}) fusion(bf16[16,2,128,768]{3,2,1,0:T(8,128)(2,1)} %bitcast.44), kind=kLoop, calls=%fused_computation.4 | loop fusion | bytes 12582912 | tf_op jit(solution)/shard_map/squeeze | solution.py:68
  20.2 138.3 %collective-permute-done.2 = f32[1,1,1,128,32]{3,4,2,1,0:T(8,128)S(1)} collective-permute-done((f32[1,1,1,128,32]{3,4,2,1,0:T(8,128)S(1)}, f32[1,1,1,128,32]{3,4,2,1,0:T(8,128)S(1)}, u32[]{:S(2)}, u32[]{:S(2)}) %collective-permute-start.2) | collective-permute-done | bytes 16416 | tf_op jit(solution)/shard_map/ppermute | solution.py:11
  159.3 3.7 all-to-all-start.1
  166.9 54.2 %collective-permute-done.5 = f32[1,1,2,128,32]{3,4,2,1,0:T(8,128)S(1)} collective-permute-done((f32[1,1,2,128,32]{3,4,2,1,0:T(8,128)S(1)}, f32[1,1,2,128,32]{3,4,2,1,0:T(8,128)S(1)}, u32[]{:S(2)}, u32[]{:S(2)}) %collective-permute-start.5) | collective-permute-done | bytes 32800 | tf_op jit(solution)/shard_map/ppermute | solution.py:11
  225.4 14.1 %all-to-all-start.2 = ((bf16[16,128,768]{2,1,0:T(8,128)(2,1)}), bf16[16,128,768]{2,1,0:T(8,128)(2,1)}, u32[]{:S(2)}, u32[]{:S(2)}) async-start(bf16[16,128,768]{2,1,0:T(8,128)(2,1)} %get-tuple-element.32), calls=%async_computation.2 | async-start | bytes 6291456 | tf_op jit(solution)/shard_map/all_to_all | solution.py:77
  243.4 6.2 %slice_bitcast_fusion.2 = (bf16[16,128,768]{2,1,0:T(8,128)(2,1)}, bf16[16,128,768]{2,1,0:T(8,128)(2,1)}) fusion(bf16[16,2,128,768]{3,2,1,0:T(8,128)(2,1)} %bitcast.46), kind=kLoop, calls=%fused_computation.5 | loop fusion | bytes 12582912 | tf_op jit(solution)/shard_map/squeeze | solution.py:68
  249.6 30.9 %collective-permute-done.8 = f32[1,2,2,128,32]{3,4,2,1,0:T(8,128)S(1)} collective-permute-done((f32[1,2,2,128,32]{3,4,2,1,0:T(8,128)S(1)}, f32[1,2,2,128,32]{3,4,2,1,0:T(8,128)S(1)}, u32[]{:S(2)}, u32[]{:S(2)}) %collective-permute-start.8) | collective-permute-done | bytes 65568 | tf_op jit(solution)/shard_map/ppermute | solution.py:11
  280.6 23.8 %collective-permute-done.7 = bf16[2,1,2,128,512]{4,3,2,1,0:T(8,128)(2,1)S(1)} collective-permute-done((bf16[2,1,2,128,512]{4,3,2,1,0:T(8,128)(2,1)}, bf16[2,1,2,128,512]{4,3,2,1,0:T(8,128)(2,1)S(1)}, u32[]{:S(2)}, u32[]{:S(2)}) %collective-permute-start.7) | collective-permute-done | bytes 524320 | tf_op jit(solution)/shard_map/ppermute | solution.py:11
  305.5 9.0 %all-to-all-start.3 = ((bf16[16,128,768]{2,1,0:T(8,128)(2,1)}), bf16[16,128,768]{2,1,0:T(8,128)(2,1)}, u32[]{:S(2)}, u32[]{:S(2)}) async-start(bf16[16,128,768]{2,1,0:T(8,128)(2,1)} %get-tuple-element.36), calls=%async_computation.3 | async-start | bytes 6291456 | tf_op jit(solution)/shard_map/all_to_all | solution.py:77
  316.6 3.7 collective-permute-done.9
  320.3 53.6 %all-to-all-done.3 = bf16[16,128,768]{2,1,0:T(8,128)(2,1)} async-done(((bf16[16,128,768]{2,1,0:T(8,128)(2,1)}), bf16[16,128,768]{2,1,0:T(8,128)(2,1)}, u32[]{:S(2)}, u32[]{:S(2)}) %all-to-all-start.3) | async-done | bytes 3145760 | tf_op jit(solution)/shard_map/all_to_all | solution.py:77
  373.9 15.5 %all-to-all-start.4 = ((bf16[16,128,768]{2,1,0:T(8,128)(2,1)}), bf16[16,128,768]{2,1,0:T(8,128)(2,1)}, u32[]{:S(2)}, u32[]{:S(2)}) async-start(bf16[16,128,768]{2,1,0:T(8,128)(2,1)} %get-tuple-element.44), calls=%async_computation.4 | async-start | bytes 6291456 | tf_op jit(solution)/shard_map/all_to_all | solution.py:77
  394.6 3.4 fusion.13
  398.0 3.9 multiply_convert_fusion.1
  402.0 5.8 %fusion.1 = f32[1024,1024]{1,0:T(8,128)} fusion(bf16[1024,768]{1,0:T(8,128)(2,1)S(1)} %multiply_convert_fusion.1, bf16[2048,768]{1,0:T(8,128)(2,1)} %bitcast.16, s32[]{:T(128)S(6)} %select_n.34), kind=kOutput, calls=%fused_computation.13 | convolution fusion | flops 1610612736 | bytes 7340036 | tf_op jit(solution)/shard_map/dot_general | solution.py:102
  407.8 3.4 fusion.12
  411.2 6.1 %multiply_convert_fusion = bf16[1024,768]{1,0:T(8,128)(2,1)S(1)} fusion(f32[1024,768]{1,0:T(8,128)S(1)} %fusion.12, bf16[2048,768]{1,0:T(8,128)(2,1)} %bitcast.18, f32[1024]{0:T(1024)S(1)} %bitcast.58, bf16[1024,1024]{1,0:T(8,128)(2,1)S(1)} %get-tuple-element.52, bf16[1024,1024]{1,0:T(8,128)(2,1)S(1)} %get-tuple-element.51), kind=kOutput, calls=%fused_computation.7 | convolution fusion | flops 3235119104 | bytes 12062720 | tf_op jit(solution)/shard_map/dot_general | solution.py:93
  417.3 31.5 %all-to-all-done.4 = bf16[16,128,768]{2,1,0:T(8,128)(2,1)} async-done(((bf16[16,128,768]{2,1,0:T(8,128)(2,1)}), bf16[16,128,768]{2,1,0:T(8,128)(2,1)}, u32[]{:S(2)}, u32[]{:S(2)}) %all-to-all-start.4) | async-done | bytes 3145760 | tf_op jit(solution)/shard_map/all_to_all | solution.py:77
  448.8 4.6 add_convert_fusion
  461.6 10.5 %collective-permute-start.14 = (bf16[2,1,2,128,512]{4,3,2,1,0:T(8,128)(2,1)S(1)}, bf16[2,1,2,128,512]{4,3,2,1,0:T(8,128)(2,1)S(1)}, u32[]{:S(2)}, u32[]{:S(2)}) collective-permute-start(bf16[2,1,2,128,512]{4,3,2,1,0:T(8,128)(2,1)S(1)} %slice.142), channel_id=1, source_target_pairs={{0,4},{2,6},{4,0},{6,2},{8,12},{10,14},{12,8},{14,10},{1,5},{3,7},... | collective-permute-start | bytes 1572872 | tf_op jit(solution)/shard_map/ppermute | solution.py:11
  475.3 9.0 %collective-permute-done.14 = bf16[2,1,2,128,512]{4,3,2,1,0:T(8,128)(2,1)S(1)} collective-permute-done((bf16[2,1,2,128,512]{4,3,2,1,0:T(8,128)(2,1)S(1)}, bf16[2,1,2,128,512]{4,3,2,1,0:T(8,128)(2,1)S(1)}, u32[]{:S(2)}, u32[]{:S(2)}) %collective-permute-start.14) | collective-permute-done | bytes 524320 | tf_op jit(solution)/shard_map/ppermute | solution.py:11
  489.7 4.2 collective-permute-done.15
  497.3 8.7 %collective-permute-done.16 = bf16[1,1,1,128,512]{4,3,2,1,0:T(8,128)(2,1)S(1)} collective-permute-done((bf16[1,1,1,128,512]{4,3,2,1,0:T(8,128)(2,1)S(1)}, bf16[1,1,1,128,512]{4,3,2,1,0:T(8,128)(2,1)S(1)}, u32[]{:S(2)}, u32[]{:S(2)}) %collective-permute-start.16) | collective-permute-done | bytes 131104 | tf_op jit(solution)/shard_map/ppermute | solution.py:11
  (83 shorter events, 50.6 us)
Async XLA Ops:
  0.0 159.3 %all-to-all-start = ((bf16[16,2,128,768]{3,2,1,0:T(8,128)(2,1)}), bf16[16,2,128,768]{3,2,1,0:T(8,128)(2,1)}, u32[]{:S(2)}, u32[]{:S(2)}) async-start(bf16[16,2,128,768]{3,2,1,0:T(8,128)(2,1)} %bitcast.45), calls=%async_computation | async-start | bytes 12582912 | tf_op jit(solution)/shard_map/all_to_all | solution.py:77
  7.6 150.8 %collective-permute-start = (bf16[1,1,1,128,512]{4,3,2,1,0:T(8,128)(2,1)S(1)}, bf16[1,1,1,128,512]{4,3,2,1,0:T(8,128)(2,1)S(1)}, u32[]{:S(2)}, u32[]{:S(2)}) collective-permute-start(bf16[1,1,1,128,512]{4,3,2,1,0:T(8,128)(2,1)S(1)} %get-tuple-element.54), channel_id=1, source_target_pairs={{0,8},{2,10},{4,12},{6,14},{8,0},{10,2},{12,4},{14,6},{1,9},{3,11}... | collective-permute-start | bytes 393224 | tf_op jit(solution)/shard_map/ppermute | solution.py:11
  10.5 148.0 %collective-permute-start.1 = (bf16[1,1,1,128,512]{4,3,2,1,0:T(8,128)(2,1)S(1)}, bf16[1,1,1,128,512]{4,3,2,1,0:T(8,128)(2,1)S(1)}, u32[]{:S(2)}, u32[]{:S(2)}) collective-permute-start(bf16[1,1,1,128,512]{4,3,2,1,0:T(8,128)(2,1)S(1)} %get-tuple-element.53), channel_id=1, source_target_pairs={{0,8},{2,10},{4,12},{6,14},{8,0},{10,2},{12,4},{14,6},{1,9},{3,11}... | collective-permute-start | bytes 393224 | tf_op jit(solution)/shard_map/ppermute | solution.py:11
  11.2 147.3 %collective-permute-start.2 = (f32[1,1,1,128,32]{3,4,2,1,0:T(8,128)S(1)}, f32[1,1,1,128,32]{3,4,2,1,0:T(8,128)S(1)}, u32[]{:S(2)}, u32[]{:S(2)}) collective-permute-start(f32[1,1,1,128,32]{3,4,2,1,0:T(8,128)S(1)} %copy.21), channel_id=1, source_target_pairs={{0,8},{2,10},{4,12},{6,14},{8,0},{10,2},{12,4},{14,6},{1,9},{3,11}... | collective-permute-start | bytes 49160 | tf_op jit(solution)/shard_map/ppermute | solution.py:11
  159.3 64.5 %all-to-all-start.1 = ((bf16[16,128,768]{2,1,0:T(8,128)(2,1)}), bf16[16,128,768]{2,1,0:T(8,128)(2,1)S(1)}, u32[]{:S(2)}, u32[]{:S(2)}) async-start(bf16[16,128,768]{2,1,0:T(8,128)(2,1)} %get-tuple-element.28), calls=%async_computation.1 | async-start | bytes 6291456 | tf_op jit(solution)/shard_map/all_to_all | solution.py:77
  163.0 58.1 %collective-permute-start.3 = (bf16[1,1,2,128,512]{4,3,2,1,0:T(8,128)(2,1)S(1)}, bf16[1,1,2,128,512]{4,3,2,1,0:T(8,128)(2,1)S(1)}, u32[]{:S(2)}, u32[]{:S(2)}) collective-permute-start(bf16[1,1,2,128,512]{4,3,2,1,0:T(8,128)(2,1)S(1)} %pad_maximum_fusion.6), channel_id=1, source_target_pairs={{0,4},{2,6},{4,0},{6,2},{8,12},{10,14},{12,8},{14,10},{1,5},{3,7},... | collective-permute-start | bytes 786440 | tf_op jit(solution)/shard_map/ppermute | solution.py:11
  164.8 56.2 %collective-permute-start.5 = (f32[1,1,2,128,32]{3,4,2,1,0:T(8,128)S(1)}, f32[1,1,2,128,32]{3,4,2,1,0:T(8,128)S(1)}, u32[]{:S(2)}, u32[]{:S(2)}) collective-permute-start(f32[1,1,2,128,32]{3,4,2,1,0:T(8,128)S(1)} %pad_maximum_fusion.11), channel_id=1, source_target_pairs={{0,4},{2,6},{4,0},{6,2},{8,12},{10,14},{12,8},{14,10},{1,5},{3,7},... | collective-permute-start | bytes 98312 | tf_op jit(solution)/shard_map/ppermute | solution.py:11
  165.1 56.8 %collective-permute-start.4 = (bf16[1,1,2,128,512]{4,3,2,1,0:T(8,128)(2,1)}, bf16[1,1,2,128,512]{4,3,2,1,0:T(8,128)(2,1)S(1)}, u32[]{:S(2)}, u32[]{:S(2)}) collective-permute-start(bf16[1,1,2,128,512]{4,3,2,1,0:T(8,128)(2,1)} %pad_maximum_fusion.7), channel_id=1, source_target_pairs={{0,2},{2,0},{4,6},{6,4},{8,10},{10,8},{12,14},{14,12},{1,3},{3,1},... | collective-permute-start | bytes 786440 | tf_op jit(solution)/shard_map/ppermute | solution.py:11
  225.4 80.1 %all-to-all-start.2 = ((bf16[16,128,768]{2,1,0:T(8,128)(2,1)}), bf16[16,128,768]{2,1,0:T(8,128)(2,1)}, u32[]{:S(2)}, u32[]{:S(2)}) async-start(bf16[16,128,768]{2,1,0:T(8,128)(2,1)} %get-tuple-element.32), calls=%async_computation.2 | async-start | bytes 6291456 | tf_op jit(solution)/shard_map/all_to_all | solution.py:77
  239.5 41.0 %collective-permute-start.6 = (bf16[1,2,2,128,512]{4,3,2,1,0:T(8,128)(2,1)}, bf16[1,2,2,128,512]{4,3,2,1,0:T(8,128)(2,1)S(1)}, u32[]{:S(2)}, u32[]{:S(2)}) collective-permute-start(bf16[1,2,2,128,512]{4,3,2,1,0:T(8,128)(2,1)} %pad_maximum_fusion.4), channel_id=1, source_target_pairs={{0,2},{2,0},{4,6},{6,4},{8,10},{10,8},{12,14},{14,12},{1,3},{3,1},... | collective-permute-start | bytes 1572872 | tf_op jit(solution)/shard_map/ppermute | solution.py:11
  241.3 63.0 %collective-permute-start.7 = (bf16[2,1,2,128,512]{4,3,2,1,0:T(8,128)(2,1)}, bf16[2,1,2,128,512]{4,3,2,1,0:T(8,128)(2,1)S(1)}, u32[]{:S(2)}, u32[]{:S(2)}) collective-permute-start(bf16[2,1,2,128,512]{4,3,2,1,0:T(8,128)(2,1)} %pad_maximum_fusion.5), channel_id=1, source_target_pairs={{0,4},{2,6},{4,0},{6,2},{8,12},{10,14},{12,8},{14,10},{1,5},{3,7},... | collective-permute-start | bytes 1572872 | tf_op jit(solution)/shard_map/ppermute | solution.py:11
  242.8 37.7 %collective-permute-start.8 = (f32[1,2,2,128,32]{3,4,2,1,0:T(8,128)S(1)}, f32[1,2,2,128,32]{3,4,2,1,0:T(8,128)S(1)}, u32[]{:S(2)}, u32[]{:S(2)}) collective-permute-start(f32[1,2,2,128,32]{3,4,2,1,0:T(8,128)S(1)} %pad_maximum_fusion.10), channel_id=1, source_target_pairs={{0,2},{2,0},{4,6},{6,4},{8,10},{10,8},{12,14},{14,12},{1,3},{3,1},... | collective-permute-start | bytes 196616 | tf_op jit(solution)/shard_map/ppermute | solution.py:11
  243.4 37.1 %copy-start.2 = (bf16[1,2,2,128,512]{4,3,2,1,0:T(8,128)(2,1)S(1)}, bf16[1,2,2,128,512]{4,3,2,1,0:T(8,128)(2,1)}, u32[]{:S(2)}) copy-start(bf16[1,2,2,128,512]{4,3,2,1,0:T(8,128)(2,1)} %pad_maximum_fusion.4) | copy-start | bytes 1572868
  243.4 61.0 %copy-start.3 = (bf16[2,1,2,128,512]{4,3,2,1,0:T(8,128)(2,1)S(1)}, bf16[2,1,2,128,512]{4,3,2,1,0:T(8,128)(2,1)}, u32[]{:S(2)}) copy-start(bf16[2,1,2,128,512]{4,3,2,1,0:T(8,128)(2,1)} %pad_maximum_fusion.5) | copy-start | bytes 1572868
  305.5 68.4 %all-to-all-start.3 = ((bf16[16,128,768]{2,1,0:T(8,128)(2,1)}), bf16[16,128,768]{2,1,0:T(8,128)(2,1)}, u32[]{:S(2)}, u32[]{:S(2)}) async-start(bf16[16,128,768]{2,1,0:T(8,128)(2,1)} %get-tuple-element.36), calls=%async_computation.3 | async-start | bytes 6291456 | tf_op jit(solution)/shard_map/all_to_all | solution.py:77
  316.0 4.4 collective-permute-start.9
  373.9 74.9 %all-to-all-start.4 = ((bf16[16,128,768]{2,1,0:T(8,128)(2,1)}), bf16[16,128,768]{2,1,0:T(8,128)(2,1)}, u32[]{:S(2)}, u32[]{:S(2)}) async-start(bf16[16,128,768]{2,1,0:T(8,128)(2,1)} %get-tuple-element.44), calls=%async_computation.4 | async-start | bytes 6291456 | tf_op jit(solution)/shard_map/all_to_all | solution.py:77
  453.4 4.6 collective-permute-start.10
  461.6 22.7 %collective-permute-start.14 = (bf16[2,1,2,128,512]{4,3,2,1,0:T(8,128)(2,1)S(1)}, bf16[2,1,2,128,512]{4,3,2,1,0:T(8,128)(2,1)S(1)}, u32[]{:S(2)}, u32[]{:S(2)}) collective-permute-start(bf16[2,1,2,128,512]{4,3,2,1,0:T(8,128)(2,1)S(1)} %slice.142), channel_id=1, source_target_pairs={{0,4},{2,6},{4,0},{6,2},{8,12},{10,14},{12,8},{14,10},{1,5},{3,7},... | collective-permute-start | bytes 1572872 | tf_op jit(solution)/shard_map/ppermute | solution.py:11
  472.1 15.6 %collective-permute-start.11 = (bf16[1,2,2,128,512]{4,3,2,1,0:T(8,128)(2,1)S(1)}, bf16[1,2,2,128,512]{4,3,2,1,0:T(8,128)(2,1)S(1)}, u32[]{:S(2)}, u32[]{:S(2)}) collective-permute-start(bf16[1,2,2,128,512]{4,3,2,1,0:T(8,128)(2,1)S(1)} %bitcast.53), channel_id=1, source_target_pairs={{0,2},{2,0},{4,6},{6,4},{8,10},{10,8},{12,14},{14,12},{1,3},{3,1},... | collective-permute-start | bytes 1572872 | tf_op jit(solution)/shard_map/ppermute | solution.py:11
  484.5 9.5 %collective-permute-start.15 = (bf16[1,1,2,128,512]{4,3,2,1,0:T(8,128)(2,1)S(1)}, bf16[1,1,2,128,512]{4,3,2,1,0:T(8,128)(2,1)S(1)}, u32[]{:S(2)}, u32[]{:S(2)}) collective-permute-start(bf16[1,1,2,128,512]{4,3,2,1,0:T(8,128)(2,1)S(1)} %slice.144), channel_id=1, source_target_pairs={{0,2},{2,0},{4,6},{6,4},{8,10},{10,8},{12,14},{14,12},{1,3},{3,1},... | collective-permute-start | bytes 786440 | tf_op jit(solution)/shard_map/ppermute | solution.py:11
  487.9 8.8 %collective-permute-start.12 = (bf16[1,1,2,128,512]{4,3,2,1,0:T(8,128)(2,1)S(1)}, bf16[1,1,2,128,512]{4,3,2,1,0:T(8,128)(2,1)S(1)}, u32[]{:S(2)}, u32[]{:S(2)}) collective-permute-start(bf16[1,1,2,128,512]{4,3,2,1,0:T(8,128)(2,1)S(1)} %slice.145), channel_id=1, source_target_pairs={{0,4},{2,6},{4,0},{6,2},{8,12},{10,14},{12,8},{14,10},{1,5},{3,7},... | collective-permute-start | bytes 786440 | tf_op jit(solution)/shard_map/ppermute | solution.py:11
  494.1 11.9 %collective-permute-start.16 = (bf16[1,1,1,128,512]{4,3,2,1,0:T(8,128)(2,1)S(1)}, bf16[1,1,1,128,512]{4,3,2,1,0:T(8,128)(2,1)S(1)}, u32[]{:S(2)}, u32[]{:S(2)}) collective-permute-start(bf16[1,1,1,128,512]{4,3,2,1,0:T(8,128)(2,1)S(1)} %slice.146), channel_id=1, source_target_pairs={{0,8},{2,10},{4,12},{6,14},{8,0},{10,2},{12,4},{14,6},{1,9},{3,11}... | collective-permute-start | bytes 393224 | tf_op jit(solution)/shard_map/ppermute | solution.py:11
  496.9 11.2 %collective-permute-start.13 = (bf16[1,1,1,128,512]{4,3,2,1,0:T(8,128)(2,1)S(1)}, bf16[1,1,1,128,512]{4,3,2,1,0:T(8,128)(2,1)S(1)}, u32[]{:S(2)}, u32[]{:S(2)}) collective-permute-start(bf16[1,1,1,128,512]{4,3,2,1,0:T(8,128)(2,1)S(1)} %slice.147), channel_id=1, source_target_pairs={{0,8},{2,10},{4,12},{6,14},{8,0},{10,2},{12,4},{14,6},{1,9},{3,11}... | collective-permute-start | bytes 393224 | tf_op jit(solution)/shard_map/ppermute | solution.py:11
  (7 other events, 45.3 us)

commit v7 on v4

--- a/solution.py
+++ b/solution.py
@@ -62,10 +62,11 @@
         return x_half, swap(x_half, "tensor", 1), state[2].reshape(-1, expert_count)
 
     stages = len(orders[0]) + 1
-    pieces = []
-    for weight in (gate_weight, up_weight, down_weight):
-        parts = weight.reshape(devices, local_count, *weight.shape[1:])
-        pieces += [parts[:, k] for k in range(local_count)]
+    gate_parts, up_parts, down_parts = [
+        weight.reshape(devices, local_count, *weight.shape[1:])
+        for weight in (gate_weight, up_weight, down_weight)
+    ]
+    pieces = [gate_parts, up_parts] + [down_parts[:, k] for k in range(local_count)]
     moved = []
     for index, piece in enumerate(pieces):
         if index > 0 and index <= stages:
@@ -82,6 +83,7 @@
         [jnp.where(side == 0, x_half, x_other), jnp.where(side == 0, x_other, x_half)], axis=1
     )
     own_shares = lax.dynamic_slice_in_dim(shares, me * local_count, local_count, axis=1)
+    moved = [both[:, k] for both in moved[:2] for k in range(local_count)] + moved[2:]
     moved = [value.reshape(model_width, value.shape[2]) for value in moved]
     w_gate, w_up, w_downs = [
         moved[i * local_count : (i + 1) * local_count] for i in range(3)

time: 522 us -> 502 us (0.962)
  blocking collectives: 85.1 us -> 0 us
  waiting for transfers between devices: 292 us -> 352 us
  starting transfers between devices: 78.8 us -> 91.9 us
    ppermute x17, waiting for transfers between devices: 208 us -> 323 us  [swap(): return lax.ppermute(value, axis, [(i, i ^ distance) for i in range(count)])]
    all_to_all x1 -> x0, blocking collectives: 85.1 us -> none  [local(): lax.all_to_all(piece, ALL, split_axis=0, concat_axis=0, tiled=True)]
    all_to_all x5 -> x4, waiting for transfers between devices: 83.8 us -> 29.3 us  [local(): lax.all_to_all(piece, ALL, split_axis=0, concat_axis=0, tiled=True)]
    slice x0 -> x2, local copies, waits for them, and re-layouts: none -> 12.3 us  [local(): both[:, k]]
    squeeze x3 -> x1, local copies, waits for them, and re-layouts: 17.3 us -> 6.11 us  [local(): down_parts[:, k]]
    all_to_all x5 -> x4, starting transfers between devices: 42.7 us -> 50.6 us  [local(): lax.all_to_all(piece, ALL, split_axis=0, concat_axis=0, tiled=True)]
  transfers between devices with their start and end apart: 22 -> 21, of which waited for: 13 -> 13; matrix products, arithmetic and copies ran while one was open for 10% -> 9% of each run, Pallas kernels for 0% -> 0%
where the time goes in v7:
time: 502 us
  waiting for transfers between devices  352 us (70%)
  starting transfers between devices  91.9 us (18%)
  matrix products  31.1 us (6%)
  local copies, waits for them, and re-layouts  19.5 us (4%)
  other arithmetic  6.51 us (1%)
    ppermute x17, waiting for transfers between devices, swap(): return lax.ppermute(value, axis, [(i, i ^ distance) for i in range(count)])  323 us
    all_to_all x4, starting transfers between devices, local(): lax.all_to_all(piece, ALL, split_axis=0, concat_axis=0, tiled=True)  50.6 us
    ppermute x17, starting transfers between devices, swap(): return lax.ppermute(value, axis, [(i, i ^ distance) for i in range(count)])  41.3 us
    all_to_all x4, waiting for transfers between devices, local(): lax.all_to_all(piece, ALL, split_axis=0, concat_axis=0, tiled=True)  29.3 us
    dot_general x4, matrix products, local(): lax.dot_general(hidden[k], w_part, (((1,), (1,)), ((), ())), preferred_el...  16.3 us
    slice x2, local copies, waits for them, and re-layouts, local(): both[:, k]  12.3 us
  transfers between devices with their start and end apart: 21, of which 13 were waited for; matrix products, arithmetic and copies ran while one was open for 9% of the time, Pallas kernels for 0%

profile of v7, /device:TPU:0, one launch (start us, length us, event | category | flops | bytes accessed | tf_op | source)
XLA Modules:
  0.0 501.7 jit_solution(3837397719684617271)
XLA Ops:
  0.0 7.6 %all-to-all-start = ((bf16[16,2,128,768]{3,2,1,0:T(8,128)(2,1)}), bf16[16,2,128,768]{3,2,1,0:T(8,128)(2,1)}, u32[]{:S(2)}, u32[]{:S(2)}) async-start(bf16[16,2,128,768]{3,2,1,0:T(8,128)(2,1)} %bitcast.44), calls=%async_computation | async-start | bytes 12582912 | tf_op jit(solution)/shard_map/all_to_all | solution.py:78
  14.0 142.1 %collective-permute-done.2 = f32[1,1,1,128,32]{3,4,2,1,0:T(8,128)S(1)} collective-permute-done((f32[1,1,1,128,32]{3,4,2,1,0:T(8,128)S(1)}, f32[1,1,1,128,32]{3,4,2,1,0:T(8,128)S(1)}, u32[]{:S(2)}, u32[]{:S(2)}) %collective-permute-start.2) | collective-permute-done | bytes 16416 | tf_op jit(solution)/shard_map/ppermute | solution.py:11
  158.5 4.7 all-to-all-start.1
  167.0 6.1 %slice_bitcast_fusion = (bf16[16,128,768]{2,1,0:T(8,128)(2,1)}, bf16[16,128,768]{2,1,0:T(8,128)(2,1)}) fusion(bf16[16,2,128,768]{3,2,1,0:T(8,128)(2,1)} %bitcast.45), kind=kLoop, calls=%fused_computation.3 | loop fusion | bytes 12582912 | tf_op jit(solution)/shard_map/squeeze | solution.py:69
  173.1 93.3 %collective-permute-done.5 = f32[1,1,2,128,32]{3,4,2,1,0:T(8,128)S(1)} collective-permute-done((f32[1,1,2,128,32]{3,4,2,1,0:T(8,128)S(1)}, f32[1,1,2,128,32]{3,4,2,1,0:T(8,128)S(1)}, u32[]{:S(2)}, u32[]{:S(2)}) %collective-permute-start.5) | collective-permute-done | bytes 32800 | tf_op jit(solution)/shard_map/ppermute | solution.py:11
  266.4 5.3 %collective-permute-done.3 = bf16[1,1,2,128,512]{4,3,2,1,0:T(8,128)(2,1)S(1)} collective-permute-done((bf16[1,1,2,128,512]{4,3,2,1,0:T(8,128)(2,1)S(1)}, bf16[1,1,2,128,512]{4,3,2,1,0:T(8,128)(2,1)S(1)}, u32[]{:S(2)}, u32[]{:S(2)}) %collective-permute-start.3) | collective-permute-done | bytes 262176 | tf_op jit(solution)/shard_map/ppermute | solution.py:11
  271.8 5.5 %all-to-all-done.1 = bf16[16,2,128,768]{3,2,1,0:T(8,128)(2,1)} async-done(((bf16[16,2,128,768]{3,2,1,0:T(8,128)(2,1)}), bf16[16,2,128,768]{3,2,1,0:T(8,128)(2,1)}, u32[]{:S(2)}, u32[]{:S(2)}) %all-to-all-start.1) | async-done | bytes 6291488 | tf_op jit(solution)/shard_map/all_to_all | solution.py:78
  277.3 28.1 %all-to-all-start.2 = ((bf16[16,128,768]{2,1,0:T(8,128)(2,1)}), bf16[16,128,768]{2,1,0:T(8,128)(2,1)}, u32[]{:S(2)}, u32[]{:S(2)}) async-start(bf16[16,128,768]{2,1,0:T(8,128)(2,1)} %get-tuple-element.27), calls=%async_computation.2 | async-start | bytes 6291456 | tf_op jit(solution)/shard_map/all_to_all | solution.py:78
  309.3 37.1 %collective-permute-done.8 = f32[1,2,2,128,32]{3,4,2,1,0:T(8,128)S(1)} collective-permute-done((f32[1,2,2,128,32]{3,4,2,1,0:T(8,128)S(1)}, f32[1,2,2,128,32]{3,4,2,1,0:T(8,128)S(1)}, u32[]{:S(2)}, u32[]{:S(2)}) %collective-permute-start.8) | collective-permute-done | bytes 65568 | tf_op jit(solution)/shard_map/ppermute | solution.py:11
  346.6 23.8 %collective-permute-done.7 = bf16[2,1,2,128,512]{4,3,2,1,0:T(8,128)(2,1)S(1)} collective-permute-done((bf16[2,1,2,128,512]{4,3,2,1,0:T(8,128)(2,1)S(1)}, bf16[2,1,2,128,512]{4,3,2,1,0:T(8,128)(2,1)S(1)}, u32[]{:S(2)}, u32[]{:S(2)}) %collective-permute-start.7) | collective-permute-done | bytes 524320 | tf_op jit(solution)/shard_map/ppermute | solution.py:11
  372.2 10.3 %all-to-all-start.3 = ((bf16[16,128,768]{2,1,0:T(8,128)(2,1)}), bf16[16,128,768]{2,1,0:T(8,128)(2,1)}, u32[]{:S(2)}, u32[]{:S(2)}) async-start(bf16[16,128,768]{2,1,0:T(8,128)(2,1)} %get-tuple-element.34), calls=%async_computation.3 | async-start | bytes 6291456 | tf_op jit(solution)/shard_map/all_to_all | solution.py:78
  382.5 6.2 %fusion.17 = (bf16[16,1,128,768]{3,2,1,0:T(8,128)(2,1)}, bf16[16,1,128,768]{3,2,1,0:T(8,128)(2,1)}) fusion(bf16[16,2,128,768]{3,2,1,0:T(8,128)(2,1)} %all-to-all-done), kind=kLoop, calls=%fused_computation.55 | loop fusion | bytes 12582912 | tf_op jit(solution)/shard_map/slice | solution.py:86
  388.7 6.1 %fusion.16 = (bf16[16,1,128,768]{3,2,1,0:T(8,128)(2,1)}, bf16[16,1,128,768]{3,2,1,0:T(8,128)(2,1)}) fusion(bf16[16,2,128,768]{3,2,1,0:T(8,128)(2,1)} %all-to-all-done.1), kind=kLoop, calls=%fused_computation.54 | loop fusion | bytes 12582912 | tf_op jit(solution)/shard_map/slice | solution.py:86
  401.3 3.9 multiply_convert_fusion.1
  405.2 5.4 %fusion.1 = f32[1024,1024]{1,0:T(8,128)} fusion(bf16[1024,768]{1,0:T(8,128)(2,1)S(1)} %multiply_convert_fusion.1, bf16[2048,768]{1,0:T(8,128)(2,1)} %bitcast.14, s32[]{:T(128)S(6)} %select_n.34), kind=kOutput, calls=%fused_computation.11 | convolution fusion | flops 1610612736 | bytes 7340036 | tf_op jit(solution)/shard_map/dot_general | solution.py:103
  414.0 4.1 multiply_convert_fusion
  418.1 23.8 %all-to-all-done.3 = bf16[16,128,768]{2,1,0:T(8,128)(2,1)} async-done(((bf16[16,128,768]{2,1,0:T(8,128)(2,1)}), bf16[16,128,768]{2,1,0:T(8,128)(2,1)}, u32[]{:S(2)}, u32[]{:S(2)}) %all-to-all-start.3) | async-done | bytes 3145760 | tf_op jit(solution)/shard_map/all_to_all | solution.py:78
  441.9 4.5 add_convert_fusion
  454.3 4.9 collective-permute-start.11
  459.5 8.6 %collective-permute-start.14 = (bf16[2,1,2,128,512]{4,3,2,1,0:T(8,128)(2,1)S(1)}, bf16[2,1,2,128,512]{4,3,2,1,0:T(8,128)(2,1)S(1)}, u32[]{:S(2)}, u32[]{:S(2)}) collective-permute-start(bf16[2,1,2,128,512]{4,3,2,1,0:T(8,128)(2,1)S(1)} %slice.138), channel_id=1, source_target_pairs={{0,4},{2,6},{4,0},{6,2},{8,12},{10,14},{12,8},{14,10},{1,5},{3,7},... | collective-permute-start | bytes 1572872 | tf_op jit(solution)/shard_map/ppermute | solution.py:11
  468.2 3.4 collective-permute-done.11
  471.9 8.6 %collective-permute-start.12 = (bf16[1,1,2,128,512]{4,3,2,1,0:T(8,128)(2,1)S(1)}, bf16[1,1,2,128,512]{4,3,2,1,0:T(8,128)(2,1)S(1)}, u32[]{:S(2)}, u32[]{:S(2)}) collective-permute-start(bf16[1,1,2,128,512]{4,3,2,1,0:T(8,128)(2,1)S(1)} %slice.141), channel_id=1, source_target_pairs={{0,4},{2,6},{4,0},{6,2},{8,12},{10,14},{12,8},{14,10},{1,5},{3,7},... | collective-permute-start | bytes 786440 | tf_op jit(solution)/shard_map/ppermute | solution.py:11
  482.5 4.2 collective-permute-done.12
  490.1 9.0 %collective-permute-done.13 = bf16[1,1,1,128,512]{4,3,2,1,0:T(8,128)(2,1)S(1)} collective-permute-done((bf16[1,1,1,128,512]{4,3,2,1,0:T(8,128)(2,1)S(1)}, bf16[1,1,1,128,512]{4,3,2,1,0:T(8,128)(2,1)S(1)}, u32[]{:S(2)}, u32[]{:S(2)}) %collective-permute-start.13) | collective-permute-done | bytes 131104 | tf_op jit(solution)/shard_map/ppermute | solution.py:11
  (77 shorter events, 44.7 us)
Async XLA Ops:
  0.0 7.6 %copy-start.4 = (bf16[4,32,2048]{2,1,0:T(8,128)(2,1)S(1)}, bf16[4,32,2048]{2,1,0:T(8,128)(2,1)}, u32[]{:S(2)}) copy-start(bf16[4,32,2048]{2,1,0:T(8,128)(2,1)} %param.6) | copy-start | bytes 1572868
  0.0 10.5 %copy-start.5 = (s32[4,32,8]{1,2,0:T(8,128)S(1)}, s32[4,32,8]{1,2,0:T(8,128)}, u32[]{:S(2)}) copy-start(s32[4,32,8]{1,2,0:T(8,128)} %param.7) | copy-start | bytes 12292
  0.0 10.6 %copy-start.6 = (f32[4,32,8]{1,2,0:T(8,128)S(1)}, f32[4,32,8]{1,2,0:T(8,128)}, u32[]{:S(2)}) copy-start(f32[4,32,8]{1,2,0:T(8,128)} %param.8) | copy-start | bytes 12292
  0.0 158.5 %all-to-all-start = ((bf16[16,2,128,768]{3,2,1,0:T(8,128)(2,1)}), bf16[16,2,128,768]{3,2,1,0:T(8,128)(2,1)}, u32[]{:S(2)}, u32[]{:S(2)}) async-start(bf16[16,2,128,768]{3,2,1,0:T(8,128)(2,1)} %bitcast.44), calls=%async_computation | async-start | bytes 12582912 | tf_op jit(solution)/shard_map/all_to_all | solution.py:78
  7.6 148.5 %collective-permute-start.1 = (bf16[1,1,1,128,512]{4,3,2,1,0:T(8,128)(2,1)S(1)}, bf16[1,1,1,128,512]{4,3,2,1,0:T(8,128)(2,1)S(1)}, u32[]{:S(2)}, u32[]{:S(2)}) collective-permute-start(bf16[1,1,1,128,512]{4,3,2,1,0:T(8,128)(2,1)S(1)} %get-tuple-element.43), channel_id=1, source_target_pairs={{0,8},{2,10},{4,12},{6,14},{8,0},{10,2},{12,4},{14,6},{1,9},{3,11}... | collective-permute-start | bytes 393224 | tf_op jit(solution)/shard_map/ppermute | solution.py:11
  11.1 145.1 %collective-permute-start.2 = (f32[1,1,1,128,32]{3,4,2,1,0:T(8,128)S(1)}, f32[1,1,1,128,32]{3,4,2,1,0:T(8,128)S(1)}, u32[]{:S(2)}, u32[]{:S(2)}) collective-permute-start(f32[1,1,1,128,32]{3,4,2,1,0:T(8,128)S(1)} %copy.21), channel_id=1, source_target_pairs={{0,8},{2,10},{4,12},{6,14},{8,0},{10,2},{12,4},{14,6},{1,9},{3,11}... | collective-permute-start | bytes 49160 | tf_op jit(solution)/shard_map/ppermute | solution.py:11
  11.2 147.2 %collective-permute-start = (bf16[1,1,1,128,512]{4,3,2,1,0:T(8,128)(2,1)S(1)}, bf16[1,1,1,128,512]{4,3,2,1,0:T(8,128)(2,1)S(1)}, u32[]{:S(2)}, u32[]{:S(2)}) collective-permute-start(bf16[1,1,1,128,512]{4,3,2,1,0:T(8,128)(2,1)S(1)} %get-tuple-element.44), channel_id=1, source_target_pairs={{0,8},{2,10},{4,12},{6,14},{8,0},{10,2},{12,4},{14,6},{1,9},{3,11}... | collective-permute-start | bytes 393224 | tf_op jit(solution)/shard_map/ppermute | solution.py:11
  158.5 118.8 %all-to-all-start.1 = ((bf16[16,2,128,768]{3,2,1,0:T(8,128)(2,1)}), bf16[16,2,128,768]{3,2,1,0:T(8,128)(2,1)}, u32[]{:S(2)}, u32[]{:S(2)}) async-start(bf16[16,2,128,768]{3,2,1,0:T(8,128)(2,1)} %bitcast.46), calls=%async_computation.1 | async-start | bytes 12582912 | tf_op jit(solution)/shard_map/all_to_all | solution.py:78
  163.2 103.2 %collective-permute-start.5 = (f32[1,1,2,128,32]{3,4,2,1,0:T(8,128)S(1)}, f32[1,1,2,128,32]{3,4,2,1,0:T(8,128)S(1)}, u32[]{:S(2)}, u32[]{:S(2)}) collective-permute-start(f32[1,1,2,128,32]{3,4,2,1,0:T(8,128)S(1)} %pad_maximum_fusion.11), channel_id=1, source_target_pairs={{0,4},{2,6},{4,0},{6,2},{8,12},{10,14},{12,8},{14,10},{1,5},{3,7},... | collective-permute-start | bytes 98312 | tf_op jit(solution)/shard_map/ppermute | solution.py:11
  165.0 106.7 %collective-permute-start.3 = (bf16[1,1,2,128,512]{4,3,2,1,0:T(8,128)(2,1)S(1)}, bf16[1,1,2,128,512]{4,3,2,1,0:T(8,128)(2,1)S(1)}, u32[]{:S(2)}, u32[]{:S(2)}) collective-permute-start(bf16[1,1,2,128,512]{4,3,2,1,0:T(8,128)(2,1)S(1)} %pad_maximum_fusion.6), channel_id=1, source_target_pairs={{0,4},{2,6},{4,0},{6,2},{8,12},{10,14},{12,8},{14,10},{1,5},{3,7},... | collective-permute-start | bytes 786440 | tf_op jit(solution)/shard_map/ppermute | solution.py:11
  165.3 106.5 %collective-permute-start.4 = (bf16[1,1,2,128,512]{4,3,2,1,0:T(8,128)(2,1)S(1)}, bf16[1,1,2,128,512]{4,3,2,1,0:T(8,128)(2,1)S(1)}, u32[]{:S(2)}, u32[]{:S(2)}) collective-permute-start(bf16[1,1,2,128,512]{4,3,2,1,0:T(8,128)(2,1)S(1)} %pad_maximum_fusion.7), channel_id=1, source_target_pairs={{0,2},{2,0},{4,6},{6,4},{8,10},{10,8},{12,14},{14,12},{1,3},{3,1},... | collective-permute-start | bytes 786440 | tf_op jit(solution)/shard_map/ppermute | solution.py:11
  277.3 93.1 %all-to-all-start.2 = ((bf16[16,128,768]{2,1,0:T(8,128)(2,1)}), bf16[16,128,768]{2,1,0:T(8,128)(2,1)}, u32[]{:S(2)}, u32[]{:S(2)}) async-start(bf16[16,128,768]{2,1,0:T(8,128)(2,1)} %get-tuple-element.27), calls=%async_computation.2 | async-start | bytes 6291456 | tf_op jit(solution)/shard_map/all_to_all | solution.py:78
  305.4 41.0 %collective-permute-start.6 = (bf16[1,2,2,128,512]{4,3,2,1,0:T(8,128)(2,1)S(1)}, bf16[1,2,2,128,512]{4,3,2,1,0:T(8,128)(2,1)S(1)}, u32[]{:S(2)}, u32[]{:S(2)}) collective-permute-start(bf16[1,2,2,128,512]{4,3,2,1,0:T(8,128)(2,1)S(1)} %pad_maximum_fusion.4), channel_id=1, source_target_pairs={{0,2},{2,0},{4,6},{6,4},{8,10},{10,8},{12,14},{14,12},{1,3},{3,1},... | collective-permute-start | bytes 1572872 | tf_op jit(solution)/shard_map/ppermute | solution.py:11
  307.3 63.0 %collective-permute-start.7 = (bf16[2,1,2,128,512]{4,3,2,1,0:T(8,128)(2,1)S(1)}, bf16[2,1,2,128,512]{4,3,2,1,0:T(8,128)(2,1)S(1)}, u32[]{:S(2)}, u32[]{:S(2)}) collective-permute-start(bf16[2,1,2,128,512]{4,3,2,1,0:T(8,128)(2,1)S(1)} %pad_maximum_fusion.5), channel_id=1, source_target_pairs={{0,4},{2,6},{4,0},{6,2},{8,12},{10,14},{12,8},{14,10},{1,5},{3,7},... | collective-permute-start | bytes 1572872 | tf_op jit(solution)/shard_map/ppermute | solution.py:11
  308.8 37.7 %collective-permute-start.8 = (f32[1,2,2,128,32]{3,4,2,1,0:T(8,128)S(1)}, f32[1,2,2,128,32]{3,4,2,1,0:T(8,128)S(1)}, u32[]{:S(2)}, u32[]{:S(2)}) collective-permute-start(f32[1,2,2,128,32]{3,4,2,1,0:T(8,128)S(1)} %pad_maximum_fusion.10), channel_id=1, source_target_pairs={{0,2},{2,0},{4,6},{6,4},{8,10},{10,8},{12,14},{14,12},{1,3},{3,1},... | collective-permute-start | bytes 196616 | tf_op jit(solution)/shard_map/ppermute | solution.py:11
  372.2 22.9 %collective-permute-start.9 = (bf16[1024,1024]{1,0:T(8,128)(2,1)}, bf16[1024,1024]{1,0:T(8,128)(2,1)}, u32[]{:S(2)}, u32[]{:S(2)}) collective-permute-start(bf16[1024,1024]{1,0:T(8,128)(2,1)} %pad_maximum_fusion.1), channel_id=1, source_target_pairs={{0,1},{1,0},{2,3},{3,2},{4,5},{5,4},{6,7},{7,6},{8,9},{9,8},{10,11... | collective-permute-start | bytes 6291464 | tf_op jit(solution)/shard_map/ppermute | solution.py:11
  372.2 69.7 %all-to-all-start.3 = ((bf16[16,128,768]{2,1,0:T(8,128)(2,1)}), bf16[16,128,768]{2,1,0:T(8,128)(2,1)}, u32[]{:S(2)}, u32[]{:S(2)}) async-start(bf16[16,128,768]{2,1,0:T(8,128)(2,1)} %get-tuple-element.34), calls=%async_computation.3 | async-start | bytes 6291456 | tf_op jit(solution)/shard_map/all_to_all | solution.py:78
  446.4 4.6 collective-permute-start.10
  454.3 17.3 %collective-permute-start.11 = (bf16[1,2,2,128,512]{4,3,2,1,0:T(8,128)(2,1)S(1)}, bf16[1,2,2,128,512]{4,3,2,1,0:T(8,128)(2,1)S(1)}, u32[]{:S(2)}, u32[]{:S(2)}) collective-permute-start(bf16[1,2,2,128,512]{4,3,2,1,0:T(8,128)(2,1)S(1)} %bitcast.52), channel_id=1, source_target_pairs={{0,2},{2,0},{4,6},{6,4},{8,10},{10,8},{12,14},{14,12},{1,3},{3,1},... | collective-permute-start | bytes 1572872 | tf_op jit(solution)/shard_map/ppermute | solution.py:11
  459.5 21.0 %collective-permute-start.14 = (bf16[2,1,2,128,512]{4,3,2,1,0:T(8,128)(2,1)S(1)}, bf16[2,1,2,128,512]{4,3,2,1,0:T(8,128)(2,1)S(1)}, u32[]{:S(2)}, u32[]{:S(2)}) collective-permute-start(bf16[2,1,2,128,512]{4,3,2,1,0:T(8,128)(2,1)S(1)} %slice.138), channel_id=1, source_target_pairs={{0,4},{2,6},{4,0},{6,2},{8,12},{10,14},{12,8},{14,10},{1,5},{3,7},... | collective-permute-start | bytes 1572872 | tf_op jit(solution)/shard_map/ppermute | solution.py:11
  471.9 14.9 %collective-permute-start.12 = (bf16[1,1,2,128,512]{4,3,2,1,0:T(8,128)(2,1)S(1)}, bf16[1,1,2,128,512]{4,3,2,1,0:T(8,128)(2,1)S(1)}, u32[]{:S(2)}, u32[]{:S(2)}) collective-permute-start(bf16[1,1,2,128,512]{4,3,2,1,0:T(8,128)(2,1)S(1)} %slice.141), channel_id=1, source_target_pairs={{0,4},{2,6},{4,0},{6,2},{8,12},{10,14},{12,8},{14,10},{1,5},{3,7},... | collective-permute-start | bytes 786440 | tf_op jit(solution)/shard_map/ppermute | solution.py:11
  480.7 8.9 %collective-permute-start.15 = (bf16[1,1,2,128,512]{4,3,2,1,0:T(8,128)(2,1)S(1)}, bf16[1,1,2,128,512]{4,3,2,1,0:T(8,128)(2,1)S(1)}, u32[]{:S(2)}, u32[]{:S(2)}) collective-permute-start(bf16[1,1,2,128,512]{4,3,2,1,0:T(8,128)(2,1)S(1)} %slice.140), channel_id=1, source_target_pairs={{0,2},{2,0},{4,6},{6,4},{8,10},{10,8},{12,14},{14,12},{1,3},{3,1},... | collective-permute-start | bytes 786440 | tf_op jit(solution)/shard_map/ppermute | solution.py:11
  486.9 12.3 %collective-permute-start.13 = (bf16[1,1,1,128,512]{4,3,2,1,0:T(8,128)(2,1)S(1)}, bf16[1,1,1,128,512]{4,3,2,1,0:T(8,128)(2,1)S(1)}, u32[]{:S(2)}, u32[]{:S(2)}) collective-permute-start(bf16[1,1,1,128,512]{4,3,2,1,0:T(8,128)(2,1)S(1)} %slice.143), channel_id=1, source_target_pairs={{0,8},{2,10},{4,12},{6,14},{8,0},{10,2},{12,4},{14,6},{1,9},{3,11}... | collective-permute-start | bytes 393224 | tf_op jit(solution)/shard_map/ppermute | solution.py:11
  489.7 11.2 %collective-permute-start.16 = (bf16[1,1,1,128,512]{4,3,2,1,0:T(8,128)(2,1)S(1)}, bf16[1,1,1,128,512]{4,3,2,1,0:T(8,128)(2,1)S(1)}, u32[]{:S(2)}, u32[]{:S(2)}) collective-permute-start(bf16[1,1,1,128,512]{4,3,2,1,0:T(8,128)(2,1)S(1)} %slice.142), channel_id=1, source_target_pairs={{0,8},{2,10},{4,12},{6,14},{8,0},{10,2},{12,4},{14,6},{1,9},{3,11}... | collective-permute-start | bytes 393224 | tf_op jit(solution)/shard_map/ppermute | solution.py:11
  (4 other events, 15.0 us)
